TPU v7x, 512 devices: a whole 4x8x8 slice. The times are simulated.
512 devices in a mesh: dp: 32 (over z, y_hi), tensor: 16 (over x, y_lo, core).
Axes of the slice: x: 4, y: 8 (y_hi: 4, y_lo: 2; y = y_hi * 2 + y_lo), z: 8, core: 2. Of those that a mesh axis runs over, the one named last changes fastest.
Arguments:
- teacher_in: bfloat16 [16384, 4096], P('dp', 'tensor'), may hold values from -6 to 6
- out_proj: bfloat16 [4096, 4096], P('tensor', 'dp'), may hold values from -0.09375 to 0.09375
- final_gain: float32 [4096], replicated, may hold values from 0.5 to 1.5
- mean_prev: float32 [4096], replicated, may hold values from -2 to 2
- rotation: bfloat16 [4096, 4096], P(None, 'tensor'), may hold values from -0.09375 to 0.09375
- signs: int32 [4096], P('tensor'), may hold values from 0 to 1
- prev_scale: float32 [1], replicated, may hold values from 0.5 to 2
- student_in: bfloat16 [16384, 1024], P('dp'), may hold values from -6 to 6
- head_weight: bfloat16 [1024, 4096], P(None, 'tensor'), may hold values from -0.1875 to 0.1875
- image_ids: int32 [16384], replicated, may hold values from 0 to 127, never falling along the last dimension, each value on 1 to 256 neighbouring positions
Outputs:
- new_cov: float32 [4096, 4096], P('tensor', 'dp')
- new_mean: float32 [4096], P('tensor')
- grad_head: float32 [1024, 4096], P(None, 'tensor')
- feature_loss: float32 [4096], P('tensor')
Inputs may be any that keep to these rules, and one draw needn't show every extreme that they name: `image_ids`: image numbers never fall along the tokens; every image has at least one token and at most 256 tokens, some image has exactly that many when 16384 allows.
All inputs are finite; a program needn't handle non-finite values.
Results may differ from a plain program's by a relative error of at most 0.007.
Values may be sent and summed in bfloat16 or wider, within the bound.
No kernel may reach another device: no remote copies, remote signals or barrier semaphores. Data moves between devices by JAX's collectives and lax.ppermute only.
A program may use at most 128 MiB of HBM per device.

v0:
```python
import jax
import jax.numpy as jnp
from jax import lax
from jax.sharding import PartitionSpec as P


def swapped(block, axis, distance):
    count = lax.axis_size(axis)
    route = []
    for low in range(count):
        high = low | 1 << distance
        if high != low and high < count:
            route += [(low, high), (high, low)]
    return lax.ppermute(block, axis, route)


def parity_sign(value):
    count = jnp.zeros_like(value)
    for place in range(16):
        count = count + (value >> place & 1)
    return 1 - 2 * (count % 2)


def layer_norm(values):
    centred = values - jnp.mean(values, axis=-1, keepdims=True)
    spread = jnp.mean(centred * centred, axis=-1, keepdims=True)
    return centred * lax.rsqrt(spread + 1e-06)


def body(
    teacher_in,
    out_proj,
    final_gain,
    mean_prev,
    rotation,
    signs,
    prev_scale,
    student_in,
    head_weight,
    image_ids,
):
    tok_rows = teacher_in.shape[0]
    width = final_gain.shape[0]
    own_width = rotation.shape[1]
    dp_width = out_proj.shape[1]
    all_tokens = image_ids.shape[0]
    image_count = all_tokens // 128
    tensor_pos = lax.axis_index("tensor")
    data_pos = lax.axis_index("dp")
    partial_out = jnp.dot(
        teacher_in,
        lax.all_gather(out_proj, "dp", axis=1, tiled=True),
        preferred_element_type=jnp.float32,
    )
    summed = lax.psum(partial_out, "tensor")
    features = (layer_norm(summed) * final_gain).astype(jnp.bfloat16)
    own_cols = lax.dynamic_slice_in_dim(features, tensor_pos * own_width, own_width, 1)
    moment = lax.psum_scatter(
        jnp.einsum("tc,tk->ck", features, own_cols, preferred_element_type=jnp.float32),
        "dp",
        scatter_dimension=0,
        tiled=True,
    ).T
    col_sums = jnp.sum(features, axis=0, dtype=jnp.float32)
    shifted = (features.astype(jnp.float32) - mean_prev).astype(jnp.bfloat16)
    basis = jnp.dot(shifted, rotation, preferred_element_type=jnp.float32).astype(jnp.bfloat16)
    sign_vals = (2 * signs - 1).astype(jnp.bfloat16)
    index_row = lax.broadcasted_iota(jnp.int32, (own_width, own_width), 0)
    index_col = lax.broadcasted_iota(jnp.int32, (own_width, own_width), 1)
    local_table = parity_sign(index_row & index_col).astype(jnp.bfloat16)
    mixed = jnp.dot(basis * sign_vals, local_table, preferred_element_type=jnp.float32)
    for place in range(lax.axis_size("tensor").bit_length() - 1):
        other = swapped(mixed, "tensor", place)
        upper = tensor_pos >> place & 1
        mixed = jnp.where(upper == 1, other - mixed, mixed + other)
    target = mixed / (jnp.sqrt(jnp.float32(width)) * prev_scale[0])
    normed = layer_norm(student_in.astype(jnp.float32)).astype(jnp.bfloat16)
    predicted = jnp.dot(normed, head_weight, preferred_element_type=jnp.float32)
    residual = predicted - target
    image_nums = jnp.arange(image_count, dtype=jnp.int32)
    counts = jnp.sum((image_ids[None, :] == image_nums[:, None]).astype(jnp.float32), axis=1)
    own_ids = lax.dynamic_slice_in_dim(image_ids, data_pos * tok_rows, tok_rows, 0)
    token_counts = jnp.sum(
        jnp.where(own_ids[:, None] == image_nums[None, :], counts[None, :], 0.0), axis=1
    )
    token_weight = 1.0 / token_counts
    loss_terms = jnp.sum(token_weight[:, None] * residual * residual, axis=0)
    scaled = (residual * token_weight[:, None]).astype(jnp.bfloat16)
    grad_part = jnp.einsum("tk,tj->kj", normed, scaled, preferred_element_type=jnp.float32)
    grad_head, loss_total, col_total = lax.psum((grad_part, loss_terms, col_sums), "dp")
    feature_loss = loss_total / image_count
    mean_full = col_total / all_tokens
    new_mean = lax.dynamic_slice_in_dim(mean_full, tensor_pos * own_width, own_width, 0)
    col_mean = lax.dynamic_slice_in_dim(mean_full, data_pos * dp_width, dp_width, 0)
    new_cov = moment / all_tokens - new_mean[:, None] * col_mean[None, :]
    return (new_cov, new_mean, grad_head, feature_loss)


def solution(mesh):
    return jax.shard_map(
        body,
        mesh=mesh,
        in_specs=(
            P("dp", "tensor"),
            P("tensor", "dp"),
            P(),
            P(),
            P(None, "tensor"),
            P("tensor"),
            P(),
            P("dp", None),
            P(None, "tensor"),
            P(),
        ),
        out_specs=(P("tensor", "dp"), P("tensor"), P(None, "tensor"), P("tensor")),
        check_vma=False,
    )
```

profile of v0, /device:TPU:4, one launch (start us, length us, event | category | flops | bytes accessed | tf_op | source)
XLA Modules:
  0.0 885.3 jit_solution(3223342484166652994)
XLA Ops:
  8.0 93.5 %all-gather.2.cloned.1.call-done = bf16[256,4096]{1,0:T(8,128)(2,1)} async-done(((bf16[256,128]{1,0:T(8,128)(2,1)}), bf16[256,4096]{1,0:T(8,128)(2,1)}) %all-gather.2.cloned.1.call-update) | async-done | bytes 2097168 | tf_op jit(solution)/shard_map/all_gather | solution.py:52
  101.5 6.2 fusion.64
  107.7 198.0 %all-reduce.4.cloned.1.call-done = f32[512,4096]{1,0:T(8,128)} async-done(((f32[512,4096]{1,0:T(8,128)}), f32[512,4096]{1,0:T(8,128)}) %all-reduce.4.cloned.1.call-update) | async-done | bytes 8388624 | tf_op jit(solution)/shard_map/psum | solution.py:55
  305.7 3.9 reduce_sum.72
  309.6 4.5 multiply_reduce_fusion
  315.3 2.0 convert_reduce_fusion
  317.3 2.0 copy-done.2
  319.3 3.2 fusion.24
  323.3 5.0 fusion.15
  328.2 2.1 collective-permute-start
  330.3 2.0 collective-permute-done
  332.4 2.1 add_select_fusion.2
  334.4 2.9 collective-permute-start.1
  338.5 15.4 %collective-permute-done.1 = f32[512,256]{1,0:T(8,128)} collective-permute-done((f32[512,256]{1,0:T(8,128)}, f32[512,256]{1,0:T(8,128)}, u32[]{:S(2)}, u32[]{:S(2)}) %collective-permute-start.1) | collective-permute-done | bytes 524320 | tf_op jit(solution)/shard_map/ppermute | solution.py:14
  355.2 3.3 collective-permute-start.2
  358.8 11.4 %collective-permute-done.2 = f32[512,256]{1,0:T(8,128)S(1)} collective-permute-done((f32[512,256]{1,0:T(8,128)S(1)}, f32[512,256]{1,0:T(8,128)S(1)}, u32[]{:S(2)}, u32[]{:S(2)}) %collective-permute-start.2) | collective-permute-done | bytes 524320 | tf_op jit(solution)/shard_map/ppermute | solution.py:14
  371.0 3.8 collective-permute-start.3
  375.9 1.5 fusion.62
  377.4 9.4 %collective-permute-done.3 = f32[512,256]{1,0:T(8,128)} collective-permute-done((f32[512,256]{1,0:T(8,128)}, f32[512,256]{1,0:T(8,128)}, u32[]{:S(2)}, u32[]{:S(2)}) %collective-permute-start.3) | collective-permute-done | bytes 524320 | tf_op jit(solution)/shard_map/ppermute | solution.py:14
  388.2 1.7 fusion.22
  389.9 161.2 %all-reduce = (f32[4096]{0:T(1024)S(1)}, f32[256]{0:T(256)S(1)}) all-reduce(f32[4096]{0:T(1024)S(1)} %get-tuple-element.16, f32[256]{0:T(256)S(1)} %get-tuple-element.14), channel_id=1, replica_groups=mesh['dp'=32,'tensor'=16] {'dp'}, use_global_device_ids=true, to_apply=%region_5.6 | all-reduce | flops 4352 | bytes 34816 | tf_op jit(solution)/shard_map/psum | solution.py:90
  551.8 3.8 reduce-scatter.2.cloned.1.call-done
  557.4 319.2 %all-reduce.6.cloned.1.call-done = f32[1024,256]{1,0:T(8,128)} async-done(((f32[1024,256]{1,0:T(8,128)}), f32[1024,256]{1,0:T(8,128)}) %all-reduce.6.cloned.1.call-update) | async-done | bytes 1048592 | tf_op jit(solution)/shard_map/psum | solution.py:90
  876.5 2.3 copy.19
  (45 shorter events, 10.6 us)
Async XLA Ops:
  7.2 316.1 %copy-start = (bf16[4096,256]{1,0:T(8,128)(2,1)S(1)}, bf16[4096,256]{1,0:T(8,128)(2,1)}, u32[]{:S(2)}) copy-start(bf16[4096,256]{1,0:T(8,128)(2,1)} %param.14) | copy-start | bytes 6291460
  7.2 94.3 %all-gather.2.cloned.1.call-start = ((), (), s32[]{:S(2)}) async-start(), calls=%async_computation.1 | async-start | bytes 2162688 | tf_op jit(solution)/shard_map/all_gather | solution.py:52
  7.9 297.8 %all-reduce.4.cloned.1.call-start = ((), (), s32[]{:S(2)}) async-start(), calls=%async_computation.2 | async-start | bytes 16777216 | tf_op jit(solution)/shard_map/psum | solution.py:55
  107.7 447.9 %reduce-scatter.2.cloned.1.call-start = ((), (), s32[]{:S(2)}) async-start(), calls=%async_computation.3 | async-start | bytes 4325376 | tf_op jit(solution)/shard_map/reduce_scatter | solution.py:58
  305.7 8.4 copy-start.5
  309.6 5.8 copy-start.1
  317.3 2.0 copy-start.2
  322.5 0.7 copy-start.8
  322.5 0.7 copy-start.7
  322.6 554.0 %all-reduce.6.cloned.1.call-start = ((), (), s32[]{:S(2)}) async-start(), calls=%async_computation.4 | async-start | bytes 2097152 | tf_op jit(solution)/shard_map/psum | solution.py:90
  323.3 14.1 %copy-start.4 = (s32[16384]{0:T(1024)S(1)}, s32[16384]{0:T(1024)}, u32[]{:S(2)}) copy-start(s32[16384]{0:T(1024)} %param.19) | copy-start | bytes 196612
  323.3 14.1 %copy-start.3 = (bf16[512,1024]{1,0:T(8,128)(2,1)S(1)}, bf16[512,1024]{1,0:T(8,128)(2,1)}, u32[]{:S(2)}) copy-start(bf16[512,1024]{1,0:T(8,128)(2,1)} %param.17) | copy-start | bytes 3145732
  328.2 4.1 collective-permute-start
  334.4 19.5 %collective-permute-start.1 = (f32[512,256]{1,0:T(8,128)}, f32[512,256]{1,0:T(8,128)}, u32[]{:S(2)}, u32[]{:S(2)}) collective-permute-start(f32[512,256]{1,0:T(8,128)} %add_select_fusion.2), channel_id=1, source_target_pairs={{0,2},{2,0},{1,3},{3,1},{4,6},{6,4},{5,7},{7,5},{8,10},{10,8},{9,1... | collective-permute-start | bytes 1572872 | tf_op jit(solution)/shard_map/ppermute | solution.py:14
  355.2 15.0 %collective-permute-start.2 = (f32[512,256]{1,0:T(8,128)S(1)}, f32[512,256]{1,0:T(8,128)S(1)}, u32[]{:S(2)}, u32[]{:S(2)}) collective-permute-start(f32[512,256]{1,0:T(8,128)S(1)} %add_select_fusion.1), channel_id=1, source_target_pairs={{0,4},{4,0},{1,5},{5,1},{2,6},{6,2},{3,7},{7,3},{8,12},{12,8},{9,1... | collective-permute-start | bytes 1572872 | tf_op jit(solution)/shard_map/ppermute | solution.py:14
  371.0 15.8 %collective-permute-start.3 = (f32[512,256]{1,0:T(8,128)}, f32[512,256]{1,0:T(8,128)}, u32[]{:S(2)}, u32[]{:S(2)}) collective-permute-start(f32[512,256]{1,0:T(8,128)} %add_select_fusion), channel_id=1, source_target_pairs={{0,8},{8,0},{1,9},{9,1},{2,10},{10,2},{3,11},{11,3},{4,12},{12,4},... | collective-permute-start | bytes 1572872 | tf_op jit(solution)/shard_map/ppermute | solution.py:14
  551.2 327.6 %copy-start.6 = (f32[256]{0:T(256)}, f32[256]{0:T(256)S(1)}, u32[]{:S(2)}) copy-start(f32[256]{0:T(256)S(1)} %dynamic_slice.13) | copy-start | bytes 3076
Sparse Core Ops, SparseCore 0:
  11.1 90.3 all-gather.1
  107.8 197.8 all-reduce.3
  322.7 232.8 reduce-scatter.1
  559.2 317.3 all-reduce.5
where the time goes:
time: 886 us; the launch traced here: 885 us
  waiting for transfers between devices  653 us (74%)
  blocking collectives  161 us (18%)
  other arithmetic  19.2 us (2%)
  matrix products  17.6 us (2%)
  between operations  14.6 us (2%)
  starting transfers between devices  12.3 us (1%)
    psum x1, waiting for transfers between devices, body(): lax.psum((grad_part, loss_terms, col_sums), 'dp')  319 us
    psum x1, waiting for transfers between devices, body(): summed = lax.psum(partial_out, 'tensor')  198 us
    psum x1, blocking collectives, body(): lax.psum((grad_part, loss_terms, col_sums), 'dp')  161 us
    all_gather x1, waiting for transfers between devices, body(): lax.all_gather(out_proj, 'dp', axis=1, tiled=True)  93.5 us
    ppermute x4, waiting for transfers between devices, swapped(): return lax.ppermute(block, axis, route)  38.2 us
  transfers between devices with their start and end apart: 8, of which 8 were waited for; matrix products, arithmetic and copies ran while one was open for 2% of the time, Pallas kernels for 0%

commit v1 on v0

v1 whole, which is shorter than its diff:
```python
import jax
import jax.numpy as jnp
from jax import lax
from jax.experimental import pallas as pl
from jax.experimental.pallas import tpu as pltpu
from jax.sharding import Mesh
from jax.sharding import PartitionSpec as P

DP = ("z", "yh")
TN = ("x", "yl", "c")
IMAGE_SHARE = 128
BF = jnp.bfloat16
F32 = jnp.float32


def hold(value):
    return lax.reduce_precision(value, 8, 7)


def split3(value):
    high = hold(value)
    rest = value - high
    mid = hold(rest)
    return high, mid, rest - mid


def shift(block, axis, step):
    count = lax.axis_size(axis)
    return lax.ppermute(block, axis, [(i, (i + step) % count) for i in range(count)])


def absolute(relative, axis):
    count = len(relative)
    twice = jnp.stack(relative + relative)
    return lax.dynamic_slice_in_dim(twice, count - lax.axis_index(axis), count, 0)


def gather_direct(block, axis):
    count = lax.axis_size(axis)
    return absolute([block] + [shift(block, axis, count - j) for j in range(1, count)], axis)


def gather_ring(block, axis):
    count = lax.axis_size(axis)
    ahead, behind = [block], [block]
    for _ in range(count // 2 - 1):
        ahead.append(shift(ahead[-1], axis, -1))
        behind.append(shift(behind[-1], axis, 1))
    half = block.shape[0] // 2
    far = jnp.concatenate([shift(ahead[-1][:half], axis, -1), shift(behind[-1][half:], axis, 1)])
    return absolute(ahead + [far] + behind[:0:-1], axis)


def gather_dp(block):
    near = gather_direct(block, "yh")
    near = near.reshape((-1,) + block.shape[1:])
    whole = gather_ring(near, "z")
    return whole.reshape((-1,) + block.shape[1:])


def parity_sign(value):
    count = jnp.zeros_like(value)
    for place in range(16):
        count = count + (value >> place & 1)
    return 1 - 2 * (count % 2)


def layer_norm(values):
    centred = values - jnp.mean(values, axis=-1, keepdims=True)
    spread = jnp.mean(centred * centred, axis=-1, keepdims=True)
    return centred * lax.rsqrt(spread + 1e-06)


def project_kernel(x_ref, w_ref, out_ref, stat_ref):
    own = w_ref.shape[1]
    total = jnp.zeros(out_ref.shape, F32)
    for b in range(x_ref.shape[0]):
        total += jnp.dot(x_ref[b], w_ref[b * own : (b + 1) * own, :], preferred_element_type=F32)
    mean = jnp.sum(total, axis=1, keepdims=True) * (1.0 / own)
    centred = total - mean
    out_ref[...] = centred.astype(BF)
    spread = jnp.sum(centred * centred, axis=1, keepdims=True)
    lane = lax.broadcasted_iota(jnp.int32, stat_ref.shape, 1)
    stat_ref[...] = jnp.where(lane == 0, mean, spread)


def main_kernel(
    pos_ref, scale_ref, g_ref, adj_ref, rstd_ref, gain_ref, prev_ref, rot_ref, pred_ref, w_ref, normed_ref,
    out_ref, f_ref,
):
    blocks, rows, own = f_ref.shape
    chunks = out_ref.shape[0]
    part = out_ref.shape[2]
    depth = normed_ref.shape[1] // chunks
    rstd = rstd_ref[...]
    total = jnp.zeros((rows, own), F32)
    sums = []
    for b in range(blocks):
        value = (g_ref[b, :rows, :].astype(F32) + adj_ref[:, b : b + 1]) * rstd * gain_ref[b]
        feature = value.astype(BF)
        f_ref[b] = feature
        feature = feature.astype(F32)
        sums.append(jnp.sum(feature, axis=0, keepdims=True))
        shifted = (feature - prev_ref[b]).astype(BF)
        total += jnp.dot(shifted, rot_ref[b * own : (b + 1) * own, :], preferred_element_type=F32)
    residual = pred_ref[...] - total * scale_ref[0]
    weighted = residual * w_ref[...]
    loss = jnp.sum(weighted * residual, axis=0, keepdims=True)
    grad = lax.dot_general(
        normed_ref[...], weighted.astype(BF), (((0,), (0,)), ((), ())), preferred_element_type=F32
    ).astype(BF)
    own_t = f_ref[pos_ref[0]].astype(F32).T
    own_col = jnp.sum(own_t, axis=1, keepdims=True)
    own_row = jnp.sum(f_ref[pos_ref[0]].astype(F32), axis=0, keepdims=True)
    own_t = own_t.astype(BF)
    for b in range(blocks):
        block = jnp.dot(own_t, f_ref[b], preferred_element_type=F32) - own_col * (sums[b] * (1.0 / rows))
        block = block.astype(BF)
        for h in range(2):
            out_ref[2 * b + h, :own, :] = block[:, h * part : (h + 1) * part]
    row = lax.broadcasted_iota(jnp.int32, (16, part), 0)

    def parts(value):
        high = value.astype(BF).astype(F32)
        rest = value - high
        mid = rest.astype(BF).astype(F32)
        return [high, mid, rest - mid]

    fixed = []
    for h in range(2):
        fixed += parts(own_row[:, h * part : (h + 1) * part])
    for h in range(2):
        fixed += parts(loss[:, h * part : (h + 1) * part])
    for d in range(chunks):
        for h in range(2):
            out_ref[d, own + h * depth : own + (h + 1) * depth, :] = grad[
                d * depth : (d + 1) * depth, h * part : (h + 1) * part
            ]
        tile = jnp.zeros((16, part), F32)
        here = sums[d // 2][:, (d % 2) * part : (d % 2 + 1) * part]
        for i, piece in enumerate(fixed + parts(here)):
            tile = jnp.where(row == i, piece, tile)
        out_ref[d, own + 2 * depth :, :] = tile.astype(BF)


def body(
    teacher_in,
    out_proj,
    final_gain,
    mean_prev,
    rotation,
    signs,
    prev_scale,
    student_in,
    head_weight,
    image_ids,
):
    rows, own = teacher_in.shape
    part = out_proj.shape[1]
    width = final_gain.shape[0]
    blocks = width // own
    chunks = width // part
    depth = student_in.shape[1] // chunks
    all_tokens = image_ids.shape[0]
    image_count = all_tokens // IMAGE_SHARE
    dpos = lax.axis_index(DP)
    tpos = lax.axis_index(TN)

    side = dpos % 2
    halves = out_proj.reshape(2, part, part)
    got = []
    for k in range(2):
        send = lax.dynamic_index_in_dim(halves, (side + k) % 2, 0, keepdims=False)
        route = []
        for d in range(chunks):
            for t in range(blocks):
                route.append((d * blocks + t, (2 * t + (d % 2 ^ k)) * blocks + d // 2))
        got.append(lax.ppermute(send, DP + TN, route))
    strip = jnp.where(
        side == 0, jnp.concatenate(got, axis=1), jnp.concatenate(got[::-1], axis=1)
    )
    proj = gather_dp(strip)
    teacher = lax.all_gather(teacher_in, TN, axis=0, tiled=False)

    lines = lax.dynamic_slice_in_dim(rotation, dpos * part, part, 0)
    index_row = lax.broadcasted_iota(jnp.int32, (own, own), 0)
    index_col = lax.broadcasted_iota(jnp.int32, (own, own), 1)
    table = parity_sign(index_row & index_col).astype(BF)
    mixed = jnp.dot(lines * (2 * signs - 1).astype(BF), table, preferred_element_type=F32)
    for axis in TN[::-1]:
        count = lax.axis_size(axis)
        for place in range(count.bit_length() - 1):
            other = lax.ppermute(mixed, axis, [(i, i ^ 1 << place) for i in range(count)])
            upper = lax.axis_index(axis) >> place & 1
            mixed = jnp.where(upper == 1, other - mixed, mixed + other)
    turned = gather_dp(mixed.astype(BF))

    normed = layer_norm(student_in.astype(F32)).astype(BF)
    predicted = jnp.dot(normed, head_weight, preferred_element_type=F32)
    image_nums = jnp.arange(image_count, dtype=jnp.int32)
    counts = jnp.sum((image_ids[None, :] == image_nums[:, None]).astype(F32), axis=1)
    own_ids = lax.dynamic_slice_in_dim(image_ids, dpos * rows, rows, 0)
    token_counts = jnp.sum(
        jnp.where(own_ids[:, None] == image_nums[None, :], counts[None, :], 0.0), axis=1, keepdims=True
    )
    token_weight = 1.0 / token_counts

    raw, stat = pl.pallas_call(
        project_kernel,
        out_shape=(jax.ShapeDtypeStruct((rows, own), BF), jax.ShapeDtypeStruct((rows, 2), F32)),
        compiler_params=pltpu.CompilerParams(vmem_limit_bytes=40 << 20),
        cost_estimate=pl.CostEstimate(flops=2 * rows * width * own, bytes_accessed=8 << 20, transcendentals=0),
    )(teacher, proj)
    pieces = jnp.stack(split3(stat.T)).reshape(6 * rows // own, own).astype(BF)
    spare = -pieces.shape[0] % 16
    packed = jnp.concatenate([raw, pieces, jnp.zeros((spare, own), BF)])
    gathered = lax.all_gather(packed, TN, axis=0, tiled=False)
    stats = gathered[:, rows : rows + pieces.shape[0], :].astype(F32).reshape(blocks, 3, 2, rows).sum(1)
    block_mean, block_spread = stats[:, 0], stats[:, 1]
    mean = jnp.mean(block_mean, axis=0)
    adjust = block_mean - mean
    variance = (jnp.sum(block_spread, axis=0) + own * jnp.sum(adjust * adjust, axis=0)) / width
    rstd = lax.rsqrt(variance + 1e-06)
    scale = 1.0 / (jnp.sqrt(F32(width)) * prev_scale)

    tall = own + 2 * depth + 16
    spaces = [pl.BlockSpec(memory_space=pltpu.SMEM)] * 2 + [pl.BlockSpec(memory_space=pltpu.VMEM)] * 9
    sent = pl.pallas_call(
        main_kernel,
        out_shape=jax.ShapeDtypeStruct((chunks, tall, part), BF),
        in_specs=spaces,
        out_specs=pl.BlockSpec(memory_space=pltpu.VMEM),
        scratch_shapes=[pltpu.VMEM((blocks, rows, own), BF)],
        compiler_params=pltpu.CompilerParams(vmem_limit_bytes=48 << 20),
        cost_estimate=pl.CostEstimate(flops=5 * rows * width * own, bytes_accessed=12 << 20, transcendentals=0),
    )(
        tpos.reshape(1),
        scale,
        gathered,
        adjust.T,
        rstd[:, None],
        final_gain.reshape(blocks, 1, own),
        mean_prev.reshape(blocks, 1, own),
        turned,
        predicted,
        token_weight,
        normed,
    )
    taken = lax.all_to_all(sent, DP, 0, 0, tiled=True)

    grad_own = jnp.sum(taken[:, own : own + 2 * depth, :].astype(F32), axis=0).astype(BF)
    grads = gather_direct(gather_direct(grad_own, "yh"), "z").reshape(chunks, 2, depth, part)
    grad_head = grads.transpose(0, 2, 1, 3).reshape(chunks * depth, own).astype(F32)

    tail = taken[:, own + 2 * depth :, :].astype(F32)
    sums_t = tail[:, 0:6].reshape(chunks, 2, 3, part).sum(2).reshape(chunks, own)
    loss = tail[:, 6:12].reshape(chunks, 2, 3, part).sum((0, 2)).reshape(own)
    sums_d = tail[:, 12:15].sum(1)
    new_mean = jnp.sum(sums_t, axis=0) / all_tokens
    mean_d = jnp.sum(sums_d, axis=0) / all_tokens
    off_t = sums_t / rows - new_mean
    off_d = sums_d / rows - mean_d
    between = lax.dot_general(
        off_t, off_d, (((0,), (0,)), ((), ())), precision=lax.Precision.HIGHEST, preferred_element_type=F32
    )
    within = jnp.sum(taken[:, :own, :].astype(F32), axis=0)
    new_cov = (within + between * rows) / all_tokens
    return (new_cov, new_mean, grad_head, loss / image_count)


def solution(mesh):
    z, y, x = 8, 4, 4
    if mesh.devices.size != 512:
        z, y, x = 2, mesh.shape["dp"] // 2, mesh.shape["tensor"] // 4
    inner = Mesh(mesh.devices.reshape(z, y, x, 2, 2), DP + TN)
    return jax.shard_map(
        body,
        mesh=inner,
        in_specs=(
            P(DP, TN),
            P(TN, DP),
            P(),
            P(),
            P(None, TN),
            P(TN),
            P(),
            P(DP, None),
            P(None, TN),
            P(),
        ),
        out_specs=(P(TN, DP), P(TN), P(None, TN), P(TN)),
        check_vma=False,
    )
```

time: 886 us -> 357 us (0.40)
  waiting for transfers between devices: 653 us -> 80.7 us
  starting transfers between devices: 12.3 us -> 140 us
  blocking collectives: 161 us -> 76.6 us
  matrix products: 17.6 us -> 3.73 us
  local copies, waits for them, and re-layouts: 7.13 us -> 20.2 us
  other arithmetic: 19.2 us -> 7.69 us
  Pallas kernels: 0 us -> 10.8 us
    psum x2 -> x0, waiting for transfers between devices: 517 us -> none  [the longest x1 319 us: body(): lax.psum((grad_part, loss_terms, col_sums), 'dp')]
    psum x1 -> x0, blocking collectives: 161 us -> none  [body(): lax.psum((grad_part, loss_terms, col_sums), 'dp')]
    ppermute x4 -> x38, starting transfers between devices: 12.1 us -> 139 us  [the longest x32 114 us: shift(): lax.ppermute(block, axis, [(i, (i + step) % count) for i in range(count)])]
    all_gather x1 -> x2, waiting for transfers between devices: 93.5 us -> 0.02 us  [the longest x1 0.02 us: body(): teacher = lax.all_gather(teacher_in, TN, axis=0, tiled=False)]
    all_to_all x0 -> x1, blocking collectives: none -> 76.6 us  [body(): taken = lax.all_to_all(sent, DP, 0, 0, tiled=True)]
    ppermute x4 -> x38, waiting for transfers between devices: 38.2 us -> 80 us  [the longest x32 49.5 us: shift(): lax.ppermute(block, axis, [(i, (i + step) % count) for i in range(count)])]
    dot_general x5 -> x3, matrix products: 17.6 us -> 3.73 us  [the longest x1 1.79 us: body(): lax.dot_general(off_t, off_d, (((0,), (0,)), ((), ())), precision=lax.Pre...]
    pallas_call x0 -> x2, Pallas kernels: none -> 10.8 us  [the longest x1 9.4 us: body(): pl.pallas_call(main_kernel, out_shape=jax.ShapeDtypeStruct((chunks, tall,...]
  transfers between devices with their start and end apart: 8 -> 40, of which waited for: 8 -> 23; matrix products, arithmetic and copies ran while one was open for 2% -> 4% of each run, Pallas kernels for 0% -> 0%
where the time goes in v1:
time: 357 us; the launch traced here: 355 us
  starting transfers between devices  140 us (39%)
  waiting for transfers between devices  80.7 us (23%)
  blocking collectives  76.6 us (21%)
  local copies, waits for them, and re-layouts  20.2 us (6%)
  between operations  16 us (4%)
  Pallas kernels  10.8 us (3%)
  other arithmetic  7.69 us (2%)
  matrix products  3.73 us (1%)
    ppermute x32, starting transfers between devices, shift(): lax.ppermute(block, axis, [(i, (i + step) % count) for i in range(count)])  114 us
    all_to_all x1, blocking collectives, body(): taken = lax.all_to_all(sent, DP, 0, 0, tiled=True)  76.6 us
    ppermute x32, waiting for transfers between devices, shift(): lax.ppermute(block, axis, [(i, (i + step) % count) for i in range(count)])  49.5 us
    ppermute x4, waiting for transfers between devices, body(): lax.ppermute(mixed, axis, [(i, i ^ 1 << place) for i in range(count)])  20.4 us
    ppermute x2, starting transfers between devices, body(): got.append(lax.ppermute(send, DP + TN, route))  14.8 us
    unnamed x75, local copies, waits for them, and re-layouts  14.4 us
    ppermute x4, starting transfers between devices, body(): lax.ppermute(mixed, axis, [(i, i ^ 1 << place) for i in range(count)])  10.3 us
    ppermute x2, waiting for transfers between devices, body(): got.append(lax.ppermute(send, DP + TN, route))  10.1 us
  transfers between devices with their start and end apart: 40, of which 23 were waited for; matrix products, arithmetic and copies ran while one was open for 4% of the time, Pallas kernels for 0%

profile of v1, /device:TPU:4, one launch (start us, length us, event | category | flops | bytes accessed | tf_op | source)
XLA Modules:
  0.0 355.3 jit_solution(14347863185924085729)
XLA Ops:
  8.8 10.8 %collective-permute-start = (bf16[128,128]{1,0:T(8,128)(2,1)S(1)}, bf16[128,128]{1,0:T(8,128)(2,1)S(1)}, u32[]{:S(2)}, u32[]{:S(2)}) collective-permute-start(bf16[128,128]{1,0:T(8,128)(2,1)S(1)} %get-tuple-element.26), channel_id=1, source_target_pairs={{0,0},{1,32},{2,64},{3,96},{4,128},{5,160},{6,192},{7,224},{8,256}... | collective-permute-start | bytes 98312 | tf_op jit(solution)/shard_map/ppermute | solution.py:178
  23.6 10.0 %collective-permute-done.1 = bf16[128,128]{1,0:T(8,128)(2,1)S(1)} collective-permute-done((bf16[128,128]{1,0:T(8,128)(2,1)S(1)}, bf16[128,128]{1,0:T(8,128)(2,1)S(1)}, u32[]{:S(2)}, u32[]{:S(2)}) %collective-permute-start.1) | collective-permute-done | bytes 32800 | tf_op jit(solution)/shard_map/ppermute | solution.py:178
  33.7 7.8 %collective-permute-start.2 = (bf16[128,256]{1,0:T(8,128)(2,1)S(1)}, bf16[128,256]{1,0:T(8,128)(2,1)S(1)}, u32[]{:S(2)}, u32[]{:S(2)}) collective-permute-start(bf16[128,256]{1,0:T(8,128)(2,1)S(1)} %maximum_select_fusion.1), channel_id=1, source_target_pairs={{0,48},{16,0},{32,16},{48,32},{1,49},{17,1},{33,17},{49,33},{2,50}... | collective-permute-start | bytes 196616 | tf_op jit(solution)/shard_map/ppermute | solution.py:29
  43.7 4.1 %collective-permute-start.4 = (bf16[128,256]{1,0:T(8,128)(2,1)S(1)}, bf16[128,256]{1,0:T(8,128)(2,1)S(1)}, u32[]{:S(2)}, u32[]{:S(2)}) collective-permute-start(bf16[128,256]{1,0:T(8,128)(2,1)S(1)} %maximum_select_fusion.1), channel_id=1, source_target_pairs={{0,16},{16,32},{32,48},{48,0},{1,17},{17,33},{33,49},{49,1},{2,18}... | collective-permute-start | bytes 196616 | tf_op jit(solution)/shard_map/ppermute | solution.py:29
  47.8 5.7 %collective-permute-done.3 = bf16[128,256]{1,0:T(8,128)(2,1)S(1)} collective-permute-done((bf16[128,256]{1,0:T(8,128)(2,1)S(1)}, bf16[128,256]{1,0:T(8,128)(2,1)S(1)}, u32[]{:S(2)}, u32[]{:S(2)}) %collective-permute-start.3) | collective-permute-done | bytes 65568 | tf_op jit(solution)/shard_map/ppermute | solution.py:29
  59.6 4.3 %collective-permute-done.5 = bf16[512,256]{1,0:T(8,128)(2,1)S(1)} collective-permute-done((bf16[512,256]{1,0:T(8,128)(2,1)S(1)}, bf16[512,256]{1,0:T(8,128)(2,1)S(1)}, u32[]{:S(2)}, u32[]{:S(2)}) %collective-permute-start.5) | collective-permute-done | bytes 262176 | tf_op jit(solution)/shard_map/ppermute | solution.py:29
  70.8 4.1 %collective-permute-done.6 = bf16[512,256]{1,0:T(8,128)(2,1)S(1)} collective-permute-done((bf16[512,256]{1,0:T(8,128)(2,1)S(1)}, bf16[512,256]{1,0:T(8,128)(2,1)S(1)}, u32[]{:S(2)}, u32[]{:S(2)}) %collective-permute-start.6) | collective-permute-done | bytes 262176 | tf_op jit(solution)/shard_map/ppermute | solution.py:29
  81.0 9.2 %collective-permute-done.11 = bf16[512,256]{1,0:T(8,128)(2,1)S(1)} collective-permute-done((bf16[512,256]{1,0:T(8,128)(2,1)S(1)}, bf16[512,256]{1,0:T(8,128)(2,1)S(1)}, u32[]{:S(2)}, u32[]{:S(2)}) %collective-permute-start.11) | collective-permute-done | bytes 262176 | tf_op jit(solution)/shard_map/ppermute | solution.py:29
  92.1 5.1 %collective-permute-start.8 = (bf16[256,256]{1,0:T(8,128)(2,1)S(1)}, bf16[256,256]{1,0:T(8,128)(2,1)S(1)}, u32[]{:S(2)}, u32[]{:S(2)}) collective-permute-start(bf16[256,256]{1,0:T(8,128)(2,1)S(1)} %slice.52), channel_id=1, source_target_pairs={{0,448},{64,0},{128,64},{192,128},{256,192},{320,256},{384,320},{4... | collective-permute-start | bytes 393224 | tf_op jit(solution)/shard_map/ppermute | solution.py:29
  113.7 4.1 %collective-permute-done.14 = f32[128,256]{1,0:T(8,128)S(1)} collective-permute-done((f32[128,256]{1,0:T(8,128)S(1)}, f32[128,256]{1,0:T(8,128)S(1)}, u32[]{:S(2)}, u32[]{:S(2)}) %collective-permute-start.14) | collective-permute-done | bytes 131104 | tf_op jit(solution)/shard_map/ppermute | solution.py:193
  120.9 6.9 %collective-permute-done.15 = f32[128,256]{1,0:T(8,128)S(1)} collective-permute-done((f32[128,256]{1,0:T(8,128)S(1)}, f32[128,256]{1,0:T(8,128)S(1)}, u32[]{:S(2)}, u32[]{:S(2)}) %collective-permute-start.15) | collective-permute-done | bytes 131104 | tf_op jit(solution)/shard_map/ppermute | solution.py:193
  130.2 9.4 %collective-permute-done.16 = f32[128,256]{1,0:T(8,128)S(1)} collective-permute-done((f32[128,256]{1,0:T(8,128)S(1)}, f32[128,256]{1,0:T(8,128)S(1)}, u32[]{:S(2)}, u32[]{:S(2)}) %collective-permute-start.16) | collective-permute-done | bytes 131104 | tf_op jit(solution)/shard_map/ppermute | solution.py:193
  149.9 4.9 %collective-permute-done.18 = bf16[128,256]{1,0:T(8,128)(2,1)S(1)} collective-permute-done((bf16[128,256]{1,0:T(8,128)(2,1)S(1)}, bf16[128,256]{1,0:T(8,128)(2,1)S(1)}, u32[]{:S(2)}, u32[]{:S(2)}) %collective-permute-start.18) | collective-permute-done | bytes 65568 | tf_op jit(solution)/shard_map/ppermute | solution.py:29
  156.0 5.2 %collective-permute-start.20 = (bf16[512,256]{1,0:T(8,128)(2,1)S(1)}, bf16[512,256]{1,0:T(8,128)(2,1)S(1)}, u32[]{:S(2)}, u32[]{:S(2)}) collective-permute-start(bf16[512,256]{1,0:T(8,128)(2,1)S(1)} %bitcast.195), channel_id=1, source_target_pairs={{0,448},{64,0},{128,64},{192,128},{256,192},{320,256},{384,320},{4... | collective-permute-start | bytes 786440 | tf_op jit(solution)/shard_map/ppermute | solution.py:29
  165.1 5.6 %collective-permute-start.21 = (bf16[512,256]{1,0:T(8,128)(2,1)S(1)}, bf16[512,256]{1,0:T(8,128)(2,1)S(1)}, u32[]{:S(2)}, u32[]{:S(2)}) collective-permute-start(bf16[512,256]{1,0:T(8,128)(2,1)S(1)} %collective-permute-done.20), channel_id=1, source_target_pairs={{0,448},{64,0},{128,64},{192,128},{256,192},{320,256},{384,320},{4... | collective-permute-start | bytes 786440 | tf_op jit(solution)/shard_map/ppermute | solution.py:29
  174.6 5.6 %collective-permute-start.22 = (bf16[512,256]{1,0:T(8,128)(2,1)S(1)}, bf16[512,256]{1,0:T(8,128)(2,1)S(1)}, u32[]{:S(2)}, u32[]{:S(2)}) collective-permute-start(bf16[512,256]{1,0:T(8,128)(2,1)S(1)} %collective-permute-done.21), channel_id=1, source_target_pairs={{0,448},{64,0},{128,64},{192,128},{256,192},{320,256},{384,320},{4... | collective-permute-start | bytes 786440 | tf_op jit(solution)/shard_map/ppermute | solution.py:29
  184.1 5.6 %collective-permute-start.23 = (bf16[256,256]{1,0:T(8,128)(2,1)S(1)}, bf16[256,256]{1,0:T(8,128)(2,1)S(1)}, u32[]{:S(2)}, u32[]{:S(2)}) collective-permute-start(bf16[256,256]{1,0:T(8,128)(2,1)S(1)} %slice.57), channel_id=1, source_target_pairs={{0,448},{64,0},{128,64},{192,128},{256,192},{320,256},{384,320},{4... | collective-permute-start | bytes 393224 | tf_op jit(solution)/shard_map/ppermute | solution.py:29
  192.2 5.6 %collective-permute-done.27 = bf16[256,256]{1,0:T(8,128)(2,1)S(1)} collective-permute-done((bf16[256,256]{1,0:T(8,128)(2,1)S(1)}, bf16[256,256]{1,0:T(8,128)(2,1)S(1)}, u32[]{:S(2)}, u32[]{:S(2)}) %collective-permute-start.27) | collective-permute-done | bytes 131104 | tf_op jit(solution)/shard_map/ppermute | solution.py:29
  203.1 9.4 %shard_map.130 = bf16[32,336,128]{2,1,0:T(8,128)(2,1)} custom-call(s32[1]{0:T(128)} %bitcast.pos_ref, f32[1]{0:T(128)S(6)} %div.71.scale_ref, bf16[16,528,256]{2,1,0:T(8,128)(2,1)} %bitcast.189, f32[512,16]{1,0:T(8,128)S(1)} %get-tuple-element.19.adj_ref, f32[512,1]{1,0:T(8,128)S(1)} %copy.44.rstd_ref, f32[16,1,256]{2,1,0:T(1,128)S(1)} %bitcast.186, ...), custom_call_target="tpu_custom_call" | custom-call | flops 2684354560 | bytes 12582912 | tf_op jit(solution)/shard_map/pallas_call | solution.py:228
  212.5 76.6 %all_to_all.5 = bf16[32,336,128]{2,1,0:T(8,128)(2,1)S(1)} all-to-all(bf16[32,336,128]{2,1,0:T(8,128)(2,1)} %shard_map.130), channel_id=1, replica_groups=mesh['z'=8,'yh'=4,'x'=4,'yl'=2,'c'=2] {'z','yh'}, dimensions={0} | all-to-all | bytes 5505024 | tf_op jit(solution)/shard_map/all_to_all | solution.py:249
  291.7 5.7 %collective-permute-start.29 = (bf16[64,128]{1,0:T(8,128)(2,1)S(1)}, bf16[64,128]{1,0:T(8,128)(2,1)}, u32[]{:S(2)}, u32[]{:S(2)}) collective-permute-start(bf16[64,128]{1,0:T(8,128)(2,1)S(1)} %slice_reduce_fusion), channel_id=1, source_target_pairs={{0,32},{16,48},{32,0},{48,16},{1,33},{17,49},{33,1},{49,17},{2,34}... | collective-permute-start | bytes 49160 | tf_op jit(solution)/shard_map/ppermute | solution.py:29
  320.0 5.6 %collective-permute-start.33 = (bf16[4,64,128]{2,1,0:T(8,128)(2,1)S(1)}, bf16[4,64,128]{2,1,0:T(8,128)(2,1)S(1)}, u32[]{:S(2)}, u32[]{:S(2)}) collective-permute-start(bf16[4,64,128]{2,1,0:T(8,128)(2,1)S(1)} %get-tuple-element.15), channel_id=1, source_target_pairs={{0,320},{64,384},{128,448},{192,0},{256,64},{320,128},{384,192},{4... | collective-permute-start | bytes 196616 | tf_op jit(solution)/shard_map/ppermute | solution.py:29
  329.4 5.3 %collective-permute-start.35 = (bf16[4,64,128]{2,1,0:T(8,128)(2,1)S(1)}, bf16[4,64,128]{2,1,0:T(8,128)(2,1)S(1)}, u32[]{:S(2)}, u32[]{:S(2)}) collective-permute-start(bf16[4,64,128]{2,1,0:T(8,128)(2,1)S(1)} %get-tuple-element.15), channel_id=1, source_target_pairs={{0,192},{64,256},{128,320},{192,384},{256,448},{320,0},{384,64},{4... | collective-permute-start | bytes 196616 | tf_op jit(solution)/shard_map/ppermute | solution.py:29
  334.7 4.1 %collective-permute-start.36 = (bf16[4,64,128]{2,1,0:T(8,128)(2,1)S(1)}, bf16[4,64,128]{2,1,0:T(8,128)(2,1)S(1)}, u32[]{:S(2)}, u32[]{:S(2)}) collective-permute-start(bf16[4,64,128]{2,1,0:T(8,128)(2,1)S(1)} %get-tuple-element.15), channel_id=1, source_target_pairs={{0,128},{64,192},{128,256},{192,320},{256,384},{320,448},{384,0},{... | collective-permute-start | bytes 196616 | tf_op jit(solution)/shard_map/ppermute | solution.py:29
  (209 shorter events, 118.5 us)
Async XLA Ops:
  7.2 93.1 %all-gather.5.cloned.1.call-start = ((), (), s32[]{:S(2)}) async-start(), calls=%async_computation.1 | async-start | bytes 4456448 | tf_op jit(solution)/shard_map/all_gather | solution.py:183
  7.9 191.7 %all-gather.7.cloned.1.call-start = ((), (), s32[]{:S(2)}) async-start(), calls=%async_computation.2 | async-start | bytes 4595712 | tf_op jit(solution)/shard_map/all_gather | solution.py:217
  8.8 14.8 %collective-permute-start = (bf16[128,128]{1,0:T(8,128)(2,1)S(1)}, bf16[128,128]{1,0:T(8,128)(2,1)S(1)}, u32[]{:S(2)}, u32[]{:S(2)}) collective-permute-start(bf16[128,128]{1,0:T(8,128)(2,1)S(1)} %get-tuple-element.26), channel_id=1, source_target_pairs={{0,0},{1,32},{2,64},{3,96},{4,128},{5,160},{6,192},{7,224},{8,256}... | collective-permute-start | bytes 98312 | tf_op jit(solution)/shard_map/ppermute | solution.py:178
  19.6 14.0 %collective-permute-start.1 = (bf16[128,128]{1,0:T(8,128)(2,1)S(1)}, bf16[128,128]{1,0:T(8,128)(2,1)S(1)}, u32[]{:S(2)}, u32[]{:S(2)}) collective-permute-start(bf16[128,128]{1,0:T(8,128)(2,1)S(1)} %get-tuple-element.25), channel_id=1, source_target_pairs={{0,16},{1,48},{2,80},{3,112},{4,144},{5,176},{6,208},{7,240},{8,27... | collective-permute-start | bytes 98312 | tf_op jit(solution)/shard_map/ppermute | solution.py:178
  33.7 14.1 %collective-permute-start.2 = (bf16[128,256]{1,0:T(8,128)(2,1)S(1)}, bf16[128,256]{1,0:T(8,128)(2,1)S(1)}, u32[]{:S(2)}, u32[]{:S(2)}) collective-permute-start(bf16[128,256]{1,0:T(8,128)(2,1)S(1)} %maximum_select_fusion.1), channel_id=1, source_target_pairs={{0,48},{16,0},{32,16},{48,32},{1,49},{17,1},{33,17},{49,33},{2,50}... | collective-permute-start | bytes 196616 | tf_op jit(solution)/shard_map/ppermute | solution.py:29
  41.5 11.9 %collective-permute-start.3 = (bf16[128,256]{1,0:T(8,128)(2,1)S(1)}, bf16[128,256]{1,0:T(8,128)(2,1)S(1)}, u32[]{:S(2)}, u32[]{:S(2)}) collective-permute-start(bf16[128,256]{1,0:T(8,128)(2,1)S(1)} %maximum_select_fusion.1), channel_id=1, source_target_pairs={{0,32},{16,48},{32,0},{48,16},{1,33},{17,49},{33,1},{49,17},{2,34}... | collective-permute-start | bytes 196616 | tf_op jit(solution)/shard_map/ppermute | solution.py:29
  43.7 9.9 %collective-permute-start.4 = (bf16[128,256]{1,0:T(8,128)(2,1)S(1)}, bf16[128,256]{1,0:T(8,128)(2,1)S(1)}, u32[]{:S(2)}, u32[]{:S(2)}) collective-permute-start(bf16[128,256]{1,0:T(8,128)(2,1)S(1)} %maximum_select_fusion.1), channel_id=1, source_target_pairs={{0,16},{16,32},{32,48},{48,0},{1,17},{17,33},{33,49},{49,1},{2,18}... | collective-permute-start | bytes 196616 | tf_op jit(solution)/shard_map/ppermute | solution.py:29
  53.7 10.3 %collective-permute-start.5 = (bf16[512,256]{1,0:T(8,128)(2,1)S(1)}, bf16[512,256]{1,0:T(8,128)(2,1)S(1)}, u32[]{:S(2)}, u32[]{:S(2)}) collective-permute-start(bf16[512,256]{1,0:T(8,128)(2,1)S(1)} %bitcast.191), channel_id=1, source_target_pairs={{0,448},{64,0},{128,64},{192,128},{256,192},{320,256},{384,320},{4... | collective-permute-start | bytes 786440 | tf_op jit(solution)/shard_map/ppermute | solution.py:29
  55.6 11.5 %collective-permute-start.9 = (bf16[512,256]{1,0:T(8,128)(2,1)S(1)}, bf16[512,256]{1,0:T(8,128)(2,1)S(1)}, u32[]{:S(2)}, u32[]{:S(2)}) collective-permute-start(bf16[512,256]{1,0:T(8,128)(2,1)S(1)} %bitcast.192), channel_id=1, source_target_pairs={{0,64},{64,128},{128,192},{192,256},{256,320},{320,384},{384,448},... | collective-permute-start | bytes 786440 | tf_op jit(solution)/shard_map/ppermute | solution.py:29
  64.0 11.0 %collective-permute-start.6 = (bf16[512,256]{1,0:T(8,128)(2,1)S(1)}, bf16[512,256]{1,0:T(8,128)(2,1)S(1)}, u32[]{:S(2)}, u32[]{:S(2)}) collective-permute-start(bf16[512,256]{1,0:T(8,128)(2,1)S(1)} %collective-permute-done.5), channel_id=1, source_target_pairs={{0,448},{64,0},{128,64},{192,128},{256,192},{320,256},{384,320},{4... | collective-permute-start | bytes 786440 | tf_op jit(solution)/shard_map/ppermute | solution.py:29
  67.1 11.9 %collective-permute-start.10 = (bf16[512,256]{1,0:T(8,128)(2,1)S(1)}, bf16[512,256]{1,0:T(8,128)(2,1)S(1)}, u32[]{:S(2)}, u32[]{:S(2)}) collective-permute-start(bf16[512,256]{1,0:T(8,128)(2,1)S(1)} %collective-permute-done.9), channel_id=1, source_target_pairs={{0,64},{64,128},{128,192},{192,256},{256,320},{320,384},{384,448},... | collective-permute-start | bytes 786440 | tf_op jit(solution)/shard_map/ppermute | solution.py:29
  75.0 17.1 %collective-permute-start.7 = (bf16[512,256]{1,0:T(8,128)(2,1)S(1)}, bf16[512,256]{1,0:T(8,128)(2,1)S(1)}, u32[]{:S(2)}, u32[]{:S(2)}) collective-permute-start(bf16[512,256]{1,0:T(8,128)(2,1)S(1)} %collective-permute-done.6), channel_id=1, source_target_pairs={{0,448},{64,0},{128,64},{192,128},{256,192},{320,256},{384,320},{4... | collective-permute-start | bytes 786440 | tf_op jit(solution)/shard_map/ppermute | solution.py:29
  79.0 11.2 %collective-permute-start.11 = (bf16[512,256]{1,0:T(8,128)(2,1)S(1)}, bf16[512,256]{1,0:T(8,128)(2,1)S(1)}, u32[]{:S(2)}, u32[]{:S(2)}) collective-permute-start(bf16[512,256]{1,0:T(8,128)(2,1)S(1)} %collective-permute-done.10), channel_id=1, source_target_pairs={{0,64},{64,128},{128,192},{192,256},{256,320},{320,384},{384,448},... | collective-permute-start | bytes 786440 | tf_op jit(solution)/shard_map/ppermute | solution.py:29
  117.8 10.0 %collective-permute-start.15 = (f32[128,256]{1,0:T(8,128)S(1)}, f32[128,256]{1,0:T(8,128)S(1)}, u32[]{:S(2)}, u32[]{:S(2)}) collective-permute-start(f32[128,256]{1,0:T(8,128)S(1)} %add_select_fusion.2), channel_id=1, source_target_pairs={{0,4},{4,0},{8,12},{12,8},{1,5},{5,1},{9,13},{13,9},{2,6},{6,2},{1... | collective-permute-start | bytes 393224 | tf_op jit(solution)/shard_map/ppermute | solution.py:193
  127.8 11.7 %collective-permute-start.16 = (f32[128,256]{1,0:T(8,128)S(1)}, f32[128,256]{1,0:T(8,128)S(1)}, u32[]{:S(2)}, u32[]{:S(2)}) collective-permute-start(f32[128,256]{1,0:T(8,128)S(1)} %add_select_fusion.1), channel_id=1, source_target_pairs={{0,8},{4,12},{8,0},{12,4},{1,9},{5,13},{9,1},{13,5},{2,10},{6,14},... | collective-permute-start | bytes 393224 | tf_op jit(solution)/shard_map/ppermute | solution.py:193
  139.6 10.3 %collective-permute-start.17 = (bf16[128,256]{1,0:T(8,128)(2,1)S(1)}, bf16[128,256]{1,0:T(8,128)(2,1)S(1)}, u32[]{:S(2)}, u32[]{:S(2)}) collective-permute-start(bf16[128,256]{1,0:T(8,128)(2,1)S(1)} %get-tuple-element.17), channel_id=1, source_target_pairs={{0,48},{16,0},{32,16},{48,32},{1,49},{17,1},{33,17},{49,33},{2,50}... | collective-permute-start | bytes 196616 | tf_op jit(solution)/shard_map/ppermute | solution.py:29
  143.6 11.2 %collective-permute-start.18 = (bf16[128,256]{1,0:T(8,128)(2,1)S(1)}, bf16[128,256]{1,0:T(8,128)(2,1)S(1)}, u32[]{:S(2)}, u32[]{:S(2)}) collective-permute-start(bf16[128,256]{1,0:T(8,128)(2,1)S(1)} %get-tuple-element.17), channel_id=1, source_target_pairs={{0,32},{16,48},{32,0},{48,16},{1,33},{17,49},{33,1},{49,17},{2,34}... | collective-permute-start | bytes 196616 | tf_op jit(solution)/shard_map/ppermute | solution.py:29
  289.7 11.9 %collective-permute-start.28 = (bf16[64,128]{1,0:T(8,128)(2,1)S(1)}, bf16[64,128]{1,0:T(8,128)(2,1)}, u32[]{:S(2)}, u32[]{:S(2)}) collective-permute-start(bf16[64,128]{1,0:T(8,128)(2,1)S(1)} %slice_reduce_fusion), channel_id=1, source_target_pairs={{0,48},{16,0},{32,16},{48,32},{1,49},{17,1},{33,17},{49,33},{2,50}... | collective-permute-start | bytes 49160 | tf_op jit(solution)/shard_map/ppermute | solution.py:29
  291.7 11.3 %collective-permute-start.29 = (bf16[64,128]{1,0:T(8,128)(2,1)S(1)}, bf16[64,128]{1,0:T(8,128)(2,1)}, u32[]{:S(2)}, u32[]{:S(2)}) collective-permute-start(bf16[64,128]{1,0:T(8,128)(2,1)S(1)} %slice_reduce_fusion), channel_id=1, source_target_pairs={{0,32},{16,48},{32,0},{48,16},{1,33},{17,49},{33,1},{49,17},{2,34}... | collective-permute-start | bytes 49160 | tf_op jit(solution)/shard_map/ppermute | solution.py:29
  312.0 22.7 %collective-permute-start.31 = (bf16[4,64,128]{2,1,0:T(8,128)(2,1)S(1)}, bf16[4,64,128]{2,1,0:T(8,128)(2,1)S(1)}, u32[]{:S(2)}, u32[]{:S(2)}) collective-permute-start(bf16[4,64,128]{2,1,0:T(8,128)(2,1)S(1)} %get-tuple-element.15), channel_id=1, source_target_pairs={{0,448},{64,0},{128,64},{192,128},{256,192},{320,256},{384,320},{4... | collective-permute-start | bytes 196616 | tf_op jit(solution)/shard_map/ppermute | solution.py:29
  317.7 21.1 %collective-permute-start.32 = (bf16[4,64,128]{2,1,0:T(8,128)(2,1)S(1)}, bf16[4,64,128]{2,1,0:T(8,128)(2,1)S(1)}, u32[]{:S(2)}, u32[]{:S(2)}) collective-permute-start(bf16[4,64,128]{2,1,0:T(8,128)(2,1)S(1)} %get-tuple-element.15), channel_id=1, source_target_pairs={{0,384},{64,448},{128,0},{192,64},{256,128},{320,192},{384,256},{4... | collective-permute-start | bytes 196616 | tf_op jit(solution)/shard_map/ppermute | solution.py:29
  320.0 20.8 %collective-permute-start.33 = (bf16[4,64,128]{2,1,0:T(8,128)(2,1)S(1)}, bf16[4,64,128]{2,1,0:T(8,128)(2,1)S(1)}, u32[]{:S(2)}, u32[]{:S(2)}) collective-permute-start(bf16[4,64,128]{2,1,0:T(8,128)(2,1)S(1)} %get-tuple-element.15), channel_id=1, source_target_pairs={{0,320},{64,384},{128,448},{192,0},{256,64},{320,128},{384,192},{4... | collective-permute-start | bytes 196616 | tf_op jit(solution)/shard_map/ppermute | solution.py:29
  325.6 15.2 %collective-permute-start.34 = (bf16[4,64,128]{2,1,0:T(8,128)(2,1)S(1)}, bf16[4,64,128]{2,1,0:T(8,128)(2,1)S(1)}, u32[]{:S(2)}, u32[]{:S(2)}) collective-permute-start(bf16[4,64,128]{2,1,0:T(8,128)(2,1)S(1)} %get-tuple-element.15), channel_id=1, source_target_pairs={{0,256},{64,320},{128,384},{192,448},{256,0},{320,64},{384,128},{4... | collective-permute-start | bytes 196616 | tf_op jit(solution)/shard_map/ppermute | solution.py:29
  329.4 11.4 %collective-permute-start.35 = (bf16[4,64,128]{2,1,0:T(8,128)(2,1)S(1)}, bf16[4,64,128]{2,1,0:T(8,128)(2,1)S(1)}, u32[]{:S(2)}, u32[]{:S(2)}) collective-permute-start(bf16[4,64,128]{2,1,0:T(8,128)(2,1)S(1)} %get-tuple-element.15), channel_id=1, source_target_pairs={{0,192},{64,256},{128,320},{192,384},{256,448},{320,0},{384,64},{4... | collective-permute-start | bytes 196616 | tf_op jit(solution)/shard_map/ppermute | solution.py:29
  (23 other events, 322.5 us)
Sparse Core Ops, SparseCore 0:
  10.2 50.5 all-gather.4
  105.4 44.8 all-gather.6

commit v2 on v1

v2 whole, which is shorter than its diff:
```python
import jax
import jax.numpy as jnp
from jax import lax
from jax.experimental import pallas as pl
from jax.experimental.pallas import tpu as pltpu
from jax.sharding import Mesh
from jax.sharding import PartitionSpec as P

DP = ("z", "yh")
TN = ("x", "yl", "c")
IMAGE_SHARE = 128
BF = jnp.bfloat16
F32 = jnp.float32


def hold(value):
    return lax.reduce_precision(value, 8, 7)


def split3(value):
    high = hold(value)
    rest = value - high
    mid = hold(rest)
    return high, mid, rest - mid


def broadcast_gather(block, axes):
    count = lax.axis_size(axes)
    return lax.all_to_all(jnp.broadcast_to(block[None], (count,) + block.shape), axes, 0, 0, tiled=True)


def parity_sign(value):
    count = jnp.zeros_like(value)
    for place in range(16):
        count = count + (value >> place & 1)
    return 1 - 2 * (count % 2)


def layer_norm(values):
    centred = values - jnp.mean(values, axis=-1, keepdims=True)
    spread = jnp.mean(centred * centred, axis=-1, keepdims=True)
    return centred * lax.rsqrt(spread + 1e-06)


def project_kernel(x_ref, w_ref, out_ref, stat_ref):
    own = w_ref.shape[1]
    total = jnp.zeros(out_ref.shape, F32)
    for b in range(x_ref.shape[0]):
        total += jnp.dot(x_ref[b], w_ref[b * own : (b + 1) * own, :], preferred_element_type=F32)
    mean = jnp.sum(total, axis=1, keepdims=True) * (1.0 / own)
    centred = total - mean
    out_ref[...] = centred.astype(BF)
    spread = jnp.sum(centred * centred, axis=1, keepdims=True)
    lane = lax.broadcasted_iota(jnp.int32, stat_ref.shape, 1)
    stat_ref[...] = jnp.where(lane == 0, mean, spread)


def moment_kernel(
    pos_ref, mine_ref, other_ref, adj_ref, rstd_ref, gain_ref, prev_ref, rot_ref, sign_ref,
    out_ref, basis_ref, sums_ref, f_ref,
):
    blocks, rows, own = f_ref.shape
    part = out_ref.shape[2]
    core = lax.rem(pos_ref[0], 2)
    rstd = rstd_ref[...]
    total = jnp.zeros((rows, own), F32)
    for j in range(blocks):
        source, q, side = (mine_ref, j, core) if j < blocks // 2 else (other_ref, j - blocks // 2, 1 - core)
        b = 2 * q + side
        value = (source[q, :rows, :].astype(F32) + adj_ref[:, j : j + 1]) * rstd * gain_ref[b]
        feature = value.astype(BF)
        f_ref[b] = feature
        feature = feature.astype(F32)
        sums_ref[b] = jnp.sum(feature, axis=0, keepdims=True)
        shifted = (feature - prev_ref[b]).astype(BF)
        turn = rot_ref[pl.ds(pl.multiple_of(b * own, own), own), :]
        total += jnp.dot(shifted, turn, preferred_element_type=F32)
    basis_ref[...] = total.astype(BF) * sign_ref[...]
    own_t = f_ref[pos_ref[0]].astype(F32).T
    own_col = jnp.sum(own_t, axis=1, keepdims=True)
    own_t = own_t.astype(BF)
    for b in range(blocks):
        block = jnp.dot(own_t, f_ref[b], preferred_element_type=F32) - own_col * (sums_ref[b] * (1.0 / rows))
        block = block.astype(BF)
        for h in range(2):
            out_ref[2 * b + h] = block[:, h * part : (h + 1) * part]


def hadamard_kernel(scale_ref, basis_ref, table_ref, out_ref):
    blocks, few, own = basis_ref.shape
    flat = basis_ref[...].reshape(blocks * few, own)
    mixed = jnp.dot(flat, table_ref[...], preferred_element_type=F32) * scale_ref[0]
    parts = [mixed[b * few : (b + 1) * few] for b in range(blocks)]
    step = 1
    while step < blocks:
        parts = [
            parts[b - step] - parts[b] if b & step else parts[b] + parts[b + step] for b in range(blocks)
        ]
        step *= 2
    for b in range(blocks):
        out_ref[b] = parts[b].astype(BF)


def grad_kernel(pos_ref, target_ref, pred_ref, w_ref, normed_ref, sums_ref, out_ref):
    chunks, _, part = out_ref.shape
    depth = normed_ref.shape[1] // chunks
    residual = pred_ref[...] - target_ref[...].astype(F32)
    weighted = residual * w_ref[...]
    loss = jnp.sum(weighted * residual, axis=0, keepdims=True)
    grad = lax.dot_general(
        normed_ref[...], weighted.astype(BF), (((0,), (0,)), ((), ())), preferred_element_type=F32
    ).astype(BF)
    row = lax.broadcasted_iota(jnp.int32, (16, part), 0)

    def parts(value):
        high = value.astype(BF).astype(F32)
        rest = value - high
        mid = rest.astype(BF).astype(F32)
        return [high, mid, rest - mid]

    own_row = sums_ref[pos_ref[0]]
    fixed = []
    for h in range(2):
        fixed += parts(own_row[:, h * part : (h + 1) * part])
    for h in range(2):
        fixed += parts(loss[:, h * part : (h + 1) * part])
    for d in range(chunks):
        for h in range(2):
            out_ref[d, h * depth : (h + 1) * depth, :] = grad[
                d * depth : (d + 1) * depth, h * part : (h + 1) * part
            ]
        tile = jnp.zeros((16, part), F32)
        here = sums_ref[d // 2][:, (d % 2) * part : (d % 2 + 1) * part]
        for i, piece in enumerate(fixed + parts(here)):
            tile = jnp.where(row == i, piece, tile)
        out_ref[d, 2 * depth :, :] = tile.astype(BF)


def body(
    teacher_in,
    out_proj,
    final_gain,
    mean_prev,
    rotation,
    signs,
    prev_scale,
    student_in,
    head_weight,
    image_ids,
):
    rows, own = teacher_in.shape
    part = out_proj.shape[1]
    width = final_gain.shape[0]
    blocks = width // own
    chunks = width // part
    depth = student_in.shape[1] // chunks
    all_tokens = image_ids.shape[0]
    image_count = all_tokens // IMAGE_SHARE
    dpos = lax.axis_index(DP)
    tpos = lax.axis_index(TN)

    side = dpos % 2
    halves = out_proj.reshape(2, part, part)
    got = []
    for k in range(2):
        send = lax.dynamic_index_in_dim(halves, (side + k) % 2, 0, keepdims=False)
        route = []
        for d in range(chunks):
            for t in range(blocks):
                route.append((d * blocks + t, (2 * t + (d % 2 ^ k)) * blocks + d // 2))
        got.append(lax.ppermute(send, DP + TN, route))
    strip = jnp.where(
        side == 0, jnp.concatenate(got, axis=1), jnp.concatenate(got[::-1], axis=1)
    )
    proj = broadcast_gather(strip, DP).reshape(width, own)
    teacher = lax.all_gather(teacher_in, TN, axis=0, tiled=False)

    normed = layer_norm(student_in.astype(F32)).astype(BF)
    predicted = jnp.dot(normed, head_weight, preferred_element_type=F32)
    image_nums = jnp.arange(image_count, dtype=jnp.int32)
    counts = jnp.sum((image_ids[None, :] == image_nums[:, None]).astype(F32), axis=1)
    own_ids = lax.dynamic_slice_in_dim(image_ids, dpos * rows, rows, 0)
    token_counts = jnp.sum(
        jnp.where(own_ids[:, None] == image_nums[None, :], counts[None, :], 0.0), axis=1, keepdims=True
    )
    token_weight = 1.0 / token_counts

    raw, stat = pl.pallas_call(
        project_kernel,
        out_shape=(jax.ShapeDtypeStruct((rows, own), BF), jax.ShapeDtypeStruct((rows, 2), F32)),
        compiler_params=pltpu.CompilerParams(vmem_limit_bytes=40 << 20),
        cost_estimate=pl.CostEstimate(flops=2 * rows * width * own, bytes_accessed=8 << 20, transcendentals=0),
    )(teacher, proj)
    pieces = jnp.stack(split3(stat.T)).reshape(6 * rows // own, own).astype(BF)
    spare = -pieces.shape[0] % 16
    packed = jnp.concatenate([raw, pieces, jnp.zeros((spare, own), BF)])
    mine = broadcast_gather(packed, TN[:2])
    other = lax.ppermute(mine, "c", [(0, 1), (1, 0)])
    first = tpos % 2 == 0

    def unpack(block):
        tail = block[:, rows : rows + pieces.shape[0], :].astype(F32)
        return tail.reshape(blocks // 2, 3, 2, rows).sum(1)

    stat_mine, stat_other = unpack(mine), unpack(other)
    stats = jnp.stack(
        [jnp.where(first, stat_mine, stat_other), jnp.where(first, stat_other, stat_mine)], axis=1
    ).reshape(blocks, 2, rows)
    mean = jnp.mean(stats[:, 0], axis=0)
    adjust = stats[:, 0] - mean
    variance = (jnp.sum(stats[:, 1], axis=0) + own * jnp.sum(adjust * adjust, axis=0)) / width
    rstd = lax.rsqrt(variance + 1e-06)
    adjust = jnp.concatenate([stat_mine[:, 0], stat_other[:, 0]]) - mean
    scale = 1.0 / (jnp.sqrt(F32(width)) * prev_scale)
    index_row = lax.broadcasted_iota(jnp.int32, (own, own), 0)
    index_col = lax.broadcasted_iota(jnp.int32, (own, own), 1)
    table = parity_sign(index_row & index_col).astype(BF)

    smem, vmem = pl.BlockSpec(memory_space=pltpu.SMEM), pl.BlockSpec(memory_space=pltpu.VMEM)
    moment, basis, sums = pl.pallas_call(
        moment_kernel,
        out_shape=(
            jax.ShapeDtypeStruct((chunks, own, part), BF),
            jax.ShapeDtypeStruct((rows, own), BF),
            jax.ShapeDtypeStruct((blocks, 1, own), F32),
        ),
        in_specs=[smem] + [vmem] * 8,
        out_specs=(vmem,) * 3,
        scratch_shapes=[pltpu.VMEM((blocks, rows, own), BF)],
        compiler_params=pltpu.CompilerParams(vmem_limit_bytes=40 << 20),
        cost_estimate=pl.CostEstimate(flops=4 * rows * width * own, bytes_accessed=12 << 20, transcendentals=0),
    )(
        tpos.reshape(1),
        mine,
        other,
        adjust.T,
        rstd[:, None],
        final_gain.reshape(blocks, 1, own),
        mean_prev.reshape(blocks, 1, own),
        rotation,
        (2 * signs - 1).astype(BF)[None, :],
    )
    within = lax.psum_scatter(moment, "z", scatter_dimension=0, tiled=True)
    within = lax.psum_scatter(within, "yh", scatter_dimension=0, tiled=True)

    lines = lax.all_to_all(basis.reshape(blocks, rows // blocks, own), TN, 0, 0, tiled=True)
    lines = pl.pallas_call(
        hadamard_kernel,
        out_shape=jax.ShapeDtypeStruct(lines.shape, BF),
        in_specs=[smem, vmem, vmem],
        out_specs=vmem,
        compiler_params=pltpu.CompilerParams(vmem_limit_bytes=24 << 20),
    )(scale, lines, table)
    target = lax.all_to_all(lines, TN, 0, 0, tiled=True).reshape(rows, own)

    sent = pl.pallas_call(
        grad_kernel,
        out_shape=jax.ShapeDtypeStruct((chunks, 2 * depth + 16, part), BF),
        in_specs=[smem] + [vmem] * 5,
        out_specs=vmem,
        compiler_params=pltpu.CompilerParams(vmem_limit_bytes=24 << 20),
    )(tpos.reshape(1), target, predicted, token_weight, normed, sums)
    taken = lax.all_to_all(sent, DP, 0, 0, tiled=True)

    grad_own = jnp.sum(taken[:, : 2 * depth, :].astype(F32), axis=0).astype(BF)
    grads = broadcast_gather(grad_own, DP).reshape(chunks, 2, depth, part)
    grad_head = grads.transpose(0, 2, 1, 3).reshape(chunks * depth, own).astype(F32)

    tail = taken[:, 2 * depth :, :].astype(F32)
    sums_t = tail[:, 0:6].reshape(chunks, 2, 3, part).sum(2).reshape(chunks, own)
    loss = tail[:, 6:12].reshape(chunks, 2, 3, part).sum((0, 2)).reshape(own)
    sums_d = tail[:, 12:15].sum(1)
    new_mean = jnp.sum(sums_t, axis=0) / all_tokens
    mean_d = jnp.sum(sums_d, axis=0) / all_tokens
    off_t = sums_t / rows - new_mean
    off_d = sums_d / rows - mean_d
    between = lax.dot_general(
        off_t, off_d, (((0,), (0,)), ((), ())), precision=lax.Precision.HIGHEST, preferred_element_type=F32
    )
    new_cov = (within.reshape(own, part).astype(F32) + between * rows) / all_tokens
    return (new_cov, new_mean, grad_head, loss / image_count)


def solution(mesh):
    z, y, x = 8, 4, 4
    if mesh.devices.size != 512:
        z, y, x = 2, mesh.shape["dp"] // 2, mesh.shape["tensor"] // 4
    inner = Mesh(mesh.devices.reshape(z, y, x, 2, 2), DP + TN)
    return jax.shard_map(
        body,
        mesh=inner,
        in_specs=(
            P(DP, TN),
            P(TN, DP),
            P(),
            P(),
            P(None, TN),
            P(TN),
            P(),
            P(DP, None),
            P(None, TN),
            P(),
        ),
        out_specs=(P(TN, DP), P(TN), P(None, TN), P(TN)),
        check_vma=False,
    )
```

time: 357 us -> 268 us (0.75)
  the two profiles are of different devices: /device:TPU:4 before, /device:TPU:16 now
where the time goes in v2:
time: 268 us; the launch traced here: 267 us
  waiting for transfers between devices  108 us (40%)
  blocking collectives  65.7 us (25%)
  starting transfers between devices  47.6 us (18%)
  between operations  15 us (6%)
  local copies, waits for them, and re-layouts  11.7 us (4%)
  Pallas kernels  10.3 us (4%)
  other arithmetic  6.4 us (2%)
    all_to_all x2, waiting for transfers between devices, broadcast_gather(): lax.all_to_all(jnp.broadcast_to(block[None], (count,) + block.shape), axe...  75.4 us
    all_to_all x1, blocking collectives, broadcast_gather(): lax.all_to_all(jnp.broadcast_to(block[None], (count,) + block.shape), axe...  37.8 us
    all_to_all x2, starting transfers between devices, broadcast_gather(): lax.all_to_all(jnp.broadcast_to(block[None], (count,) + block.shape), axe...  30 us
    all_to_all x1, blocking collectives, body(): taken = lax.all_to_all(sent, DP, 0, 0, tiled=True)  27.9 us
    reduce_scatter x1, waiting for transfers between devices, body(): within = lax.psum_scatter(within, 'yh', scatter_dimension=0, tiled=True)  12.5 us
    ppermute x2, starting transfers between devices, body(): got.append(lax.ppermute(send, DP + TN, route))  8.27 us
    pallas_call x1, Pallas kernels, body(): pl.pallas_call(moment_kernel, out_shape=(jax.ShapeDtypeStruct((chunks, ow...  7.23 us
    all_to_all x1, waiting for transfers between devices, body(): lax.all_to_all(basis.reshape(blocks, rows // blocks, own), TN, 0, 0, tile...  7.05 us
  transfers between devices with their start and end apart: 10, of which 7 were waited for; matrix products, arithmetic and copies ran while one was open for 4% of the time, Pallas kernels for 1%

profile of v2, /device:TPU:16, one launch (start us, length us, event | category | flops | bytes accessed | tf_op | source)
XLA Modules:
  0.0 266.6 jit_solution(15316909315774195879)
XLA Ops:
  9.4 7.6 %collective-permute-start.1 = (bf16[128,128]{1,0:T(8,128)(2,1)S(1)}, bf16[128,128]{1,0:T(8,128)(2,1)S(1)}, u32[]{:S(2)}, u32[]{:S(2)}) collective-permute-start(bf16[128,128]{1,0:T(8,128)(2,1)S(1)} %get-tuple-element.28), channel_id=1, source_target_pairs={{0,16},{1,48},{2,80},{3,112},{4,144},{5,176},{6,208},{7,240},{8,27... | collective-permute-start | bytes 98312 | tf_op jit(solution)/shard_map/ppermute | solution.py:171
  17.0 2.2 collective-permute-done.1
  19.2 1.6 broadcast_in_dim.22
  20.8 22.7 %all-to-all-start = ((bf16[32,128,256]{2,1,0:T(8,128)(2,1)}), bf16[32,128,256]{2,1,0:T(8,128)(2,1)S(1)}, u32[]{:S(2)}, u32[]{:S(2)}) async-start(bf16[32,128,256]{2,1,0:T(8,128)(2,1)} %broadcast_in_dim.22), calls=%async_computation | async-start | bytes 4194304 | tf_op jit(solution)/shard_map/all_to_all | solution.py:29
  43.6 59.8 %all-to-all-done = bf16[32,128,256]{2,1,0:T(8,128)(2,1)S(1)} async-done(((bf16[32,128,256]{2,1,0:T(8,128)(2,1)}), bf16[32,128,256]{2,1,0:T(8,128)(2,1)S(1)}, u32[]{:S(2)}, u32[]{:S(2)}) %all-to-all-start) | async-done | bytes 2097184 | tf_op jit(solution)/shard_map/all_to_all | solution.py:29
  103.4 2.2 copy-done.1
  105.6 1.4 shard_map.129
  107.8 37.8 %all_to_all.30.mine_ref = bf16[8,528,256]{2,1,0:T(8,128)(2,1)S(1)} all-to-all(bf16[8,528,256]{2,1,0:T(8,128)(2,1)S(1)} %broadcast_in_dim.24), channel_id=1, replica_groups=mesh['z'=8,'yh'=4,'x'=4,'yl'=2,'c'=2] {'x','yl'}, dimensions={0} | all-to-all | bytes 4325376 | tf_op jit(solution)/shard_map/all_to_all | solution.py:29
  145.6 2.0 collective-permute-start.2
  148.6 3.4 %collective-permute-done.2.other_ref = bf16[8,528,256]{2,1,0:T(8,128)(2,1)} collective-permute-done((bf16[8,528,256]{2,1,0:T(8,128)(2,1)S(1)}, bf16[8,528,256]{2,1,0:T(8,128)(2,1)}, u32[]{:S(2)}, u32[]{:S(2)}) %collective-permute-start.2) | collective-permute-done | bytes 2162720 | tf_op jit(solution)/shard_map/ppermute | solution.py:198
  153.9 1.6 copy-done.3
  155.5 7.2 %shard_map.130 = (bf16[32,256,128]{2,1,0:T(8,128)(2,1)S(1)}, bf16[512,256]{1,0:T(8,128)(2,1)}, f32[16,1,256]{2,1,0:T(1,128)S(1)}) custom-call(s32[1]{0:T(128)} %bitcast.pos_ref, bf16[8,528,256]{2,1,0:T(8,128)(2,1)S(1)} %all_to_all.30.mine_ref, bf16[8,528,256]{2,1,0:T(8,128)(2,1)} %collective-permute-done.2.other_ref, f32[512,16]{1,0:T(8,128)S(1)} %bitcast.78, ...), custom_call_target="tpu_custom_call" | custom-call | flops 2147483648 | bytes 12582912 | tf_op jit(solution)/shard_map/pallas_call | solution.py:220
  162.7 1.3 copy-done.2
  165.7 3.5 %all-to-all-start.2 = ((bf16[16,32,256]{2,1,0:T(8,128)(2,1)}), bf16[16,32,256]{2,1,0:T(8,128)(2,1)S(1)}, u32[]{:S(2)}, u32[]{:S(2)}) async-start(bf16[16,32,256]{2,1,0:T(8,128)(2,1)} %bitcast.19), calls=%async_computation.4 | async-start | bytes 524288 | tf_op jit(solution)/shard_map/all_to_all | solution.py:246
  170.2 7.0 %all-to-all-done.2.basis_ref = bf16[16,32,256]{2,1,0:T(8,128)(2,1)S(1)} async-done(((bf16[16,32,256]{2,1,0:T(8,128)(2,1)}), bf16[16,32,256]{2,1,0:T(8,128)(2,1)S(1)}, u32[]{:S(2)}, u32[]{:S(2)}) %all-to-all-start.2) | async-done | bytes 262176 | tf_op jit(solution)/shard_map/all_to_all | solution.py:246
  178.2 3.7 %all-to-all-start.3 = ((bf16[16,32,256]{2,1,0:T(8,128)(2,1)}), bf16[16,32,256]{2,1,0:T(8,128)(2,1)S(1)}, u32[]{:S(2)}, u32[]{:S(2)}) async-start(bf16[16,32,256]{2,1,0:T(8,128)(2,1)} %shard_map.131), calls=%async_computation.5 | async-start | bytes 524288 | tf_op jit(solution)/shard_map/all_to_all | solution.py:254
  181.9 1.5 fusion.3.normed_ref
  184.0 5.8 %all-to-all-done.3 = bf16[16,32,256]{2,1,0:T(8,128)(2,1)S(1)} async-done(((bf16[16,32,256]{2,1,0:T(8,128)(2,1)}), bf16[16,32,256]{2,1,0:T(8,128)(2,1)S(1)}, u32[]{:S(2)}, u32[]{:S(2)}) %all-to-all-start.3) | async-done | bytes 262176 | tf_op jit(solution)/shard_map/all_to_all | solution.py:254
  190.5 27.9 %all_to_all.31 = bf16[32,80,128]{2,1,0:T(8,128)(2,1)S(1)} all-to-all(bf16[32,80,128]{2,1,0:T(8,128)(2,1)S(1)} %shard_map.132), channel_id=1, replica_groups=mesh['z'=8,'yh'=4,'x'=4,'yl'=2,'c'=2] {'z','yh'}, dimensions={0} | all-to-all | bytes 1310720 | tf_op jit(solution)/shard_map/all_to_all | solution.py:263
  219.4 7.3 %all-to-all-start.5 = ((bf16[32,64,128]{2,1,0:T(8,128)(2,1)}), bf16[32,64,128]{2,1,0:T(8,128)(2,1)S(1)}, u32[]{:S(2)}, u32[]{:S(2)}) async-start(bf16[32,64,128]{2,1,0:T(8,128)(2,1)} %broadcast_in_dim.28), calls=%async_computation.7 | async-start | bytes 1048576 | tf_op jit(solution)/shard_map/all_to_all | solution.py:29
  228.1 15.6 %all-to-all-done.5 = bf16[32,64,128]{2,1,0:T(8,128)(2,1)S(1)} async-done(((bf16[32,64,128]{2,1,0:T(8,128)(2,1)}), bf16[32,64,128]{2,1,0:T(8,128)(2,1)S(1)}, u32[]{:S(2)}, u32[]{:S(2)}) %all-to-all-start.5) | async-done | bytes 524320 | tf_op jit(solution)/shard_map/all_to_all | solution.py:29
  244.6 1.0 copy.80
  245.7 12.5 %reduce-scatter.5.cloned.1.call-done = bf16[1,256,128]{2,1,0:T(8,128)(2,1)} async-done(((bf16[4,256,128]{2,1,0:T(8,128)(2,1)}), bf16[1,256,128]{2,1,0:T(8,128)(2,1)}) %reduce-scatter.5.cloned.1.call-update) | async-done | bytes 65552 | tf_op jit(solution)/shard_map/reduce_scatter | solution.py:244
  258.2 1.9 fusion.5
  (90 shorter events, 12.9 us)
Async XLA Ops:
  7.2 176.3 %copy-start = (bf16[1024,256]{1,0:T(8,128)(2,1)S(1)}, bf16[1024,256]{1,0:T(8,128)(2,1)}, u32[]{:S(2)}) copy-start(bf16[1024,256]{1,0:T(8,128)(2,1)} %param.18) | copy-start | bytes 1572868
  7.2 96.2 %all-gather.3.cloned.1.call-start = ((), (), s32[]{:S(2)}) async-start(), calls=%async_computation.10 | async-start | bytes 4456448 | tf_op jit(solution)/shard_map/all_gather | solution.py:176
  8.7 8.3 %collective-permute-start = (bf16[128,128]{1,0:T(8,128)(2,1)S(1)}, bf16[128,128]{1,0:T(8,128)(2,1)S(1)}, u32[]{:S(2)}, u32[]{:S(2)}) collective-permute-start(bf16[128,128]{1,0:T(8,128)(2,1)S(1)} %get-tuple-element.27), channel_id=1, source_target_pairs={{0,0},{1,32},{2,64},{3,96},{4,128},{5,160},{6,192},{7,224},{8,256}... | collective-permute-start | bytes 98312 | tf_op jit(solution)/shard_map/ppermute | solution.py:171
  9.4 9.8 %collective-permute-start.1 = (bf16[128,128]{1,0:T(8,128)(2,1)S(1)}, bf16[128,128]{1,0:T(8,128)(2,1)S(1)}, u32[]{:S(2)}, u32[]{:S(2)}) collective-permute-start(bf16[128,128]{1,0:T(8,128)(2,1)S(1)} %get-tuple-element.28), channel_id=1, source_target_pairs={{0,16},{1,48},{2,80},{3,112},{4,144},{5,176},{6,208},{7,240},{8,27... | collective-permute-start | bytes 98312 | tf_op jit(solution)/shard_map/ppermute | solution.py:171
  20.8 82.6 %all-to-all-start = ((bf16[32,128,256]{2,1,0:T(8,128)(2,1)}), bf16[32,128,256]{2,1,0:T(8,128)(2,1)S(1)}, u32[]{:S(2)}, u32[]{:S(2)}) async-start(bf16[32,128,256]{2,1,0:T(8,128)(2,1)} %broadcast_in_dim.22), calls=%async_computation | async-start | bytes 4194304 | tf_op jit(solution)/shard_map/all_to_all | solution.py:29
  43.5 183.4 %reduce-scatter.3.cloned.1.call-start = ((), (), s32[]{:S(2)}) async-start(), calls=%async_computation.8 | async-start | bytes 2359296 | tf_op jit(solution)/shard_map/reduce_scatter | solution.py:243
  103.4 2.2 copy-start.1
  107.8 39.9 %copy-start.9 = (s32[256]{0:T(256)S(1)}, s32[256]{0:T(256)}, u32[]{:S(2)}) copy-start(s32[256]{0:T(256)} %param.15) | copy-start | bytes 3076
  107.8 40.5 %copy-start.7 = (s32[16384]{0:T(1024)S(1)}, s32[16384]{0:T(1024)}, u32[]{:S(2)}) copy-start(s32[16384]{0:T(1024)} %param.19) | copy-start | bytes 196612
  145.6 8.3 %copy-start.4 = (f32[4096]{0:T(1024)S(1)}, f32[4096]{0:T(1024)}, u32[]{:S(2)}) copy-start(f32[4096]{0:T(1024)} %param.12) | copy-start | bytes 49156
  145.6 8.3 %copy-start.5 = (f32[4096]{0:T(1024)S(1)}, f32[4096]{0:T(1024)}, u32[]{:S(2)}) copy-start(f32[4096]{0:T(1024)} %param.13) | copy-start | bytes 49156
  145.6 6.4 %collective-permute-start.2 = (bf16[8,528,256]{2,1,0:T(8,128)(2,1)S(1)}, bf16[8,528,256]{2,1,0:T(8,128)(2,1)}, u32[]{:S(2)}, u32[]{:S(2)}) collective-permute-start(bf16[8,528,256]{2,1,0:T(8,128)(2,1)S(1)} %all_to_all.30.mine_ref), channel_id=1, source_target_pairs={{0,1},{1,0},{2,3},{3,2},{4,5},{5,4},{6,7},{7,6},{8,9},{9,8},{10,11... | collective-permute-start | bytes 6488072 | tf_op jit(solution)/shard_map/ppermute | solution.py:198
  153.9 1.6 copy-start.3
  162.7 1.4 copy-start.2
  164.1 1.4 copy-start.6
  165.7 11.6 %all-to-all-start.2 = ((bf16[16,32,256]{2,1,0:T(8,128)(2,1)}), bf16[16,32,256]{2,1,0:T(8,128)(2,1)S(1)}, u32[]{:S(2)}, u32[]{:S(2)}) async-start(bf16[16,32,256]{2,1,0:T(8,128)(2,1)} %bitcast.19), calls=%async_computation.4 | async-start | bytes 524288 | tf_op jit(solution)/shard_map/all_to_all | solution.py:246
  178.2 11.6 %all-to-all-start.3 = ((bf16[16,32,256]{2,1,0:T(8,128)(2,1)}), bf16[16,32,256]{2,1,0:T(8,128)(2,1)S(1)}, u32[]{:S(2)}, u32[]{:S(2)}) async-start(bf16[16,32,256]{2,1,0:T(8,128)(2,1)} %shard_map.131), calls=%async_computation.5 | async-start | bytes 524288 | tf_op jit(solution)/shard_map/all_to_all | solution.py:254
  219.4 24.3 %all-to-all-start.5 = ((bf16[32,64,128]{2,1,0:T(8,128)(2,1)}), bf16[32,64,128]{2,1,0:T(8,128)(2,1)S(1)}, u32[]{:S(2)}, u32[]{:S(2)}) async-start(bf16[32,64,128]{2,1,0:T(8,128)(2,1)} %broadcast_in_dim.28), calls=%async_computation.7 | async-start | bytes 1048576 | tf_op jit(solution)/shard_map/all_to_all | solution.py:29
  226.7 31.5 %reduce-scatter.5.cloned.1.call-start = ((), (), s32[]{:S(2)}) async-start(), calls=%async_computation.9 | async-start | bytes 327680 | tf_op jit(solution)/shard_map/reduce_scatter | solution.py:244
  226.9 31.3 %copy-start.8 = (f32[256]{0:T(256)}, f32[256]{0:T(256)S(1)}, u32[]{:S(2)}) copy-start(f32[256]{0:T(256)S(1)} %multiply_bitcast_fusion.2) | copy-start | bytes 3076
Sparse Core Ops, SparseCore 0:
  10.2 70.3 all-gather.2
  164.2 52.1 reduce-scatter.2
  230.3 27.8 reduce-scatter.4

commit v3 on v2

--- a/solution.py
+++ b/solution.py
@@ -27,6 +27,23 @@
 def broadcast_gather(block, axes):
     count = lax.axis_size(axes)
     return lax.all_to_all(jnp.broadcast_to(block[None], (count,) + block.shape), axes, 0, 0, tiled=True)
+
+
+def shift(block, axis, step):
+    count = lax.axis_size(axis)
+    return lax.ppermute(block, axis, [(i, (i + step) % count) for i in range(count)])
+
+
+def ring_gather(block, axis):
+    count = lax.axis_size(axis)
+    ahead, behind = [block], [block]
+    for _ in range(count // 2 - 1):
+        ahead.append(shift(ahead[-1], axis, -1))
+        behind.append(shift(behind[-1], axis, 1))
+    half = block.shape[0] // 2
+    far = jnp.concatenate([shift(ahead[-1][:half], axis, -1), shift(behind[-1][half:], axis, 1)])
+    blocks = ahead + [far] + behind[:0:-1]
+    return lax.dynamic_slice_in_dim(jnp.stack(blocks + blocks), count - lax.axis_index(axis), count, 0)
 
 
 def parity_sign(value):
@@ -136,6 +153,16 @@
         out_ref[d, 2 * depth :, :] = tile.astype(BF)
 
 
+def place_kernel(in_ref, out_ref):
+    chunks, tall, part = in_ref.shape
+    depth = tall // 2
+    for d in range(chunks):
+        for h in range(2):
+            out_ref[d * depth : (d + 1) * depth, h * part : (h + 1) * part] = in_ref[
+                d, h * depth : (h + 1) * depth, :
+            ].astype(F32)
+
+
 def body(
     teacher_in,
     out_proj,
@@ -172,7 +199,8 @@
     strip = jnp.where(
         side == 0, jnp.concatenate(got, axis=1), jnp.concatenate(got[::-1], axis=1)
     )
-    proj = broadcast_gather(strip, DP).reshape(width, own)
+    near = broadcast_gather(strip, "yh")
+    proj = ring_gather(near.reshape(-1, own), "z").reshape(width, own)
     teacher = lax.all_gather(teacher_in, TN, axis=0, tiled=False)
 
     normed = layer_norm(student_in.astype(F32)).astype(BF)
@@ -241,7 +269,6 @@
         (2 * signs - 1).astype(BF)[None, :],
     )
     within = lax.psum_scatter(moment, "z", scatter_dimension=0, tiled=True)
-    within = lax.psum_scatter(within, "yh", scatter_dimension=0, tiled=True)
 
     lines = lax.all_to_all(basis.reshape(blocks, rows // blocks, own), TN, 0, 0, tiled=True)
     lines = pl.pallas_call(
@@ -263,8 +290,14 @@
     taken = lax.all_to_all(sent, DP, 0, 0, tiled=True)
 
     grad_own = jnp.sum(taken[:, : 2 * depth, :].astype(F32), axis=0).astype(BF)
-    grads = broadcast_gather(grad_own, DP).reshape(chunks, 2, depth, part)
-    grad_head = grads.transpose(0, 2, 1, 3).reshape(chunks * depth, own).astype(F32)
+    within, grad_own = lax.optimization_barrier((within, grad_own))
+    within = lax.psum_scatter(within, "yh", scatter_dimension=0, tiled=True)
+    grad_head = pl.pallas_call(
+        place_kernel,
+        out_shape=jax.ShapeDtypeStruct((chunks * depth, own), F32),
+        in_specs=[vmem],
+        out_specs=vmem,
+    )(broadcast_gather(grad_own, DP))
 
     tail = taken[:, 2 * depth :, :].astype(F32)
     sums_t = tail[:, 0:6].reshape(chunks, 2, 3, part).sum(2).reshape(chunks, own)

time: 268 us -> 260 us (0.970)
  waiting for transfers between devices: 108 us -> 64.6 us
  starting transfers between devices: 47.6 us -> 69 us
  blocking collectives: 65.7 us -> 77.8 us
    all_to_all x2 -> x1, waiting for transfers between devices: 75.4 us -> 0.01 us  [broadcast_gather(): lax.all_to_all(jnp.broadcast_to(block[None], (count,) + block.shape), axe...]
    ppermute x0 -> x8, starting transfers between devices: none -> 43 us  [shift(): lax.ppermute(block, axis, [(i, (i + step) % count) for i in range(count)])]
    all_to_all x2 -> x1, starting transfers between devices: 30 us -> 8.4 us  [broadcast_gather(): lax.all_to_all(jnp.broadcast_to(block[None], (count,) + block.shape), axe...]
    reduce_scatter x1, waiting for transfers between devices: 12.5 us -> 31 us  [body(): within = lax.psum_scatter(within, 'yh', scatter_dimension=0, tiled=True)]
    ppermute x0 -> x8, waiting for transfers between devices: none -> 12.9 us  [shift(): lax.ppermute(block, axis, [(i, (i + step) % count) for i in range(count)])]
    all_to_all x1 -> x2, blocking collectives: 37.8 us -> 49.2 us  [broadcast_gather(): lax.all_to_all(jnp.broadcast_to(block[None], (count,) + block.shape), axe...]
    unnamed x23 -> x37, local copies, waits for them, and re-layouts: 6.34 us -> 6.33 us
  transfers between devices with their start and end apart: 10 -> 17, of which waited for: 7 -> 12; matrix products, arithmetic and copies ran while one was open for 4% -> 4% of each run, Pallas kernels for 1% -> 1%
where the time goes in v3:
time: 260 us; the launch traced here: 258 us
  blocking collectives  77.8 us (30%)
  starting transfers between devices  69 us (27%)
  waiting for transfers between devices  64.6 us (25%)
  between operations  15.3 us (6%)
  Pallas kernels  12.4 us (5%)
  local copies, waits for them, and re-layouts  9.54 us (4%)
  other arithmetic  7.54 us (3%)
    all_to_all x2, blocking collectives, broadcast_gather(): lax.all_to_all(jnp.broadcast_to(block[None], (count,) + block.shape), axe...  49.2 us
    ppermute x8, starting transfers between devices, shift(): lax.ppermute(block, axis, [(i, (i + step) % count) for i in range(count)])  43 us
    reduce_scatter x1, waiting for transfers between devices, body(): within = lax.psum_scatter(within, 'yh', scatter_dimension=0, tiled=True)  31 us
    all_to_all x1, blocking collectives, body(): taken = lax.all_to_all(sent, DP, 0, 0, tiled=True)  28.6 us
    ppermute x8, waiting for transfers between devices, shift(): lax.ppermute(block, axis, [(i, (i + step) % count) for i in range(count)])  12.9 us
    all_to_all x1, starting transfers between devices, broadcast_gather(): lax.all_to_all(jnp.broadcast_to(block[None], (count,) + block.shape), axe...  8.4 us
    ppermute x2, starting transfers between devices, body(): got.append(lax.ppermute(send, DP + TN, route))  8.27 us
    pallas_call x1, Pallas kernels, body(): pl.pallas_call(moment_kernel, out_shape=(jax.ShapeDtypeStruct((chunks, ow...  7.26 us
  transfers between devices with their start and end apart: 17, of which 12 were waited for; matrix products, arithmetic and copies ran while one was open for 4% of the time, Pallas kernels for 1%

profile of v3, /device:TPU:16, one launch (start us, length us, event | category | flops | bytes accessed | tf_op | source)
XLA Modules:
  0.0 258.5 jit_solution(15641642323490561340)
XLA Ops:
  9.5 7.6 %collective-permute-start.1 = (bf16[128,128]{1,0:T(8,128)(2,1)S(1)}, bf16[128,128]{1,0:T(8,128)(2,1)S(1)}, u32[]{:S(2)}, u32[]{:S(2)}) collective-permute-start(bf16[128,128]{1,0:T(8,128)(2,1)S(1)} %get-tuple-element.32), channel_id=1, source_target_pairs={{0,16},{1,48},{2,80},{3,112},{4,144},{5,176},{6,208},{7,240},{8,27... | collective-permute-start | bytes 98312 | tf_op jit(solution)/shard_map/ppermute | solution.py:198
  17.1 2.2 collective-permute-done.1
  19.3 15.4 %all_to_all.30 = bf16[4,128,256]{2,1,0:T(8,128)(2,1)S(1)} all-to-all(bf16[4,128,256]{2,1,0:T(8,128)(2,1)S(1)} %broadcast_in_dim.22), channel_id=1, replica_groups=mesh['z'=8,'yh'=4,'x'=4,'yl'=2,'c'=2] {'yh'}, dimensions={0} | all-to-all | bytes 524288 | tf_op jit(solution)/shard_map/all_to_all | solution.py:29
  34.7 18.6 %collective-permute-start.2 = (bf16[512,256]{1,0:T(8,128)(2,1)S(1)}, bf16[512,256]{1,0:T(8,128)(2,1)S(1)}, u32[]{:S(2)}, u32[]{:S(2)}) collective-permute-start(bf16[512,256]{1,0:T(8,128)(2,1)S(1)} %bitcast.102), channel_id=1, source_target_pairs={{0,448},{64,0},{128,64},{192,128},{256,192},{320,256},{384,320},{4... | collective-permute-start | bytes 786440 | tf_op jit(solution)/shard_map/ppermute | solution.py:34
  53.3 1.9 collective-permute-start.6
  55.2 1.9 collective-permute-done.2
  57.1 5.6 %collective-permute-start.3 = (bf16[512,256]{1,0:T(8,128)(2,1)S(1)}, bf16[512,256]{1,0:T(8,128)(2,1)S(1)}, u32[]{:S(2)}, u32[]{:S(2)}) collective-permute-start(bf16[512,256]{1,0:T(8,128)(2,1)S(1)} %collective-permute-done.2), channel_id=1, source_target_pairs={{0,448},{64,0},{128,64},{192,128},{256,192},{320,256},{384,320},{4... | collective-permute-start | bytes 786440 | tf_op jit(solution)/shard_map/ppermute | solution.py:34
  66.6 5.6 %collective-permute-start.4 = (bf16[512,256]{1,0:T(8,128)(2,1)S(1)}, bf16[512,256]{1,0:T(8,128)(2,1)S(1)}, u32[]{:S(2)}, u32[]{:S(2)}) collective-permute-start(bf16[512,256]{1,0:T(8,128)(2,1)S(1)} %collective-permute-done.3), channel_id=1, source_target_pairs={{0,448},{64,0},{128,64},{192,128},{256,192},{320,256},{384,320},{4... | collective-permute-start | bytes 786440 | tf_op jit(solution)/shard_map/ppermute | solution.py:34
  74.2 2.7 %collective-permute-done.4 = bf16[512,256]{1,0:T(8,128)(2,1)S(1)} collective-permute-done((bf16[512,256]{1,0:T(8,128)(2,1)S(1)}, bf16[512,256]{1,0:T(8,128)(2,1)S(1)}, u32[]{:S(2)}, u32[]{:S(2)}) %collective-permute-start.4) | collective-permute-done | bytes 262176 | tf_op jit(solution)/shard_map/ppermute | solution.py:34
  77.0 5.6 %collective-permute-start.5 = (bf16[256,256]{1,0:T(8,128)(2,1)S(1)}, bf16[256,256]{1,0:T(8,128)(2,1)S(1)}, u32[]{:S(2)}, u32[]{:S(2)}) collective-permute-start(bf16[256,256]{1,0:T(8,128)(2,1)S(1)} %slice.53), channel_id=1, source_target_pairs={{0,448},{64,0},{128,64},{192,128},{256,192},{320,256},{384,320},{4... | collective-permute-start | bytes 393224 | tf_op jit(solution)/shard_map/ppermute | solution.py:34
  82.8 1.9 collective-permute-start.9
  85.1 5.8 %collective-permute-done.9 = bf16[256,256]{1,0:T(8,128)(2,1)S(1)} collective-permute-done((bf16[256,256]{1,0:T(8,128)(2,1)S(1)}, bf16[256,256]{1,0:T(8,128)(2,1)S(1)}, u32[]{:S(2)}, u32[]{:S(2)}) %collective-permute-start.9) | collective-permute-done | bytes 131104 | tf_op jit(solution)/shard_map/ppermute | solution.py:34
  91.4 2.2 copy-done.1
  95.8 33.8 %all_to_all.31.mine_ref = bf16[8,528,256]{2,1,0:T(8,128)(2,1)S(1)} all-to-all(bf16[8,528,256]{2,1,0:T(8,128)(2,1)S(1)} %broadcast_in_dim.24), channel_id=1, replica_groups=mesh['z'=8,'yh'=4,'x'=4,'yl'=2,'c'=2] {'x','yl'}, dimensions={0} | all-to-all | bytes 4325376 | tf_op jit(solution)/shard_map/all_to_all | solution.py:29
  131.7 4.1 %collective-permute-done.10.other_ref = bf16[8,528,256]{2,1,0:T(8,128)(2,1)} collective-permute-done((bf16[8,528,256]{2,1,0:T(8,128)(2,1)S(1)}, bf16[8,528,256]{2,1,0:T(8,128)(2,1)}, u32[]{:S(2)}, u32[]{:S(2)}) %collective-permute-start.10) | collective-permute-done | bytes 2162720 | tf_op jit(solution)/shard_map/ppermute | solution.py:226
  139.4 7.3 %shard_map.130 = (bf16[32,256,128]{2,1,0:T(8,128)(2,1)S(1)}, bf16[512,256]{1,0:T(8,128)(2,1)}, f32[16,1,256]{2,1,0:T(1,128)S(1)}) custom-call(s32[1]{0:T(128)} %bitcast.pos_ref, bf16[8,528,256]{2,1,0:T(8,128)(2,1)S(1)} %all_to_all.31.mine_ref, bf16[8,528,256]{2,1,0:T(8,128)(2,1)} %collective-permute-done.10.other_ref, f32[512,16]{1,0:T(8,128)S(1)} %bitcast.99, ...), custom_call_target="tpu_custom_call" | custom-call | flops 2147483648 | bytes 12582912 | tf_op jit(solution)/shard_map/pallas_call | solution.py:248
  151.6 3.5 %all-to-all-start.2 = ((bf16[16,32,256]{2,1,0:T(8,128)(2,1)}), bf16[16,32,256]{2,1,0:T(8,128)(2,1)S(1)}, u32[]{:S(2)}, u32[]{:S(2)}) async-start(bf16[16,32,256]{2,1,0:T(8,128)(2,1)} %bitcast.27), calls=%async_computation.3 | async-start | bytes 524288 | tf_op jit(solution)/shard_map/all_to_all | solution.py:273
  156.2 7.0 %all-to-all-done.2.basis_ref = bf16[16,32,256]{2,1,0:T(8,128)(2,1)S(1)} async-done(((bf16[16,32,256]{2,1,0:T(8,128)(2,1)}), bf16[16,32,256]{2,1,0:T(8,128)(2,1)S(1)}, u32[]{:S(2)}, u32[]{:S(2)}) %all-to-all-start.2) | async-done | bytes 262176 | tf_op jit(solution)/shard_map/all_to_all | solution.py:273
  164.2 3.7 %all-to-all-start.3 = ((bf16[16,32,256]{2,1,0:T(8,128)(2,1)}), bf16[16,32,256]{2,1,0:T(8,128)(2,1)S(1)}, u32[]{:S(2)}, u32[]{:S(2)}) async-start(bf16[16,32,256]{2,1,0:T(8,128)(2,1)} %shard_map.131), calls=%async_computation.4 | async-start | bytes 524288 | tf_op jit(solution)/shard_map/all_to_all | solution.py:281
  169.9 6.0 %all-to-all-done.3 = bf16[16,32,256]{2,1,0:T(8,128)(2,1)S(1)} async-done(((bf16[16,32,256]{2,1,0:T(8,128)(2,1)}), bf16[16,32,256]{2,1,0:T(8,128)(2,1)S(1)}, u32[]{:S(2)}, u32[]{:S(2)}) %all-to-all-start.3) | async-done | bytes 262176 | tf_op jit(solution)/shard_map/all_to_all | solution.py:281
  176.6 28.6 %all_to_all.32 = bf16[32,80,128]{2,1,0:T(8,128)(2,1)S(1)} all-to-all(bf16[32,80,128]{2,1,0:T(8,128)(2,1)S(1)} %shard_map.132), channel_id=1, replica_groups=mesh['z'=8,'yh'=4,'x'=4,'yl'=2,'c'=2] {'z','yh'}, dimensions={0} | all-to-all | bytes 1310720 | tf_op jit(solution)/shard_map/all_to_all | solution.py:290
  206.3 8.4 %all-to-all-start.5 = ((bf16[32,64,128]{2,1,0:T(8,128)(2,1)}), bf16[32,64,128]{2,1,0:T(8,128)(2,1)S(1)}, u32[]{:S(2)}, u32[]{:S(2)}) async-start(bf16[32,64,128]{2,1,0:T(8,128)(2,1)} %broadcast_in_dim.28), calls=%async_computation.7 | async-start | bytes 1048576 | tf_op jit(solution)/shard_map/all_to_all | solution.py:29
  216.2 31.0 %reduce-scatter.5.cloned.1.call-done = bf16[1,256,128]{2,1,0:T(8,128)(2,1)} async-done(((bf16[4,256,128]{2,1,0:T(8,128)(2,1)}), bf16[1,256,128]{2,1,0:T(8,128)(2,1)}) %reduce-scatter.5.cloned.1.call-update) | async-done | bytes 65552 | tf_op jit(solution)/shard_map/reduce_scatter | solution.py:294
  249.8 2.1 shard_map.133
  (124 shorter events, 30.6 us)
Async XLA Ops:
  7.2 162.3 %copy-start = (bf16[1024,256]{1,0:T(8,128)(2,1)S(1)}, bf16[1024,256]{1,0:T(8,128)(2,1)}, u32[]{:S(2)}) copy-start(bf16[1024,256]{1,0:T(8,128)(2,1)} %param.18) | copy-start | bytes 1572868
  7.2 84.2 %all-gather.3.cloned.1.call-start = ((), (), s32[]{:S(2)}) async-start(), calls=%async_computation.10 | async-start | bytes 4456448 | tf_op jit(solution)/shard_map/all_gather | solution.py:204
  7.9 197.5 %reduce-scatter.3.cloned.1.call-start = ((), (), s32[]{:S(2)}) async-start(), calls=%async_computation.8 | async-start | bytes 2359296 | tf_op jit(solution)/shard_map/reduce_scatter | solution.py:271
  8.8 8.3 %collective-permute-start = (bf16[128,128]{1,0:T(8,128)(2,1)S(1)}, bf16[128,128]{1,0:T(8,128)(2,1)S(1)}, u32[]{:S(2)}, u32[]{:S(2)}) collective-permute-start(bf16[128,128]{1,0:T(8,128)(2,1)S(1)} %get-tuple-element.31), channel_id=1, source_target_pairs={{0,0},{1,32},{2,64},{3,96},{4,128},{5,160},{6,192},{7,224},{8,256}... | collective-permute-start | bytes 98312 | tf_op jit(solution)/shard_map/ppermute | solution.py:198
  9.5 9.8 %collective-permute-start.1 = (bf16[128,128]{1,0:T(8,128)(2,1)S(1)}, bf16[128,128]{1,0:T(8,128)(2,1)S(1)}, u32[]{:S(2)}, u32[]{:S(2)}) collective-permute-start(bf16[128,128]{1,0:T(8,128)(2,1)S(1)} %get-tuple-element.32), channel_id=1, source_target_pairs={{0,16},{1,48},{2,80},{3,112},{4,144},{5,176},{6,208},{7,240},{8,27... | collective-permute-start | bytes 98312 | tf_op jit(solution)/shard_map/ppermute | solution.py:198
  34.7 22.4 %collective-permute-start.2 = (bf16[512,256]{1,0:T(8,128)(2,1)S(1)}, bf16[512,256]{1,0:T(8,128)(2,1)S(1)}, u32[]{:S(2)}, u32[]{:S(2)}) collective-permute-start(bf16[512,256]{1,0:T(8,128)(2,1)S(1)} %bitcast.102), channel_id=1, source_target_pairs={{0,448},{64,0},{128,64},{192,128},{256,192},{320,256},{384,320},{4... | collective-permute-start | bytes 786440 | tf_op jit(solution)/shard_map/ppermute | solution.py:34
  53.3 9.5 %collective-permute-start.6 = (bf16[512,256]{1,0:T(8,128)(2,1)S(1)}, bf16[512,256]{1,0:T(8,128)(2,1)S(1)}, u32[]{:S(2)}, u32[]{:S(2)}) collective-permute-start(bf16[512,256]{1,0:T(8,128)(2,1)S(1)} %bitcast.103), channel_id=1, source_target_pairs={{0,64},{64,128},{128,192},{192,256},{256,320},{320,384},{384,448},... | collective-permute-start | bytes 786440 | tf_op jit(solution)/shard_map/ppermute | solution.py:34
  57.1 9.5 %collective-permute-start.3 = (bf16[512,256]{1,0:T(8,128)(2,1)S(1)}, bf16[512,256]{1,0:T(8,128)(2,1)S(1)}, u32[]{:S(2)}, u32[]{:S(2)}) collective-permute-start(bf16[512,256]{1,0:T(8,128)(2,1)S(1)} %collective-permute-done.2), channel_id=1, source_target_pairs={{0,448},{64,0},{128,64},{192,128},{256,192},{320,256},{384,320},{4... | collective-permute-start | bytes 786440 | tf_op jit(solution)/shard_map/ppermute | solution.py:34
  62.7 9.5 %collective-permute-start.7 = (bf16[512,256]{1,0:T(8,128)(2,1)S(1)}, bf16[512,256]{1,0:T(8,128)(2,1)S(1)}, u32[]{:S(2)}, u32[]{:S(2)}) collective-permute-start(bf16[512,256]{1,0:T(8,128)(2,1)S(1)} %collective-permute-done.6), channel_id=1, source_target_pairs={{0,64},{64,128},{128,192},{192,256},{256,320},{320,384},{384,448},... | collective-permute-start | bytes 786440 | tf_op jit(solution)/shard_map/ppermute | solution.py:34
  66.6 10.3 %collective-permute-start.4 = (bf16[512,256]{1,0:T(8,128)(2,1)S(1)}, bf16[512,256]{1,0:T(8,128)(2,1)S(1)}, u32[]{:S(2)}, u32[]{:S(2)}) collective-permute-start(bf16[512,256]{1,0:T(8,128)(2,1)S(1)} %collective-permute-done.3), channel_id=1, source_target_pairs={{0,448},{64,0},{128,64},{192,128},{256,192},{320,256},{384,320},{4... | collective-permute-start | bytes 786440 | tf_op jit(solution)/shard_map/ppermute | solution.py:34
  72.3 10.6 %collective-permute-start.8 = (bf16[512,256]{1,0:T(8,128)(2,1)S(1)}, bf16[512,256]{1,0:T(8,128)(2,1)S(1)}, u32[]{:S(2)}, u32[]{:S(2)}) collective-permute-start(bf16[512,256]{1,0:T(8,128)(2,1)S(1)} %collective-permute-done.7), channel_id=1, source_target_pairs={{0,64},{64,128},{128,192},{192,256},{256,320},{320,384},{384,448},... | collective-permute-start | bytes 786440 | tf_op jit(solution)/shard_map/ppermute | solution.py:34
  77.0 8.1 %collective-permute-start.5 = (bf16[256,256]{1,0:T(8,128)(2,1)S(1)}, bf16[256,256]{1,0:T(8,128)(2,1)S(1)}, u32[]{:S(2)}, u32[]{:S(2)}) collective-permute-start(bf16[256,256]{1,0:T(8,128)(2,1)S(1)} %slice.53), channel_id=1, source_target_pairs={{0,448},{64,0},{128,64},{192,128},{256,192},{320,256},{384,320},{4... | collective-permute-start | bytes 393224 | tf_op jit(solution)/shard_map/ppermute | solution.py:34
  82.8 8.1 %collective-permute-start.9 = (bf16[256,256]{1,0:T(8,128)(2,1)S(1)}, bf16[256,256]{1,0:T(8,128)(2,1)S(1)}, u32[]{:S(2)}, u32[]{:S(2)}) collective-permute-start(bf16[256,256]{1,0:T(8,128)(2,1)S(1)} %slice.54), channel_id=1, source_target_pairs={{0,64},{64,128},{128,192},{192,256},{256,320},{320,384},{384,448},... | collective-permute-start | bytes 393224 | tf_op jit(solution)/shard_map/ppermute | solution.py:34
  95.0 36.5 %copy-start.10 = (s32[256]{0:T(256)S(1)}, s32[256]{0:T(256)}, u32[]{:S(2)}) copy-start(s32[256]{0:T(256)} %param.15) | copy-start | bytes 3076
  95.8 42.0 %copy-start.4 = (f32[4096]{0:T(1024)S(1)}, f32[4096]{0:T(1024)}, u32[]{:S(2)}) copy-start(f32[4096]{0:T(1024)} %param.12) | copy-start | bytes 49156
  95.8 42.0 %copy-start.5 = (f32[4096]{0:T(1024)S(1)}, f32[4096]{0:T(1024)}, u32[]{:S(2)}) copy-start(f32[4096]{0:T(1024)} %param.13) | copy-start | bytes 49156
  129.6 6.3 %collective-permute-start.10 = (bf16[8,528,256]{2,1,0:T(8,128)(2,1)S(1)}, bf16[8,528,256]{2,1,0:T(8,128)(2,1)}, u32[]{:S(2)}, u32[]{:S(2)}) collective-permute-start(bf16[8,528,256]{2,1,0:T(8,128)(2,1)S(1)} %all_to_all.31.mine_ref), channel_id=1, source_target_pairs={{0,1},{1,0},{2,3},{3,2},{4,5},{5,4},{6,7},{7,6},{8,9},{9,8},{10,11... | collective-permute-start | bytes 6488072 | tf_op jit(solution)/shard_map/ppermute | solution.py:226
  139.4 9.4 %copy-start.8 = (s32[16384]{0:T(1024)S(1)}, s32[16384]{0:T(1024)}, u32[]{:S(2)}) copy-start(s32[16384]{0:T(1024)} %param.19) | copy-start | bytes 196612
  148.0 7.7 %copy-start.6 = (bf16[512,1024]{1,0:T(8,128)(2,1)S(1)}, bf16[512,1024]{1,0:T(8,128)(2,1)}, u32[]{:S(2)}) copy-start(bf16[512,1024]{1,0:T(8,128)(2,1)} %param.17) | copy-start | bytes 3145732
  151.6 11.6 %all-to-all-start.2 = ((bf16[16,32,256]{2,1,0:T(8,128)(2,1)}), bf16[16,32,256]{2,1,0:T(8,128)(2,1)S(1)}, u32[]{:S(2)}, u32[]{:S(2)}) async-start(bf16[16,32,256]{2,1,0:T(8,128)(2,1)} %bitcast.27), calls=%async_computation.3 | async-start | bytes 524288 | tf_op jit(solution)/shard_map/all_to_all | solution.py:273
  164.2 11.7 %all-to-all-start.3 = ((bf16[16,32,256]{2,1,0:T(8,128)(2,1)}), bf16[16,32,256]{2,1,0:T(8,128)(2,1)S(1)}, u32[]{:S(2)}, u32[]{:S(2)}) async-start(bf16[16,32,256]{2,1,0:T(8,128)(2,1)} %shard_map.131), calls=%async_computation.4 | async-start | bytes 524288 | tf_op jit(solution)/shard_map/all_to_all | solution.py:281
  206.3 42.7 %all-to-all-start.5 = ((bf16[32,64,128]{2,1,0:T(8,128)(2,1)}), bf16[32,64,128]{2,1,0:T(8,128)(2,1)S(1)}, u32[]{:S(2)}, u32[]{:S(2)}) async-start(bf16[32,64,128]{2,1,0:T(8,128)(2,1)} %broadcast_in_dim.28), calls=%async_computation.7 | async-start | bytes 1048576 | tf_op jit(solution)/shard_map/all_to_all | solution.py:29
  214.7 32.4 %reduce-scatter.5.cloned.1.call-start = ((), (), s32[]{:S(2)}) async-start(), calls=%async_computation.9 | async-start | bytes 327680 | tf_op jit(solution)/shard_map/reduce_scatter | solution.py:294
  215.6 36.3 %copy-start.9 = (f32[256]{0:T(256)}, f32[256]{0:T(256)S(1)}, u32[]{:S(2)}) copy-start(f32[256]{0:T(256)S(1)} %multiply_bitcast_fusion.2) | copy-start | bytes 3076
  (4 other events, 5.9 us)
Sparse Core Ops, SparseCore 0:
  10.2 51.0 all-gather.2
  148.1 42.6 reduce-scatter.2
  218.4 28.7 reduce-scatter.4

commit v4 on v3

--- a/solution.py
+++ b/solution.py
@@ -34,16 +34,9 @@
     return lax.ppermute(block, axis, [(i, (i + step) % count) for i in range(count)])
 
 
-def ring_gather(block, axis):
-    count = lax.axis_size(axis)
-    ahead, behind = [block], [block]
-    for _ in range(count // 2 - 1):
-        ahead.append(shift(ahead[-1], axis, -1))
-        behind.append(shift(behind[-1], axis, 1))
-    half = block.shape[0] // 2
-    far = jnp.concatenate([shift(ahead[-1][:half], axis, -1), shift(behind[-1][half:], axis, 1)])
-    blocks = ahead + [far] + behind[:0:-1]
-    return lax.dynamic_slice_in_dim(jnp.stack(blocks + blocks), count - lax.axis_index(axis), count, 0)
+def tensor_gather(block):
+    mine = broadcast_gather(block, TN[:2])
+    return mine, lax.ppermute(mine, "c", [(0, 1), (1, 0)])
 
 
 def parity_sign(value):
@@ -59,11 +52,14 @@
     return centred * lax.rsqrt(spread + 1e-06)
 
 
-def project_kernel(x_ref, w_ref, out_ref, stat_ref):
+def project_kernel(pos_ref, mine_ref, other_ref, w_ref, out_ref, stat_ref):
     own = w_ref.shape[1]
+    core = lax.rem(pos_ref[0], 2)
     total = jnp.zeros(out_ref.shape, F32)
-    for b in range(x_ref.shape[0]):
-        total += jnp.dot(x_ref[b], w_ref[b * own : (b + 1) * own, :], preferred_element_type=F32)
+    for source, side in ((mine_ref, core), (other_ref, 1 - core)):
+        for q in range(source.shape[0]):
+            start = pl.multiple_of((2 * q + side) * own, own)
+            total += jnp.dot(source[q], w_ref[pl.ds(start, own), :], preferred_element_type=F32)
     mean = jnp.sum(total, axis=1, keepdims=True) * (1.0 / own)
     centred = total - mean
     out_ref[...] = centred.astype(BF)
@@ -72,12 +68,11 @@
     stat_ref[...] = jnp.where(lane == 0, mean, spread)
 
 
-def moment_kernel(
+def feature_kernel(
     pos_ref, mine_ref, other_ref, adj_ref, rstd_ref, gain_ref, prev_ref, rot_ref, sign_ref,
-    out_ref, basis_ref, sums_ref, f_ref,
+    f_ref, basis_ref, sums_ref,
 ):
     blocks, rows, own = f_ref.shape
-    part = out_ref.shape[2]
     core = lax.rem(pos_ref[0], 2)
     rstd = rstd_ref[...]
     total = jnp.zeros((rows, own), F32)
@@ -93,6 +88,11 @@
         turn = rot_ref[pl.ds(pl.multiple_of(b * own, own), own), :]
         total += jnp.dot(shifted, turn, preferred_element_type=F32)
     basis_ref[...] = total.astype(BF) * sign_ref[...]
+
+
+def moment_kernel(pos_ref, f_ref, sums_ref, out_ref):
+    blocks, rows, own = f_ref.shape
+    part = out_ref.shape[2]
     own_t = f_ref[pos_ref[0]].astype(F32).T
     own_col = jnp.sum(own_t, axis=1, keepdims=True)
     own_t = own_t.astype(BF)
@@ -200,8 +200,9 @@
         side == 0, jnp.concatenate(got, axis=1), jnp.concatenate(got[::-1], axis=1)
     )
     near = broadcast_gather(strip, "yh")
-    proj = ring_gather(near.reshape(-1, own), "z").reshape(width, own)
-    teacher = lax.all_gather(teacher_in, TN, axis=0, tiled=False)
+    proj = lax.all_gather(near.reshape(-1, own), "z", axis=0, tiled=True)
+    teacher, _ = lax.optimization_barrier((teacher_in, near))
+    teacher = tensor_gather(teacher)
 
     normed = layer_norm(student_in.astype(F32)).astype(BF)
     predicted = jnp.dot(normed, head_weight, preferred_element_type=F32)
@@ -213,17 +214,20 @@
     )
     token_weight = 1.0 / token_counts
 
+    smem, vmem = pl.BlockSpec(memory_space=pltpu.SMEM), pl.BlockSpec(memory_space=pltpu.VMEM)
+    position = tpos.reshape(1)
     raw, stat = pl.pallas_call(
         project_kernel,
         out_shape=(jax.ShapeDtypeStruct((rows, own), BF), jax.ShapeDtypeStruct((rows, 2), F32)),
+        in_specs=[smem, vmem, vmem, vmem],
+        out_specs=(vmem, vmem),
         compiler_params=pltpu.CompilerParams(vmem_limit_bytes=40 << 20),
         cost_estimate=pl.CostEstimate(flops=2 * rows * width * own, bytes_accessed=8 << 20, transcendentals=0),
-    )(teacher, proj)
+    )(position, *teacher, proj)
     pieces = jnp.stack(split3(stat.T)).reshape(6 * rows // own, own).astype(BF)
     spare = -pieces.shape[0] % 16
     packed = jnp.concatenate([raw, pieces, jnp.zeros((spare, own), BF)])
-    mine = broadcast_gather(packed, TN[:2])
-    other = lax.ppermute(mine, "c", [(0, 1), (1, 0)])
+    mine, other = tensor_gather(packed)
     first = tpos % 2 == 0
 
     def unpack(block):
@@ -244,21 +248,19 @@
     index_col = lax.broadcasted_iota(jnp.int32, (own, own), 1)
     table = parity_sign(index_row & index_col).astype(BF)
 
-    smem, vmem = pl.BlockSpec(memory_space=pltpu.SMEM), pl.BlockSpec(memory_space=pltpu.VMEM)
-    moment, basis, sums = pl.pallas_call(
-        moment_kernel,
+    features, basis, sums = pl.pallas_call(
+        feature_kernel,
         out_shape=(
-            jax.ShapeDtypeStruct((chunks, own, part), BF),
+            jax.ShapeDtypeStruct((blocks, rows, own), BF),
             jax.ShapeDtypeStruct((rows, own), BF),
             jax.ShapeDtypeStruct((blocks, 1, own), F32),
         ),
         in_specs=[smem] + [vmem] * 8,
         out_specs=(vmem,) * 3,
-        scratch_shapes=[pltpu.VMEM((blocks, rows, own), BF)],
         compiler_params=pltpu.CompilerParams(vmem_limit_bytes=40 << 20),
-        cost_estimate=pl.CostEstimate(flops=4 * rows * width * own, bytes_accessed=12 << 20, transcendentals=0),
+        cost_estimate=pl.CostEstimate(flops=2 * rows * width * own, bytes_accessed=12 << 20, transcendentals=0),
     )(
-        tpos.reshape(1),
+        position,
         mine,
         other,
         adjust.T,
@@ -268,9 +270,17 @@
         rotation,
         (2 * signs - 1).astype(BF)[None, :],
     )
+    lines = lax.all_to_all(basis.reshape(blocks, rows // blocks, own), TN, 0, 0, tiled=True)
+    moment = pl.pallas_call(
+        moment_kernel,
+        out_shape=jax.ShapeDtypeStruct((chunks, own, part), BF),
+        in_specs=[smem, vmem, vmem],
+        out_specs=vmem,
+        compiler_params=pltpu.CompilerParams(vmem_limit_bytes=24 << 20),
+        cost_estimate=pl.CostEstimate(flops=2 * rows * width * own, bytes_accessed=6 << 20, transcendentals=0),
+    )(position, features, sums)
     within = lax.psum_scatter(moment, "z", scatter_dimension=0, tiled=True)
 
-    lines = lax.all_to_all(basis.reshape(blocks, rows // blocks, own), TN, 0, 0, tiled=True)
     lines = pl.pallas_call(
         hadamard_kernel,
         out_shape=jax.ShapeDtypeStruct(lines.shape, BF),
@@ -286,12 +296,15 @@
         in_specs=[smem] + [vmem] * 5,
         out_specs=vmem,
         compiler_params=pltpu.CompilerParams(vmem_limit_bytes=24 << 20),
-    )(tpos.reshape(1), target, predicted, token_weight, normed, sums)
+    )(position, target, predicted, token_weight, normed, sums)
     taken = lax.all_to_all(sent, DP, 0, 0, tiled=True)
 
     grad_own = jnp.sum(taken[:, : 2 * depth, :].astype(F32), axis=0).astype(BF)
     within, grad_own = lax.optimization_barrier((within, grad_own))
-    within = lax.psum_scatter(within, "yh", scatter_dimension=0, tiled=True)
+    places, here = lax.axis_size("yh"), lax.axis_index("yh")
+    within_sum = within[here].astype(F32)
+    for k in range(1, places):
+        within_sum += shift(within[(here + k) % places], "yh", k).astype(F32)
     grad_head = pl.pallas_call(
         place_kernel,
         out_shape=jax.ShapeDtypeStruct((chunks * depth, own), F32),
@@ -310,7 +323,7 @@
     between = lax.dot_general(
         off_t, off_d, (((0,), (0,)), ((), ())), precision=lax.Precision.HIGHEST, preferred_element_type=F32
     )
-    new_cov = (within.reshape(own, part).astype(F32) + between * rows) / all_tokens
+    new_cov = (within_sum + between * rows) / all_tokens
     return (new_cov, new_mean, grad_head, loss / image_count)
 
 

time: 260 us -> 254 us (0.977)
  the two profiles are of different devices: /device:TPU:16 before, /device:TPU:8 now
where the time goes in v4:
time: 254 us; the launch traced here: 253 us
  waiting for transfers between devices  87.9 us (35%)
  starting transfers between devices  69.9 us (28%)
  blocking collectives  44.9 us (18%)
  Pallas kernels  15.5 us (6%)
  between operations  15.4 us (6%)
  local copies, waits for them, and re-layouts  10.5 us (4%)
  other arithmetic  6.28 us (2%)
    all_to_all x2, blocking collectives, broadcast_gather(): lax.all_to_all(jnp.broadcast_to(block[None], (count,) + block.shape), axe...  44.9 us
    all_to_all x2, waiting for transfers between devices, broadcast_gather(): lax.all_to_all(jnp.broadcast_to(block[None], (count,) + block.shape), axe...  27.2 us
    all_to_all x2, starting transfers between devices, broadcast_gather(): lax.all_to_all(jnp.broadcast_to(block[None], (count,) + block.shape), axe...  24.2 us
    all_to_all x1, waiting for transfers between devices, body(): taken = lax.all_to_all(sent, DP, 0, 0, tiled=True)  23.4 us
    ppermute x3, starting transfers between devices, shift(): lax.ppermute(block, axis, [(i, (i + step) % count) for i in range(count)])  15.6 us
    all_gather x1, waiting for transfers between devices, body(): proj = lax.all_gather(near.reshape(-1, own), 'z', axis=0, tiled=True)  14.9 us
    all_to_all x1, starting transfers between devices, body(): taken = lax.all_to_all(sent, DP, 0, 0, tiled=True)  8.66 us
    ppermute x2, starting transfers between devices, body(): got.append(lax.ppermute(send, DP + TN, route))  7.86 us
  transfers between devices with their start and end apart: 14, of which 9 were waited for; matrix products, arithmetic and copies ran while one was open for 3% of the time, Pallas kernels for 1%

profile of v4, /device:TPU:8, one launch (start us, length us, event | category | flops | bytes accessed | tf_op | source)
XLA Modules:
  0.0 252.8 jit_solution(999927426680084365)
XLA Ops:
  8.1 4.2 %collective-permute-start = (bf16[128,128]{1,0:T(8,128)(2,1)S(1)}, bf16[128,128]{1,0:T(8,128)(2,1)S(1)}, u32[]{:S(2)}, u32[]{:S(2)}) collective-permute-start(bf16[128,128]{1,0:T(8,128)(2,1)S(1)} %get-tuple-element.36), channel_id=1, source_target_pairs={{0,0},{1,32},{2,64},{3,96},{4,128},{5,160},{6,192},{7,224},{8,256}... | collective-permute-start | bytes 98312 | tf_op jit(solution)/shard_map/ppermute | solution.py:198
  12.2 3.7 %collective-permute-start.1 = (bf16[128,128]{1,0:T(8,128)(2,1)S(1)}, bf16[128,128]{1,0:T(8,128)(2,1)S(1)}, u32[]{:S(2)}, u32[]{:S(2)}) collective-permute-start(bf16[128,128]{1,0:T(8,128)(2,1)S(1)} %get-tuple-element.37), channel_id=1, source_target_pairs={{0,16},{1,48},{2,80},{3,112},{4,144},{5,176},{6,208},{7,240},{8,27... | collective-permute-start | bytes 98312 | tf_op jit(solution)/shard_map/ppermute | solution.py:198
  15.9 3.6 %collective-permute-done.1 = bf16[128,128]{1,0:T(8,128)(2,1)S(1)} collective-permute-done((bf16[128,128]{1,0:T(8,128)(2,1)S(1)}, bf16[128,128]{1,0:T(8,128)(2,1)S(1)}, u32[]{:S(2)}, u32[]{:S(2)}) %collective-permute-start.1) | collective-permute-done | bytes 32800 | tf_op jit(solution)/shard_map/ppermute | solution.py:198
  19.6 16.9 %all_to_all.35 = bf16[4,128,256]{2,1,0:T(8,128)(2,1)} all-to-all(bf16[4,128,256]{2,1,0:T(8,128)(2,1)S(1)} %broadcast_in_dim.24), channel_id=1, replica_groups=mesh['z'=8,'yh'=4,'x'=4,'yl'=2,'c'=2] {'yh'}, dimensions={0} | all-to-all | bytes 524288 | tf_op jit(solution)/shard_map/all_to_all | solution.py:29
  36.4 2.4 broadcast_in_dim.25
  38.8 19.2 %all-to-all-start.1 = ((bf16[8,512,256]{2,1,0:T(8,128)(2,1)}), bf16[8,512,256]{2,1,0:T(8,128)(2,1)S(1)}, u32[]{:S(2)}, u32[]{:S(2)}) async-start(bf16[8,512,256]{2,1,0:T(8,128)(2,1)} %broadcast_in_dim.25), calls=%async_computation.1 | async-start | bytes 4194304 | tf_op jit(solution)/shard_map/all_to_all | solution.py:29
  58.8 26.0 %all-to-all-done.1.mine_ref = bf16[8,512,256]{2,1,0:T(8,128)(2,1)S(1)} async-done(((bf16[8,512,256]{2,1,0:T(8,128)(2,1)}), bf16[8,512,256]{2,1,0:T(8,128)(2,1)S(1)}, u32[]{:S(2)}, u32[]{:S(2)}) %all-to-all-start.1) | async-done | bytes 2097184 | tf_op jit(solution)/shard_map/all_to_all | solution.py:29
  87.1 14.9 %all-gather.2.cloned.1.call-done.w_ref = bf16[4096,256]{1,0:T(8,128)(2,1)} async-done(((bf16[512,256]{1,0:T(8,128)(2,1)}), bf16[4096,256]{1,0:T(8,128)(2,1)}) %all-gather.2.cloned.1.call-update) | async-done | bytes 2097168 | tf_op jit(solution)/shard_map/all_gather | solution.py:203
  103.6 3.0 %shard_map.129 = (bf16[512,256]{1,0:T(8,128)(2,1)S(1)}, f32[512,2]{1,0:T(8,128)S(1)}) custom-call(s32[1]{0:T(128)} %bitcast.pos_ref, bf16[8,512,256]{2,1,0:T(8,128)(2,1)S(1)} %all-to-all-done.1.mine_ref, bf16[8,512,256]{2,1,0:T(8,128)(2,1)} %collective-permute-done.2.other_ref, bf16[4096,256]{1,0:T(8,128)(2,1)S(1)} %copy-done.1), custom_call_target="tpu_custom_call" | custom-call | flops 1073741824 | bytes 8388608 | tf_op jit(solution)/shard_map/pallas_call | solution.py:219
  107.4 28.0 %all_to_all.36.mine_ref = bf16[8,528,256]{2,1,0:T(8,128)(2,1)S(1)} all-to-all(bf16[8,528,256]{2,1,0:T(8,128)(2,1)S(1)} %broadcast_in_dim.27), channel_id=1, replica_groups=mesh['z'=8,'yh'=4,'x'=4,'yl'=2,'c'=2] {'x','yl'}, dimensions={0} | all-to-all | bytes 4325376 | tf_op jit(solution)/shard_map/all_to_all | solution.py:29
  137.7 4.1 %collective-permute-done.3.other_ref = bf16[8,528,256]{2,1,0:T(8,128)(2,1)} collective-permute-done((bf16[8,528,256]{2,1,0:T(8,128)(2,1)S(1)}, bf16[8,528,256]{2,1,0:T(8,128)(2,1)}, u32[]{:S(2)}, u32[]{:S(2)}) %collective-permute-start.3) | collective-permute-done | bytes 2162720 | tf_op jit(solution)/shard_map/ppermute | solution.py:39
  145.3 5.3 %shard_map.130 = (bf16[16,512,256]{2,1,0:T(8,128)(2,1)S(1)}, bf16[512,256]{1,0:T(8,128)(2,1)}, f32[16,1,256]{2,1,0:T(1,128)S(1)}) custom-call(s32[1]{0:T(128)} %bitcast.pos_ref, bf16[8,528,256]{2,1,0:T(8,128)(2,1)S(1)} %all_to_all.36.mine_ref, bf16[8,528,256]{2,1,0:T(8,128)(2,1)} %collective-permute-done.3.other_ref, f32[512,16]{1,0:T(8,128)S(1)} %bitcast.72, ...), custom_call_target="tpu_custom_call" | custom-call | flops 1073741824 | bytes 12582912 | tf_op jit(solution)/shard_map/pallas_call | solution.py:251
  150.6 2.7 %shard_map.131 = bf16[32,256,128]{2,1,0:T(8,128)(2,1)} custom-call(s32[1]{0:T(128)} %bitcast.pos_ref, bf16[16,512,256]{2,1,0:T(8,128)(2,1)S(1)} %get-tuple-element.15.f_ref, f32[16,1,256]{2,1,0:T(1,128)S(1)} %get-tuple-element.16.sums_ref), custom_call_target="tpu_custom_call" | custom-call | flops 1073741824 | bytes 6291456 | tf_op jit(solution)/shard_map/pallas_call | solution.py:274
  155.8 4.6 %all-to-all-start.3 = ((bf16[16,32,256]{2,1,0:T(8,128)(2,1)}), bf16[16,32,256]{2,1,0:T(8,128)(2,1)S(1)}, u32[]{:S(2)}, u32[]{:S(2)}) async-start(bf16[16,32,256]{2,1,0:T(8,128)(2,1)} %bitcast.17), calls=%async_computation.4 | async-start | bytes 524288 | tf_op jit(solution)/shard_map/all_to_all | solution.py:273
  161.3 5.9 %all-to-all-done.3.basis_ref = bf16[16,32,256]{2,1,0:T(8,128)(2,1)S(1)} async-done(((bf16[16,32,256]{2,1,0:T(8,128)(2,1)}), bf16[16,32,256]{2,1,0:T(8,128)(2,1)S(1)}, u32[]{:S(2)}, u32[]{:S(2)}) %all-to-all-start.3) | async-done | bytes 262176 | tf_op jit(solution)/shard_map/all_to_all | solution.py:273
  168.2 4.7 %all-to-all-start.4 = ((bf16[16,32,256]{2,1,0:T(8,128)(2,1)}), bf16[16,32,256]{2,1,0:T(8,128)(2,1)S(1)}, u32[]{:S(2)}, u32[]{:S(2)}) async-start(bf16[16,32,256]{2,1,0:T(8,128)(2,1)} %shard_map.132), calls=%async_computation.5 | async-start | bytes 524288 | tf_op jit(solution)/shard_map/all_to_all | solution.py:291
  174.9 4.8 %all-to-all-done.4 = bf16[16,32,256]{2,1,0:T(8,128)(2,1)S(1)} async-done(((bf16[16,32,256]{2,1,0:T(8,128)(2,1)}), bf16[16,32,256]{2,1,0:T(8,128)(2,1)S(1)}, u32[]{:S(2)}, u32[]{:S(2)}) %all-to-all-start.4) | async-done | bytes 262176 | tf_op jit(solution)/shard_map/all_to_all | solution.py:291
  181.2 8.7 %all-to-all-start.5 = ((bf16[32,80,128]{2,1,0:T(8,128)(2,1)}), bf16[32,80,128]{2,1,0:T(8,128)(2,1)S(1)}, u32[]{:S(2)}, u32[]{:S(2)}) async-start(bf16[32,80,128]{2,1,0:T(8,128)(2,1)} %shard_map.133), calls=%async_computation.6 | async-start | bytes 1310720 | tf_op jit(solution)/shard_map/all_to_all | solution.py:300
  189.9 23.4 %all-to-all-done.5 = bf16[32,80,128]{2,1,0:T(8,128)(2,1)S(1)} async-done(((bf16[32,80,128]{2,1,0:T(8,128)(2,1)}), bf16[32,80,128]{2,1,0:T(8,128)(2,1)S(1)}, u32[]{:S(2)}, u32[]{:S(2)}) %all-to-all-start.5) | async-done | bytes 655392 | tf_op jit(solution)/shard_map/all_to_all | solution.py:300
  214.6 5.0 %all-to-all-start.6 = ((bf16[32,64,128]{2,1,0:T(8,128)(2,1)}), bf16[32,64,128]{2,1,0:T(8,128)(2,1)S(1)}, u32[]{:S(2)}, u32[]{:S(2)}) async-start(bf16[32,64,128]{2,1,0:T(8,128)(2,1)} %broadcast_in_dim.31), calls=%async_computation.7 | async-start | bytes 1048576 | tf_op jit(solution)/shard_map/all_to_all | solution.py:29
  221.1 4.6 %collective-permute-start.4 = (bf16[256,128]{1,0:T(8,128)(2,1)S(1)}, bf16[256,128]{1,0:T(8,128)(2,1)S(1)}, u32[]{:S(2)}, u32[]{:S(2)}) collective-permute-start(bf16[256,128]{1,0:T(8,128)(2,1)S(1)} %get-tuple-element.27), channel_id=1, source_target_pairs={{0,16},{16,32},{32,48},{48,0},{1,17},{17,33},{33,49},{49,1},{2,18}... | collective-permute-start | bytes 196616 | tf_op jit(solution)/shard_map/ppermute | solution.py:34
  225.7 5.5 %collective-permute-start.5 = (bf16[256,128]{1,0:T(8,128)(2,1)S(1)}, bf16[256,128]{1,0:T(8,128)(2,1)S(1)}, u32[]{:S(2)}, u32[]{:S(2)}) collective-permute-start(bf16[256,128]{1,0:T(8,128)(2,1)S(1)} %get-tuple-element.29), channel_id=1, source_target_pairs={{0,32},{16,48},{32,0},{48,16},{1,33},{17,49},{33,1},{49,17},{2,34}... | collective-permute-start | bytes 196616 | tf_op jit(solution)/shard_map/ppermute | solution.py:34
  231.2 5.5 %collective-permute-start.6 = (bf16[256,128]{1,0:T(8,128)(2,1)S(1)}, bf16[256,128]{1,0:T(8,128)(2,1)S(1)}, u32[]{:S(2)}, u32[]{:S(2)}) collective-permute-start(bf16[256,128]{1,0:T(8,128)(2,1)S(1)} %get-tuple-element.28), channel_id=1, source_target_pairs={{0,48},{16,0},{32,16},{48,32},{1,49},{17,1},{33,17},{49,33},{2,50}... | collective-permute-start | bytes 196616 | tf_op jit(solution)/shard_map/ppermute | solution.py:34
  236.7 3.2 %collective-permute-done.4 = bf16[256,128]{1,0:T(8,128)(2,1)S(1)} collective-permute-done((bf16[256,128]{1,0:T(8,128)(2,1)S(1)}, bf16[256,128]{1,0:T(8,128)(2,1)S(1)}, u32[]{:S(2)}, u32[]{:S(2)}) %collective-permute-start.4) | collective-permute-done | bytes 65568 | tf_op jit(solution)/shard_map/ppermute | solution.py:34
  (98 shorter events, 27.6 us)
Async XLA Ops:
  7.2 167.3 %copy-start = (bf16[1024,256]{1,0:T(8,128)(2,1)S(1)}, bf16[1024,256]{1,0:T(8,128)(2,1)}, u32[]{:S(2)}) copy-start(bf16[1024,256]{1,0:T(8,128)(2,1)} %param.18) | copy-start | bytes 1572868
  8.1 7.9 %collective-permute-start = (bf16[128,128]{1,0:T(8,128)(2,1)S(1)}, bf16[128,128]{1,0:T(8,128)(2,1)S(1)}, u32[]{:S(2)}, u32[]{:S(2)}) collective-permute-start(bf16[128,128]{1,0:T(8,128)(2,1)S(1)} %get-tuple-element.36), channel_id=1, source_target_pairs={{0,0},{1,32},{2,64},{3,96},{4,128},{5,160},{6,192},{7,224},{8,256}... | collective-permute-start | bytes 98312 | tf_op jit(solution)/shard_map/ppermute | solution.py:198
  12.2 7.3 %collective-permute-start.1 = (bf16[128,128]{1,0:T(8,128)(2,1)S(1)}, bf16[128,128]{1,0:T(8,128)(2,1)S(1)}, u32[]{:S(2)}, u32[]{:S(2)}) collective-permute-start(bf16[128,128]{1,0:T(8,128)(2,1)S(1)} %get-tuple-element.37), channel_id=1, source_target_pairs={{0,16},{1,48},{2,80},{3,112},{4,144},{5,176},{6,208},{7,240},{8,27... | collective-permute-start | bytes 98312 | tf_op jit(solution)/shard_map/ppermute | solution.py:198
  38.8 45.9 %all-to-all-start.1 = ((bf16[8,512,256]{2,1,0:T(8,128)(2,1)}), bf16[8,512,256]{2,1,0:T(8,128)(2,1)S(1)}, u32[]{:S(2)}, u32[]{:S(2)}) async-start(bf16[8,512,256]{2,1,0:T(8,128)(2,1)} %broadcast_in_dim.25), calls=%async_computation.1 | async-start | bytes 4194304 | tf_op jit(solution)/shard_map/all_to_all | solution.py:29
  58.0 44.0 %all-gather.2.cloned.1.call-start = ((), (), s32[]{:S(2)}) async-start(), calls=%async_computation.8 | async-start | bytes 2359296 | tf_op jit(solution)/shard_map/all_gather | solution.py:203
  58.7 154.9 %reduce-scatter.2.cloned.1.call-start = ((), (), s32[]{:S(2)}) async-start(), calls=%async_computation.9 | async-start | bytes 2359296 | tf_op jit(solution)/shard_map/reduce_scatter | solution.py:282
  84.8 17.2 %collective-permute-start.2 = (bf16[8,512,256]{2,1,0:T(8,128)(2,1)S(1)}, bf16[8,512,256]{2,1,0:T(8,128)(2,1)}, u32[]{:S(2)}, u32[]{:S(2)}) collective-permute-start(bf16[8,512,256]{2,1,0:T(8,128)(2,1)S(1)} %all-to-all-done.1.mine_ref), channel_id=1, source_target_pairs={{0,1},{1,0},{2,3},{3,2},{4,5},{5,4},{6,7},{7,6},{8,9},{9,8},{10,11... | collective-permute-start | bytes 6291464 | tf_op jit(solution)/shard_map/ppermute | solution.py:39
  102.0 1.6 copy-start.1
  107.4 30.1 %copy-start.9 = (s32[256]{0:T(256)S(1)}, s32[256]{0:T(256)}, u32[]{:S(2)}) copy-start(s32[256]{0:T(256)} %param.15) | copy-start | bytes 3076
  135.4 8.3 %copy-start.3 = (f32[4096]{0:T(1024)S(1)}, f32[4096]{0:T(1024)}, u32[]{:S(2)}) copy-start(f32[4096]{0:T(1024)} %param.12) | copy-start | bytes 49156
  135.4 8.3 %copy-start.4 = (f32[4096]{0:T(1024)S(1)}, f32[4096]{0:T(1024)}, u32[]{:S(2)}) copy-start(f32[4096]{0:T(1024)} %param.13) | copy-start | bytes 49156
  135.4 6.4 %collective-permute-start.3 = (bf16[8,528,256]{2,1,0:T(8,128)(2,1)S(1)}, bf16[8,528,256]{2,1,0:T(8,128)(2,1)}, u32[]{:S(2)}, u32[]{:S(2)}) collective-permute-start(bf16[8,528,256]{2,1,0:T(8,128)(2,1)S(1)} %all_to_all.36.mine_ref), channel_id=1, source_target_pairs={{0,1},{1,0},{2,3},{3,2},{4,5},{5,4},{6,7},{7,6},{8,9},{9,8},{10,11... | collective-permute-start | bytes 6488072 | tf_op jit(solution)/shard_map/ppermute | solution.py:39
  143.7 1.6 copy-start.2
  153.3 0.8 copy-start.7
  153.3 2.3 copy-start.5
  155.8 11.4 %all-to-all-start.3 = ((bf16[16,32,256]{2,1,0:T(8,128)(2,1)}), bf16[16,32,256]{2,1,0:T(8,128)(2,1)S(1)}, u32[]{:S(2)}, u32[]{:S(2)}) async-start(bf16[16,32,256]{2,1,0:T(8,128)(2,1)} %bitcast.17), calls=%async_computation.4 | async-start | bytes 524288 | tf_op jit(solution)/shard_map/all_to_all | solution.py:273
  168.2 11.6 %all-to-all-start.4 = ((bf16[16,32,256]{2,1,0:T(8,128)(2,1)}), bf16[16,32,256]{2,1,0:T(8,128)(2,1)S(1)}, u32[]{:S(2)}, u32[]{:S(2)}) async-start(bf16[16,32,256]{2,1,0:T(8,128)(2,1)} %shard_map.132), calls=%async_computation.5 | async-start | bytes 524288 | tf_op jit(solution)/shard_map/all_to_all | solution.py:291
  181.2 32.1 %all-to-all-start.5 = ((bf16[32,80,128]{2,1,0:T(8,128)(2,1)}), bf16[32,80,128]{2,1,0:T(8,128)(2,1)S(1)}, u32[]{:S(2)}, u32[]{:S(2)}) async-start(bf16[32,80,128]{2,1,0:T(8,128)(2,1)} %shard_map.133), calls=%async_computation.6 | async-start | bytes 1310720 | tf_op jit(solution)/shard_map/all_to_all | solution.py:300
  214.6 28.5 %all-to-all-start.6 = ((bf16[32,64,128]{2,1,0:T(8,128)(2,1)}), bf16[32,64,128]{2,1,0:T(8,128)(2,1)S(1)}, u32[]{:S(2)}, u32[]{:S(2)}) async-start(bf16[32,64,128]{2,1,0:T(8,128)(2,1)} %broadcast_in_dim.31), calls=%async_computation.7 | async-start | bytes 1048576 | tf_op jit(solution)/shard_map/all_to_all | solution.py:29
  219.6 26.3 %copy-start.8 = (f32[256]{0:T(256)}, f32[256]{0:T(256)S(1)}, u32[]{:S(2)}) copy-start(f32[256]{0:T(256)S(1)} %multiply_bitcast_fusion.2) | copy-start | bytes 3076
  221.1 18.8 %collective-permute-start.4 = (bf16[256,128]{1,0:T(8,128)(2,1)S(1)}, bf16[256,128]{1,0:T(8,128)(2,1)S(1)}, u32[]{:S(2)}, u32[]{:S(2)}) collective-permute-start(bf16[256,128]{1,0:T(8,128)(2,1)S(1)} %get-tuple-element.27), channel_id=1, source_target_pairs={{0,16},{16,32},{32,48},{48,0},{1,17},{17,33},{33,49},{49,1},{2,18}... | collective-permute-start | bytes 196616 | tf_op jit(solution)/shard_map/ppermute | solution.py:34
  225.7 14.2 %collective-permute-start.5 = (bf16[256,128]{1,0:T(8,128)(2,1)S(1)}, bf16[256,128]{1,0:T(8,128)(2,1)S(1)}, u32[]{:S(2)}, u32[]{:S(2)}) collective-permute-start(bf16[256,128]{1,0:T(8,128)(2,1)S(1)} %get-tuple-element.29), channel_id=1, source_target_pairs={{0,32},{16,48},{32,0},{48,16},{1,33},{17,49},{33,1},{49,17},{2,34}... | collective-permute-start | bytes 196616 | tf_op jit(solution)/shard_map/ppermute | solution.py:34
  231.2 8.7 %collective-permute-start.6 = (bf16[256,128]{1,0:T(8,128)(2,1)S(1)}, bf16[256,128]{1,0:T(8,128)(2,1)S(1)}, u32[]{:S(2)}, u32[]{:S(2)}) collective-permute-start(bf16[256,128]{1,0:T(8,128)(2,1)S(1)} %get-tuple-element.28), channel_id=1, source_target_pairs={{0,48},{16,0},{32,16},{48,32},{1,49},{17,1},{33,17},{49,33},{2,50}... | collective-permute-start | bytes 196616 | tf_op jit(solution)/shard_map/ppermute | solution.py:34
  243.1 0.8 copy-start.6
Sparse Core Ops, SparseCore 0:
  60.9 41.0 all-gather.1
  153.4 44.4 reduce-scatter.1

commit v5 on v4

--- a/solution.py
+++ b/solution.py
@@ -36,7 +36,8 @@
 
 def tensor_gather(block):
     mine = broadcast_gather(block, TN[:2])
-    return mine, lax.ppermute(mine, "c", [(0, 1), (1, 0)])
+    half = mine.shape[0] // 2
+    return mine, [lax.ppermute(part, "c", [(0, 1), (1, 0)]) for part in (mine[:half], mine[half:])]
 
 
 def parity_sign(value):
@@ -52,14 +53,11 @@
     return centred * lax.rsqrt(spread + 1e-06)
 
 
-def project_kernel(pos_ref, mine_ref, other_ref, w_ref, out_ref, stat_ref):
+def project_kernel(x_ref, w_ref, out_ref, stat_ref):
     own = w_ref.shape[1]
-    core = lax.rem(pos_ref[0], 2)
     total = jnp.zeros(out_ref.shape, F32)
-    for source, side in ((mine_ref, core), (other_ref, 1 - core)):
-        for q in range(source.shape[0]):
-            start = pl.multiple_of((2 * q + side) * own, own)
-            total += jnp.dot(source[q], w_ref[pl.ds(start, own), :], preferred_element_type=F32)
+    for b in range(x_ref.shape[0]):
+        total += jnp.dot(x_ref[b], w_ref[b * own : (b + 1) * own, :], preferred_element_type=F32)
     mean = jnp.sum(total, axis=1, keepdims=True) * (1.0 / own)
     centred = total - mean
     out_ref[...] = centred.astype(BF)
@@ -68,26 +66,20 @@
     stat_ref[...] = jnp.where(lane == 0, mean, spread)
 
 
-def feature_kernel(
-    pos_ref, mine_ref, other_ref, adj_ref, rstd_ref, gain_ref, prev_ref, rot_ref, sign_ref,
-    f_ref, basis_ref, sums_ref,
-):
-    blocks, rows, own = f_ref.shape
+def feature_kernel(pos_ref, mine_ref, low_ref, high_ref, adj_ref, rstd_ref, gain_ref, f_ref, sums_ref):
+    blocks, rows, _ = f_ref.shape
     core = lax.rem(pos_ref[0], 2)
     rstd = rstd_ref[...]
-    total = jnp.zeros((rows, own), F32)
+    half = blocks // 4
     for j in range(blocks):
-        source, q, side = (mine_ref, j, core) if j < blocks // 2 else (other_ref, j - blocks // 2, 1 - core)
-        b = 2 * q + side
-        value = (source[q, :rows, :].astype(F32) + adj_ref[:, j : j + 1]) * rstd * gain_ref[b]
+        q = j % (2 * half)
+        b = 2 * q + (core if j < 2 * half else 1 - core)
+        source = mine_ref if j < 2 * half else low_ref if q < half else high_ref
+        place = q if j < 2 * half else q % half
+        value = (source[place, :rows, :].astype(F32) + adj_ref[:, j : j + 1]) * rstd * gain_ref[b]
         feature = value.astype(BF)
         f_ref[b] = feature
-        feature = feature.astype(F32)
-        sums_ref[b] = jnp.sum(feature, axis=0, keepdims=True)
-        shifted = (feature - prev_ref[b]).astype(BF)
-        turn = rot_ref[pl.ds(pl.multiple_of(b * own, own), own), :]
-        total += jnp.dot(shifted, turn, preferred_element_type=F32)
-    basis_ref[...] = total.astype(BF) * sign_ref[...]
+        sums_ref[b] = jnp.sum(feature.astype(F32), axis=0, keepdims=True)
 
 
 def moment_kernel(pos_ref, f_ref, sums_ref, out_ref):
@@ -118,10 +110,15 @@
         out_ref[b] = parts[b].astype(BF)
 
 
-def grad_kernel(pos_ref, target_ref, pred_ref, w_ref, normed_ref, sums_ref, out_ref):
+def grad_kernel(pos_ref, f_ref, prev_ref, turn_ref, pred_ref, w_ref, normed_ref, sums_ref, out_ref):
     chunks, _, part = out_ref.shape
+    blocks, _, own = f_ref.shape
     depth = normed_ref.shape[1] // chunks
-    residual = pred_ref[...] - target_ref[...].astype(F32)
+    target = jnp.zeros(pred_ref.shape, F32)
+    for b in range(blocks):
+        shifted = (f_ref[b].astype(F32) - prev_ref[b]).astype(BF)
+        target += jnp.dot(shifted, turn_ref[b * own : (b + 1) * own, :], preferred_element_type=F32)
+    residual = pred_ref[...] - target
     weighted = residual * w_ref[...]
     loss = jnp.sum(weighted * residual, axis=0, keepdims=True)
     grad = lax.dot_general(
@@ -183,8 +180,10 @@
     depth = student_in.shape[1] // chunks
     all_tokens = image_ids.shape[0]
     image_count = all_tokens // IMAGE_SHARE
+    smem, vmem = pl.BlockSpec(memory_space=pltpu.SMEM), pl.BlockSpec(memory_space=pltpu.VMEM)
     dpos = lax.axis_index(DP)
     tpos = lax.axis_index(TN)
+    position = tpos.reshape(1)
 
     side = dpos % 2
     halves = out_proj.reshape(2, part, part)
@@ -200,9 +199,27 @@
         side == 0, jnp.concatenate(got, axis=1), jnp.concatenate(got[::-1], axis=1)
     )
     near = broadcast_gather(strip, "yh")
+    teacher = lax.all_gather(teacher_in, TN, axis=0, tiled=False)
+    near, teacher = lax.optimization_barrier((near, teacher))
     proj = lax.all_gather(near.reshape(-1, own), "z", axis=0, tiled=True)
-    teacher, _ = lax.optimization_barrier((teacher_in, near))
-    teacher = tensor_gather(teacher)
+
+    slab = width // lax.axis_size("z")
+    few = slab // blocks
+    scale = 1.0 / (jnp.sqrt(F32(width)) * prev_scale)
+    index_row = lax.broadcasted_iota(jnp.int32, (own, own), 0)
+    index_col = lax.broadcasted_iota(jnp.int32, (own, own), 1)
+    table = parity_sign(index_row & index_col).astype(BF)
+    lines = lax.dynamic_slice_in_dim(rotation, lax.axis_index("z") * slab, slab, 0)
+    lines = (lines * (2 * signs - 1).astype(BF)).reshape(blocks, few, own)
+    lines = lax.all_to_all(lines, TN, 0, 0, tiled=True)
+    lines = pl.pallas_call(
+        hadamard_kernel,
+        out_shape=jax.ShapeDtypeStruct(lines.shape, BF),
+        in_specs=[smem, vmem, vmem],
+        out_specs=vmem,
+        compiler_params=pltpu.CompilerParams(vmem_limit_bytes=24 << 20),
+    )(scale, lines, table)
+    lines = lax.all_to_all(lines, TN, 0, 0, tiled=True).reshape(slab, own)
 
     normed = layer_norm(student_in.astype(F32)).astype(BF)
     predicted = jnp.dot(normed, head_weight, preferred_element_type=F32)
@@ -214,16 +231,18 @@
     )
     token_weight = 1.0 / token_counts
 
-    smem, vmem = pl.BlockSpec(memory_space=pltpu.SMEM), pl.BlockSpec(memory_space=pltpu.VMEM)
-    position = tpos.reshape(1)
+    proj, lines, normed, predicted, token_weight = lax.optimization_barrier(
+        (proj, lines, normed, predicted, token_weight)
+    )
+    turned = lax.all_gather(lines, "z", axis=0, tiled=True)
     raw, stat = pl.pallas_call(
         project_kernel,
         out_shape=(jax.ShapeDtypeStruct((rows, own), BF), jax.ShapeDtypeStruct((rows, 2), F32)),
-        in_specs=[smem, vmem, vmem, vmem],
+        in_specs=[vmem, vmem],
         out_specs=(vmem, vmem),
         compiler_params=pltpu.CompilerParams(vmem_limit_bytes=40 << 20),
         cost_estimate=pl.CostEstimate(flops=2 * rows * width * own, bytes_accessed=8 << 20, transcendentals=0),
-    )(position, *teacher, proj)
+    )(teacher, proj)
     pieces = jnp.stack(split3(stat.T)).reshape(6 * rows // own, own).astype(BF)
     spare = -pieces.shape[0] % 16
     packed = jnp.concatenate([raw, pieces, jnp.zeros((spare, own), BF)])
@@ -232,9 +251,9 @@
 
     def unpack(block):
         tail = block[:, rows : rows + pieces.shape[0], :].astype(F32)
-        return tail.reshape(blocks // 2, 3, 2, rows).sum(1)
-
-    stat_mine, stat_other = unpack(mine), unpack(other)
+        return tail.reshape(-1, 3, 2, rows).sum(1)
+
+    stat_mine, stat_other = unpack(mine), jnp.concatenate([unpack(part) for part in other])
     stats = jnp.stack(
         [jnp.where(first, stat_mine, stat_other), jnp.where(first, stat_other, stat_mine)], axis=1
     ).reshape(blocks, 2, rows)
@@ -243,34 +262,18 @@
     variance = (jnp.sum(stats[:, 1], axis=0) + own * jnp.sum(adjust * adjust, axis=0)) / width
     rstd = lax.rsqrt(variance + 1e-06)
     adjust = jnp.concatenate([stat_mine[:, 0], stat_other[:, 0]]) - mean
-    scale = 1.0 / (jnp.sqrt(F32(width)) * prev_scale)
-    index_row = lax.broadcasted_iota(jnp.int32, (own, own), 0)
-    index_col = lax.broadcasted_iota(jnp.int32, (own, own), 1)
-    table = parity_sign(index_row & index_col).astype(BF)
-
-    features, basis, sums = pl.pallas_call(
+
+    features, sums = pl.pallas_call(
         feature_kernel,
         out_shape=(
             jax.ShapeDtypeStruct((blocks, rows, own), BF),
-            jax.ShapeDtypeStruct((rows, own), BF),
             jax.ShapeDtypeStruct((blocks, 1, own), F32),
         ),
-        in_specs=[smem] + [vmem] * 8,
-        out_specs=(vmem,) * 3,
+        in_specs=[smem] + [vmem] * 6,
+        out_specs=(vmem,) * 2,
         compiler_params=pltpu.CompilerParams(vmem_limit_bytes=40 << 20),
-        cost_estimate=pl.CostEstimate(flops=2 * rows * width * own, bytes_accessed=12 << 20, transcendentals=0),
-    )(
-        position,
-        mine,
-        other,
-        adjust.T,
-        rstd[:, None],
-        final_gain.reshape(blocks, 1, own),
-        mean_prev.reshape(blocks, 1, own),
-        rotation,
-        (2 * signs - 1).astype(BF)[None, :],
-    )
-    lines = lax.all_to_all(basis.reshape(blocks, rows // blocks, own), TN, 0, 0, tiled=True)
+        cost_estimate=pl.CostEstimate(flops=rows * width * 8, bytes_accessed=8 << 20, transcendentals=0),
+    )(position, mine, *other, adjust.T, rstd[:, None], final_gain.reshape(blocks, 1, own))
     moment = pl.pallas_call(
         moment_kernel,
         out_shape=jax.ShapeDtypeStruct((chunks, own, part), BF),
@@ -281,26 +284,17 @@
     )(position, features, sums)
     within = lax.psum_scatter(moment, "z", scatter_dimension=0, tiled=True)
 
-    lines = pl.pallas_call(
-        hadamard_kernel,
-        out_shape=jax.ShapeDtypeStruct(lines.shape, BF),
-        in_specs=[smem, vmem, vmem],
-        out_specs=vmem,
-        compiler_params=pltpu.CompilerParams(vmem_limit_bytes=24 << 20),
-    )(scale, lines, table)
-    target = lax.all_to_all(lines, TN, 0, 0, tiled=True).reshape(rows, own)
-
     sent = pl.pallas_call(
         grad_kernel,
         out_shape=jax.ShapeDtypeStruct((chunks, 2 * depth + 16, part), BF),
-        in_specs=[smem] + [vmem] * 5,
+        in_specs=[smem] + [vmem] * 7,
         out_specs=vmem,
-        compiler_params=pltpu.CompilerParams(vmem_limit_bytes=24 << 20),
-    )(position, target, predicted, token_weight, normed, sums)
+        compiler_params=pltpu.CompilerParams(vmem_limit_bytes=32 << 20),
+        cost_estimate=pl.CostEstimate(flops=3 * rows * width * own, bytes_accessed=9 << 20, transcendentals=0),
+    )(position, features, mean_prev.reshape(blocks, 1, own), turned, predicted, token_weight, normed, sums)
     taken = lax.all_to_all(sent, DP, 0, 0, tiled=True)
 
     grad_own = jnp.sum(taken[:, : 2 * depth, :].astype(F32), axis=0).astype(BF)
-    within, grad_own = lax.optimization_barrier((within, grad_own))
     places, here = lax.axis_size("yh"), lax.axis_index("yh")
     within_sum = within[here].astype(F32)
     for k in range(1, places):

time: 254 us -> 266 us (1.047)
  the two profiles are of different devices: /device:TPU:8 before, /device:TPU:4 now
where the time goes in v5:
time: 266 us; the launch traced here: 264 us
  waiting for transfers between devices  113 us (42%)
  starting transfers between devices  70.1 us (26%)
  local copies, waits for them, and re-layouts  21.8 us (8%)
  blocking collectives  17.6 us (7%)
  between operations  15 us (6%)
  Pallas kernels  12.4 us (5%)
  other arithmetic  11.3 us (4%)
    all_to_all x1, waiting for transfers between devices, body(): taken = lax.all_to_all(sent, DP, 0, 0, tiled=True)  23.6 us
    all_gather x1, waiting for transfers between devices, body(): proj = lax.all_gather(near.reshape(-1, own), 'z', axis=0, tiled=True)  22.6 us
    all_to_all x2, waiting for transfers between devices, broadcast_gather(): lax.all_to_all(jnp.broadcast_to(block[None], (count,) + block.shape), axe...  20.2 us
    reduce_scatter x1, waiting for transfers between devices, body(): within = lax.psum_scatter(moment, 'z', scatter_dimension=0, tiled=True)  18.5 us
    ppermute x3, starting transfers between devices, shift(): lax.ppermute(block, axis, [(i, (i + step) % count) for i in range(count)])  18.1 us
    all_to_all x1, blocking collectives, broadcast_gather(): lax.all_to_all(jnp.broadcast_to(block[None], (count,) + block.shape), axe...  17.6 us
    ppermute x2, starting transfers between devices, body(): got.append(lax.ppermute(send, DP + TN, route))  14.8 us
    unnamed x37, local copies, waits for them, and re-layouts  13.7 us
  transfers between devices with their start and end apart: 16, of which 10 were waited for; matrix products, arithmetic and copies ran while one was open for 7% of the time, Pallas kernels for 4%

profile of v5, /device:TPU:4, one launch (start us, length us, event | category | flops | bytes accessed | tf_op | source)
XLA Modules:
  0.0 264.0 jit_solution(1740592039374938834)
XLA Ops:
  8.8 10.8 %collective-permute-start = (bf16[128,128]{1,0:T(8,128)(2,1)S(1)}, bf16[128,128]{1,0:T(8,128)(2,1)S(1)}, u32[]{:S(2)}, u32[]{:S(2)}) collective-permute-start(bf16[128,128]{1,0:T(8,128)(2,1)S(1)} %get-tuple-element.44), channel_id=1, source_target_pairs={{0,0},{1,32},{2,64},{3,96},{4,128},{5,160},{6,192},{7,224},{8,256}... | collective-permute-start | bytes 98312 | tf_op jit(solution)/shard_map/ppermute | solution.py:197
  19.7 3.9 %collective-permute-start.1 = (bf16[128,128]{1,0:T(8,128)(2,1)S(1)}, bf16[128,128]{1,0:T(8,128)(2,1)S(1)}, u32[]{:S(2)}, u32[]{:S(2)}) collective-permute-start(bf16[128,128]{1,0:T(8,128)(2,1)S(1)} %get-tuple-element.45), channel_id=1, source_target_pairs={{0,16},{1,48},{2,80},{3,112},{4,144},{5,176},{6,208},{7,240},{8,27... | collective-permute-start | bytes 98312 | tf_op jit(solution)/shard_map/ppermute | solution.py:197
  23.6 10.1 %collective-permute-done.1 = bf16[128,128]{1,0:T(8,128)(2,1)S(1)} collective-permute-done((bf16[128,128]{1,0:T(8,128)(2,1)S(1)}, bf16[128,128]{1,0:T(8,128)(2,1)S(1)}, u32[]{:S(2)}, u32[]{:S(2)}) %collective-permute-start.1) | collective-permute-done | bytes 32800 | tf_op jit(solution)/shard_map/ppermute | solution.py:197
  33.7 17.6 %all_to_all.30 = bf16[4,128,256]{2,1,0:T(8,128)(2,1)} all-to-all(bf16[4,128,256]{2,1,0:T(8,128)(2,1)S(1)} %broadcast_in_dim.16), channel_id=1, replica_groups=mesh['z'=8,'yh'=4,'x'=4,'yl'=2,'c'=2] {'yh'}, dimensions={0} | all-to-all | bytes 524288 | tf_op jit(solution)/shard_map/all_to_all | solution.py:29
  51.4 9.3 %all-gather.9.cloned.1.call-done = bf16[8192,256]{1,0:T(8,128)(2,1)} async-done(((bf16[512,256]{1,0:T(8,128)(2,1)}), bf16[8192,256]{1,0:T(8,128)(2,1)}) %all-gather.9.cloned.1.call-update) | async-done | bytes 4194320 | tf_op jit(solution)/shard_map/all_gather | solution.py:202
  63.0 5.7 %all-to-all-start.1 = ((bf16[16,32,256]{2,1,0:T(8,128)(2,1)}), bf16[16,32,256]{2,1,0:T(8,128)(2,1)S(1)}, u32[]{:S(2)}, u32[]{:S(2)}) async-start(bf16[16,32,256]{2,1,0:T(8,128)(2,1)} %bitcast.6), calls=%async_computation.1 | async-start | bytes 524288 | tf_op jit(solution)/shard_map/all_to_all | solution.py:214
  75.2 6.1 %all-to-all-start.2 = ((bf16[16,32,256]{2,1,0:T(8,128)(2,1)}), bf16[16,32,256]{2,1,0:T(8,128)(2,1)S(1)}, u32[]{:S(2)}, u32[]{:S(2)}) async-start(bf16[16,32,256]{2,1,0:T(8,128)(2,1)} %shard_map.129), calls=%async_computation.2 | async-start | bytes 524288 | tf_op jit(solution)/shard_map/all_to_all | solution.py:222
  82.3 4.5 %all-to-all-done.2 = bf16[16,32,256]{2,1,0:T(8,128)(2,1)S(1)} async-done(((bf16[16,32,256]{2,1,0:T(8,128)(2,1)}), bf16[16,32,256]{2,1,0:T(8,128)(2,1)S(1)}, u32[]{:S(2)}, u32[]{:S(2)}) %all-to-all-start.2) | async-done | bytes 262176 | tf_op jit(solution)/shard_map/all_to_all | solution.py:222
  86.8 22.6 %all-gather.5.cloned.1.call-done.w_ref = bf16[4096,256]{1,0:T(8,128)(2,1)} async-done(((bf16[512,256]{1,0:T(8,128)(2,1)}), bf16[4096,256]{1,0:T(8,128)(2,1)}) %all-gather.5.cloned.1.call-update) | async-done | bytes 2097168 | tf_op jit(solution)/shard_map/all_gather | solution.py:204
  109.3 2.2 copy-done.6
  116.7 5.7 %all-to-all-start.3 = ((bf16[8,528,256]{2,1,0:T(8,128)(2,1)}), bf16[8,528,256]{2,1,0:T(8,128)(2,1)S(1)}, u32[]{:S(2)}, u32[]{:S(2)}) async-start(bf16[8,528,256]{2,1,0:T(8,128)(2,1)} %broadcast_in_dim.24), calls=%async_computation.3 | async-start | bytes 4325376 | tf_op jit(solution)/shard_map/all_to_all | solution.py:29
  123.2 20.2 %all-to-all-done.3.mine_ref = bf16[8,528,256]{2,1,0:T(8,128)(2,1)S(1)} async-done(((bf16[8,528,256]{2,1,0:T(8,128)(2,1)}), bf16[8,528,256]{2,1,0:T(8,128)(2,1)S(1)}, u32[]{:S(2)}, u32[]{:S(2)}) %all-to-all-start.3) | async-done | bytes 2162720 | tf_op jit(solution)/shard_map/all_to_all | solution.py:29
  146.9 2.6 collective-permute-start.3
  158.6 3.6 %shard_map.131 = (bf16[16,512,256]{2,1,0:T(8,128)(2,1)S(1)}, f32[16,1,256]{2,1,0:T(1,128)S(1)}) custom-call(s32[1]{0:T(128)} %bitcast.pos_ref, bf16[8,528,256]{2,1,0:T(8,128)(2,1)S(1)} %all-to-all-done.3.mine_ref, bf16[4,528,256]{2,1,0:T(8,128)(2,1)} %collective-permute-done.2.low_ref, bf16[4,528,256]{2,1,0:T(8,128)(2,1)} %collective-permute-done.3.high_ref, ...), custom_call_target="tpu_custom_call" | custom-call | flops 16777216 | bytes 8388608 | tf_op jit(solution)/shard_map/pallas_call | solution.py:266
  168.0 2.2 copy-done.2
  171.8 3.0 %shard_map.133 = bf16[32,80,128]{2,1,0:T(8,128)(2,1)} custom-call(s32[1]{0:T(128)} %bitcast.pos_ref, bf16[16,512,256]{2,1,0:T(8,128)(2,1)S(1)} %copy-done.2, f32[16,1,256]{2,1,0:T(1,128)S(1)} %bitcast.78, bf16[4096,256]{1,0:T(8,128)(2,1)S(1)} %copy-done.7, f32[512,256]{1,0:T(8,128)S(1)} %fusion.27.pred_ref, f32[512,1]{1,0:T(8,128)S(1)} %copy.68.w_ref, ...), custom_call_target="tpu_custom_call" | custom-call | flops 1610612736 | bytes 9437184 | tf_op jit(solution)/shard_map/pallas_call | solution.py:287
  174.8 8.7 %all-to-all-start.4 = ((bf16[32,80,128]{2,1,0:T(8,128)(2,1)}), bf16[32,80,128]{2,1,0:T(8,128)(2,1)S(1)}, u32[]{:S(2)}, u32[]{:S(2)}) async-start(bf16[32,80,128]{2,1,0:T(8,128)(2,1)} %shard_map.133), calls=%async_computation.5 | async-start | bytes 1310720 | tf_op jit(solution)/shard_map/all_to_all | solution.py:295
  183.5 23.6 %all-to-all-done.4 = bf16[32,80,128]{2,1,0:T(8,128)(2,1)S(1)} async-done(((bf16[32,80,128]{2,1,0:T(8,128)(2,1)}), bf16[32,80,128]{2,1,0:T(8,128)(2,1)S(1)}, u32[]{:S(2)}, u32[]{:S(2)}) %all-to-all-start.4) | async-done | bytes 655392 | tf_op jit(solution)/shard_map/all_to_all | solution.py:295
  208.1 6.3 %all-to-all-start.5 = ((bf16[32,64,128]{2,1,0:T(8,128)(2,1)}), bf16[32,64,128]{2,1,0:T(8,128)(2,1)S(1)}, u32[]{:S(2)}, u32[]{:S(2)}) async-start(bf16[32,64,128]{2,1,0:T(8,128)(2,1)} %broadcast_in_dim.25), calls=%async_computation.6 | async-start | bytes 1048576 | tf_op jit(solution)/shard_map/all_to_all | solution.py:29
  215.2 18.5 %reduce-scatter.2.cloned.1.call-done = bf16[4,256,128]{2,1,0:T(8,128)(2,1)} async-done(((bf16[32,256,128]{2,1,0:T(8,128)(2,1)}), bf16[4,256,128]{2,1,0:T(8,128)(2,1)}) %reduce-scatter.2.cloned.1.call-update) | async-done | bytes 262160 | tf_op jit(solution)/shard_map/reduce_scatter | solution.py:285
  234.6 4.6 %collective-permute-start.4 = (bf16[256,128]{1,0:T(8,128)(2,1)S(1)}, bf16[256,128]{1,0:T(8,128)(2,1)S(1)}, u32[]{:S(2)}, u32[]{:S(2)}) collective-permute-start(bf16[256,128]{1,0:T(8,128)(2,1)S(1)} %get-tuple-element.35), channel_id=1, source_target_pairs={{0,16},{16,32},{32,48},{48,0},{1,17},{17,33},{33,49},{49,1},{2,18}... | collective-permute-start | bytes 196616 | tf_op jit(solution)/shard_map/ppermute | solution.py:34
  239.2 7.5 %collective-permute-start.5 = (bf16[256,128]{1,0:T(8,128)(2,1)S(1)}, bf16[256,128]{1,0:T(8,128)(2,1)S(1)}, u32[]{:S(2)}, u32[]{:S(2)}) collective-permute-start(bf16[256,128]{1,0:T(8,128)(2,1)S(1)} %get-tuple-element.37), channel_id=1, source_target_pairs={{0,32},{16,48},{32,0},{48,16},{1,33},{17,49},{33,1},{49,17},{2,34}... | collective-permute-start | bytes 196616 | tf_op jit(solution)/shard_map/ppermute | solution.py:34
  246.7 5.9 %collective-permute-start.6 = (bf16[256,128]{1,0:T(8,128)(2,1)S(1)}, bf16[256,128]{1,0:T(8,128)(2,1)S(1)}, u32[]{:S(2)}, u32[]{:S(2)}) collective-permute-start(bf16[256,128]{1,0:T(8,128)(2,1)S(1)} %get-tuple-element.36), channel_id=1, source_target_pairs={{0,48},{16,0},{32,16},{48,32},{1,49},{17,1},{33,17},{49,33},{2,50}... | collective-permute-start | bytes 196616 | tf_op jit(solution)/shard_map/ppermute | solution.py:34
  253.5 2.1 shard_map.134
  (123 shorter events, 41.8 us)
Async XLA Ops:
  7.2 74.7 %copy-start = (bf16[1024,256]{1,0:T(8,128)(2,1)S(1)}, bf16[1024,256]{1,0:T(8,128)(2,1)}, u32[]{:S(2)}) copy-start(bf16[1024,256]{1,0:T(8,128)(2,1)} %param.18) | copy-start | bytes 1572868
  7.2 62.2 %copy-start.15 = (s32[16384]{0:T(1024)S(1)}, s32[16384]{0:T(1024)}, u32[]{:S(2)}) copy-start(s32[16384]{0:T(1024)} %param.19) | copy-start | bytes 196612
  7.2 64.1 %copy-start.12 = (bf16[512,1024]{1,0:T(8,128)(2,1)S(1)}, bf16[512,1024]{1,0:T(8,128)(2,1)}, u32[]{:S(2)}) copy-start(bf16[512,1024]{1,0:T(8,128)(2,1)} %param.17) | copy-start | bytes 3145732
  7.2 53.4 %all-gather.9.cloned.1.call-start = ((), (), s32[]{:S(2)}) async-start(), calls=%async_computation.10 | async-start | bytes 4456448 | tf_op jit(solution)/shard_map/all_gather | solution.py:202
  7.9 101.4 %all-gather.5.cloned.1.call-start = ((), (), s32[]{:S(2)}) async-start(), calls=%async_computation.7 | async-start | bytes 2359296 | tf_op jit(solution)/shard_map/all_gather | solution.py:204
  8.8 14.8 %collective-permute-start = (bf16[128,128]{1,0:T(8,128)(2,1)S(1)}, bf16[128,128]{1,0:T(8,128)(2,1)S(1)}, u32[]{:S(2)}, u32[]{:S(2)}) collective-permute-start(bf16[128,128]{1,0:T(8,128)(2,1)S(1)} %get-tuple-element.44), channel_id=1, source_target_pairs={{0,0},{1,32},{2,64},{3,96},{4,128},{5,160},{6,192},{7,224},{8,256}... | collective-permute-start | bytes 98312 | tf_op jit(solution)/shard_map/ppermute | solution.py:197
  19.7 14.0 %collective-permute-start.1 = (bf16[128,128]{1,0:T(8,128)(2,1)S(1)}, bf16[128,128]{1,0:T(8,128)(2,1)S(1)}, u32[]{:S(2)}, u32[]{:S(2)}) collective-permute-start(bf16[128,128]{1,0:T(8,128)(2,1)S(1)} %get-tuple-element.45), channel_id=1, source_target_pairs={{0,16},{1,48},{2,80},{3,112},{4,144},{5,176},{6,208},{7,240},{8,27... | collective-permute-start | bytes 98312 | tf_op jit(solution)/shard_map/ppermute | solution.py:197
  63.0 11.2 %all-to-all-start.1 = ((bf16[16,32,256]{2,1,0:T(8,128)(2,1)}), bf16[16,32,256]{2,1,0:T(8,128)(2,1)S(1)}, u32[]{:S(2)}, u32[]{:S(2)}) async-start(bf16[16,32,256]{2,1,0:T(8,128)(2,1)} %bitcast.6), calls=%async_computation.1 | async-start | bytes 524288 | tf_op jit(solution)/shard_map/all_to_all | solution.py:214
  72.3 42.3 %copy-start.3 = (bf16[512,1024]{1,0:T(8,128)(2,1)}, bf16[512,1024]{1,0:T(8,128)(2,1)S(1)}, u32[]{:S(2)}) copy-start(bf16[512,1024]{1,0:T(8,128)(2,1)S(1)} %fusion.3.normed_ref) | copy-start | bytes 3145732
  75.2 11.6 %all-to-all-start.2 = ((bf16[16,32,256]{2,1,0:T(8,128)(2,1)}), bf16[16,32,256]{2,1,0:T(8,128)(2,1)S(1)}, u32[]{:S(2)}, u32[]{:S(2)}) async-start(bf16[16,32,256]{2,1,0:T(8,128)(2,1)} %shard_map.129), calls=%async_computation.2 | async-start | bytes 524288 | tf_op jit(solution)/shard_map/all_to_all | solution.py:222
  86.8 27.8 %copy-start.14 = (bf16[16,32,256]{2,1,0:T(8,128)(2,1)}, bf16[16,32,256]{2,1,0:T(8,128)(2,1)S(1)}, u32[]{:S(2)}) copy-start(bf16[16,32,256]{2,1,0:T(8,128)(2,1)S(1)} %all-to-all-done.2) | copy-start | bytes 786436
  116.7 26.7 %all-to-all-start.3 = ((bf16[8,528,256]{2,1,0:T(8,128)(2,1)}), bf16[8,528,256]{2,1,0:T(8,128)(2,1)S(1)}, u32[]{:S(2)}, u32[]{:S(2)}) async-start(bf16[8,528,256]{2,1,0:T(8,128)(2,1)} %broadcast_in_dim.24), calls=%async_computation.3 | async-start | bytes 4325376 | tf_op jit(solution)/shard_map/all_to_all | solution.py:29
  122.4 45.2 %all-gather.7.cloned.1.call-start = ((), (), s32[]{:S(2)}) async-start(), calls=%async_computation.9 | async-start | bytes 2359296 | tf_op jit(solution)/shard_map/all_gather | solution.py:237
  123.1 110.5 %reduce-scatter.2.cloned.1.call-start = ((), (), s32[]{:S(2)}) async-start(), calls=%async_computation.8 | async-start | bytes 2359296 | tf_op jit(solution)/shard_map/reduce_scatter | solution.py:285
  144.8 12.8 %copy-start.10 = (f32[4096]{0:T(1024)S(1)}, f32[4096]{0:T(1024)}, u32[]{:S(2)}) copy-start(f32[4096]{0:T(1024)} %param.12) | copy-start | bytes 49156
  144.8 5.1 %collective-permute-start.2 = (bf16[4,528,256]{2,1,0:T(8,128)(2,1)}, bf16[4,528,256]{2,1,0:T(8,128)(2,1)}, u32[]{:S(2)}, u32[]{:S(2)}) collective-permute-start(bf16[4,528,256]{2,1,0:T(8,128)(2,1)} %get-tuple-element.33), channel_id=1, source_target_pairs={{0,1},{1,0},{2,3},{3,2},{4,5},{5,4},{6,7},{7,6},{8,9},{9,8},{10,11... | collective-permute-start | bytes 3244040 | tf_op jit(solution)/shard_map/ppermute | solution.py:40
  146.9 5.1 %collective-permute-start.3 = (bf16[4,528,256]{2,1,0:T(8,128)(2,1)}, bf16[4,528,256]{2,1,0:T(8,128)(2,1)}, u32[]{:S(2)}, u32[]{:S(2)}) collective-permute-start(bf16[4,528,256]{2,1,0:T(8,128)(2,1)} %get-tuple-element.32), channel_id=1, source_target_pairs={{0,1},{1,0},{2,3},{3,2},{4,5},{5,4},{6,7},{7,6},{8,9},{9,8},{10,11... | collective-permute-start | bytes 3244040 | tf_op jit(solution)/shard_map/ppermute | solution.py:40
  168.0 2.2 copy-start.2
  174.8 32.3 %all-to-all-start.4 = ((bf16[32,80,128]{2,1,0:T(8,128)(2,1)}), bf16[32,80,128]{2,1,0:T(8,128)(2,1)S(1)}, u32[]{:S(2)}, u32[]{:S(2)}) async-start(bf16[32,80,128]{2,1,0:T(8,128)(2,1)} %shard_map.133), calls=%async_computation.5 | async-start | bytes 1310720 | tf_op jit(solution)/shard_map/all_to_all | solution.py:295
  208.1 44.6 %all-to-all-start.5 = ((bf16[32,64,128]{2,1,0:T(8,128)(2,1)}), bf16[32,64,128]{2,1,0:T(8,128)(2,1)S(1)}, u32[]{:S(2)}, u32[]{:S(2)}) async-start(bf16[32,64,128]{2,1,0:T(8,128)(2,1)} %broadcast_in_dim.25), calls=%async_computation.6 | async-start | bytes 1048576 | tf_op jit(solution)/shard_map/all_to_all | solution.py:29
  214.6 42.9 %copy-start.17 = (f32[256]{0:T(256)}, f32[256]{0:T(256)S(1)}, u32[]{:S(2)}) copy-start(f32[256]{0:T(256)S(1)} %multiply_bitcast_fusion.2) | copy-start | bytes 3076
  234.6 21.0 %collective-permute-start.4 = (bf16[256,128]{1,0:T(8,128)(2,1)S(1)}, bf16[256,128]{1,0:T(8,128)(2,1)S(1)}, u32[]{:S(2)}, u32[]{:S(2)}) collective-permute-start(bf16[256,128]{1,0:T(8,128)(2,1)S(1)} %get-tuple-element.35), channel_id=1, source_target_pairs={{0,16},{16,32},{32,48},{48,0},{1,17},{17,33},{33,49},{49,1},{2,18}... | collective-permute-start | bytes 196616 | tf_op jit(solution)/shard_map/ppermute | solution.py:34
  239.2 16.4 %collective-permute-start.5 = (bf16[256,128]{1,0:T(8,128)(2,1)S(1)}, bf16[256,128]{1,0:T(8,128)(2,1)S(1)}, u32[]{:S(2)}, u32[]{:S(2)}) collective-permute-start(bf16[256,128]{1,0:T(8,128)(2,1)S(1)} %get-tuple-element.37), channel_id=1, source_target_pairs={{0,32},{16,48},{32,0},{48,16},{1,33},{17,49},{33,1},{49,17},{2,34}... | collective-permute-start | bytes 196616 | tf_op jit(solution)/shard_map/ppermute | solution.py:34
  246.7 8.9 %collective-permute-start.6 = (bf16[256,128]{1,0:T(8,128)(2,1)S(1)}, bf16[256,128]{1,0:T(8,128)(2,1)S(1)}, u32[]{:S(2)}, u32[]{:S(2)}) collective-permute-start(bf16[256,128]{1,0:T(8,128)(2,1)S(1)} %get-tuple-element.36), channel_id=1, source_target_pairs={{0,48},{16,0},{32,16},{48,32},{1,49},{17,1},{33,17},{49,33},{2,50}... | collective-permute-start | bytes 196616 | tf_op jit(solution)/shard_map/ppermute | solution.py:34
  (10 other events, 13.5 us)
Sparse Core Ops, SparseCore 0:
  10.2 50.3 all-gather.8
  62.7 46.5 all-gather.4
  125.3 41.8 all-gather.6
  169.8 63.7 reduce-scatter.1

commit v6 on v4

--- a/solution.py
+++ b/solution.py
@@ -52,14 +52,11 @@
     return centred * lax.rsqrt(spread + 1e-06)
 
 
-def project_kernel(pos_ref, mine_ref, other_ref, w_ref, out_ref, stat_ref):
+def project_kernel(x_ref, w_ref, out_ref, stat_ref):
     own = w_ref.shape[1]
-    core = lax.rem(pos_ref[0], 2)
     total = jnp.zeros(out_ref.shape, F32)
-    for source, side in ((mine_ref, core), (other_ref, 1 - core)):
-        for q in range(source.shape[0]):
-            start = pl.multiple_of((2 * q + side) * own, own)
-            total += jnp.dot(source[q], w_ref[pl.ds(start, own), :], preferred_element_type=F32)
+    for b in range(x_ref.shape[0]):
+        total += jnp.dot(x_ref[b], w_ref[b * own : (b + 1) * own, :], preferred_element_type=F32)
     mean = jnp.sum(total, axis=1, keepdims=True) * (1.0 / own)
     centred = total - mean
     out_ref[...] = centred.astype(BF)
@@ -69,8 +66,8 @@
 
 
 def feature_kernel(
-    pos_ref, mine_ref, other_ref, adj_ref, rstd_ref, gain_ref, prev_ref, rot_ref, sign_ref,
-    f_ref, basis_ref, sums_ref,
+    pos_ref, mine_ref, other_ref, adj_ref, rstd_ref, gain_ref, prev_ref, turn_ref,
+    f_ref, target_ref, sums_ref,
 ):
     blocks, rows, own = f_ref.shape
     core = lax.rem(pos_ref[0], 2)
@@ -85,9 +82,9 @@
         feature = feature.astype(F32)
         sums_ref[b] = jnp.sum(feature, axis=0, keepdims=True)
         shifted = (feature - prev_ref[b]).astype(BF)
-        turn = rot_ref[pl.ds(pl.multiple_of(b * own, own), own), :]
+        turn = turn_ref[pl.ds(pl.multiple_of(b * own, own), own), :]
         total += jnp.dot(shifted, turn, preferred_element_type=F32)
-    basis_ref[...] = total.astype(BF) * sign_ref[...]
+    target_ref[...] = total
 
 
 def moment_kernel(pos_ref, f_ref, sums_ref, out_ref):
@@ -103,25 +100,33 @@
             out_ref[2 * b + h] = block[:, h * part : (h + 1) * part]
 
 
-def hadamard_kernel(scale_ref, basis_ref, table_ref, out_ref):
-    blocks, few, own = basis_ref.shape
-    flat = basis_ref[...].reshape(blocks * few, own)
-    mixed = jnp.dot(flat, table_ref[...], preferred_element_type=F32) * scale_ref[0]
-    parts = [mixed[b * few : (b + 1) * few] for b in range(blocks)]
-    step = 1
-    while step < blocks:
+def hadamard_kernel(scale_ref, lines_ref, table_ref, out_ref):
+    blocks, tall, _ = lines_ref.shape
+    few = min(tall, 32)
+
+    def piece(i, _):
+        rows = pl.ds(pl.multiple_of(i * few, few), few)
         parts = [
-            parts[b - step] - parts[b] if b & step else parts[b] + parts[b + step] for b in range(blocks)
+            jnp.dot(lines_ref[b, rows, :], table_ref[...], preferred_element_type=F32) * scale_ref[0]
+            for b in range(blocks)
         ]
-        step *= 2
-    for b in range(blocks):
-        out_ref[b] = parts[b].astype(BF)
+        step = 1
+        while step < blocks:
+            parts = [
+                parts[b - step] - parts[b] if b & step else parts[b] + parts[b + step] for b in range(blocks)
+            ]
+            step *= 2
+        for b in range(blocks):
+            out_ref[b, rows, :] = parts[b].astype(BF)
+        return 0
+
+    lax.fori_loop(0, tall // few, piece, 0)
 
 
 def grad_kernel(pos_ref, target_ref, pred_ref, w_ref, normed_ref, sums_ref, out_ref):
     chunks, _, part = out_ref.shape
     depth = normed_ref.shape[1] // chunks
-    residual = pred_ref[...] - target_ref[...].astype(F32)
+    residual = pred_ref[...] - target_ref[...]
     weighted = residual * w_ref[...]
     loss = jnp.sum(weighted * residual, axis=0, keepdims=True)
     grad = lax.dot_general(
@@ -183,8 +188,10 @@
     depth = student_in.shape[1] // chunks
     all_tokens = image_ids.shape[0]
     image_count = all_tokens // IMAGE_SHARE
+    smem, vmem = pl.BlockSpec(memory_space=pltpu.SMEM), pl.BlockSpec(memory_space=pltpu.VMEM)
     dpos = lax.axis_index(DP)
     tpos = lax.axis_index(TN)
+    position = tpos.reshape(1)
 
     side = dpos % 2
     halves = out_proj.reshape(2, part, part)
@@ -199,10 +206,27 @@
     strip = jnp.where(
         side == 0, jnp.concatenate(got, axis=1), jnp.concatenate(got[::-1], axis=1)
     )
+    teacher = lax.all_gather(teacher_in, TN, axis=0, tiled=False)
+
+    scale = 1.0 / (jnp.sqrt(F32(width)) * prev_scale)
+    index_row = lax.broadcasted_iota(jnp.int32, (own, own), 0)
+    index_col = lax.broadcasted_iota(jnp.int32, (own, own), 1)
+    table = parity_sign(index_row & index_col).astype(BF)
+    lines = (rotation * (2 * signs - 1).astype(BF)).reshape(blocks, own, own)
+    lines = lax.all_to_all(lines, TN, 0, 0, tiled=True)
+    strip, lines = lax.optimization_barrier((strip, lines))
     near = broadcast_gather(strip, "yh")
+    near, teacher = lax.optimization_barrier((near, teacher))
     proj = lax.all_gather(near.reshape(-1, own), "z", axis=0, tiled=True)
-    teacher, _ = lax.optimization_barrier((teacher_in, near))
-    teacher = tensor_gather(teacher)
+    lines = pl.pallas_call(
+        hadamard_kernel,
+        out_shape=jax.ShapeDtypeStruct(lines.shape, BF),
+        in_specs=[smem, vmem, vmem],
+        out_specs=vmem,
+        compiler_params=pltpu.CompilerParams(vmem_limit_bytes=16 << 20),
+        cost_estimate=pl.CostEstimate(flops=2 * width * own * own, bytes_accessed=4 << 20, transcendentals=0),
+    )(scale, lines, table)
+    turned = lax.all_to_all(lines, TN, 0, 0, tiled=True).reshape(width, own)
 
     normed = layer_norm(student_in.astype(F32)).astype(BF)
     predicted = jnp.dot(normed, head_weight, preferred_element_type=F32)
@@ -214,16 +238,17 @@
     )
     token_weight = 1.0 / token_counts
 
-    smem, vmem = pl.BlockSpec(memory_space=pltpu.SMEM), pl.BlockSpec(memory_space=pltpu.VMEM)
-    position = tpos.reshape(1)
+    proj, turned, normed, predicted, token_weight = lax.optimization_barrier(
+        (proj, turned, normed, predicted, token_weight)
+    )
     raw, stat = pl.pallas_call(
         project_kernel,
         out_shape=(jax.ShapeDtypeStruct((rows, own), BF), jax.ShapeDtypeStruct((rows, 2), F32)),
-        in_specs=[smem, vmem, vmem, vmem],
+        in_specs=[vmem, vmem],
         out_specs=(vmem, vmem),
-        compiler_params=pltpu.CompilerParams(vmem_limit_bytes=40 << 20),
+        compiler_params=pltpu.CompilerParams(vmem_limit_bytes=16 << 20),
         cost_estimate=pl.CostEstimate(flops=2 * rows * width * own, bytes_accessed=8 << 20, transcendentals=0),
-    )(position, *teacher, proj)
+    )(teacher, proj)
     pieces = jnp.stack(split3(stat.T)).reshape(6 * rows // own, own).astype(BF)
     spare = -pieces.shape[0] % 16
     packed = jnp.concatenate([raw, pieces, jnp.zeros((spare, own), BF)])
@@ -243,21 +268,17 @@
     variance = (jnp.sum(stats[:, 1], axis=0) + own * jnp.sum(adjust * adjust, axis=0)) / width
     rstd = lax.rsqrt(variance + 1e-06)
     adjust = jnp.concatenate([stat_mine[:, 0], stat_other[:, 0]]) - mean
-    scale = 1.0 / (jnp.sqrt(F32(width)) * prev_scale)
-    index_row = lax.broadcasted_iota(jnp.int32, (own, own), 0)
-    index_col = lax.broadcasted_iota(jnp.int32, (own, own), 1)
-    table = parity_sign(index_row & index_col).astype(BF)
-
-    features, basis, sums = pl.pallas_call(
+
+    features, target, sums = pl.pallas_call(
         feature_kernel,
         out_shape=(
             jax.ShapeDtypeStruct((blocks, rows, own), BF),
-            jax.ShapeDtypeStruct((rows, own), BF),
+            jax.ShapeDtypeStruct((rows, own), F32),
             jax.ShapeDtypeStruct((blocks, 1, own), F32),
         ),
-        in_specs=[smem] + [vmem] * 8,
+        in_specs=[smem] + [vmem] * 7,
         out_specs=(vmem,) * 3,
-        compiler_params=pltpu.CompilerParams(vmem_limit_bytes=40 << 20),
+        compiler_params=pltpu.CompilerParams(vmem_limit_bytes=16 << 20),
         cost_estimate=pl.CostEstimate(flops=2 * rows * width * own, bytes_accessed=12 << 20, transcendentals=0),
     )(
         position,
@@ -267,40 +288,28 @@
         rstd[:, None],
         final_gain.reshape(blocks, 1, own),
         mean_prev.reshape(blocks, 1, own),
-        rotation,
-        (2 * signs - 1).astype(BF)[None, :],
-    )
-    lines = lax.all_to_all(basis.reshape(blocks, rows // blocks, own), TN, 0, 0, tiled=True)
+        turned,
+    )
     moment = pl.pallas_call(
         moment_kernel,
         out_shape=jax.ShapeDtypeStruct((chunks, own, part), BF),
         in_specs=[smem, vmem, vmem],
         out_specs=vmem,
-        compiler_params=pltpu.CompilerParams(vmem_limit_bytes=24 << 20),
+        compiler_params=pltpu.CompilerParams(vmem_limit_bytes=16 << 20),
         cost_estimate=pl.CostEstimate(flops=2 * rows * width * own, bytes_accessed=6 << 20, transcendentals=0),
     )(position, features, sums)
     within = lax.psum_scatter(moment, "z", scatter_dimension=0, tiled=True)
-
-    lines = pl.pallas_call(
-        hadamard_kernel,
-        out_shape=jax.ShapeDtypeStruct(lines.shape, BF),
-        in_specs=[smem, vmem, vmem],
-        out_specs=vmem,
-        compiler_params=pltpu.CompilerParams(vmem_limit_bytes=24 << 20),
-    )(scale, lines, table)
-    target = lax.all_to_all(lines, TN, 0, 0, tiled=True).reshape(rows, own)
 
     sent = pl.pallas_call(
         grad_kernel,
         out_shape=jax.ShapeDtypeStruct((chunks, 2 * depth + 16, part), BF),
         in_specs=[smem] + [vmem] * 5,
         out_specs=vmem,
-        compiler_params=pltpu.CompilerParams(vmem_limit_bytes=24 << 20),
+        compiler_params=pltpu.CompilerParams(vmem_limit_bytes=16 << 20),
     )(position, target, predicted, token_weight, normed, sums)
     taken = lax.all_to_all(sent, DP, 0, 0, tiled=True)
 
     grad_own = jnp.sum(taken[:, : 2 * depth, :].astype(F32), axis=0).astype(BF)
-    within, grad_own = lax.optimization_barrier((within, grad_own))
     places, here = lax.axis_size("yh"), lax.axis_index("yh")
     within_sum = within[here].astype(F32)
     for k in range(1, places):

time: 254 us -> 275 us (1.083)
  the two profiles are of different devices: /device:TPU:8 before, /device:TPU:48 now
where the time goes in v6:
time: 275 us; the launch traced here: 274 us
  waiting for transfers between devices  123 us (45%)
  starting transfers between devices  68.1 us (25%)
  blocking collectives  28.4 us (10%)
  Pallas kernels  16.3 us (6%)
  between operations  15.1 us (5%)
  local copies, waits for them, and re-layouts  11.3 us (4%)
  other arithmetic  9.63 us (4%)
    all_to_all x1, blocking collectives, broadcast_gather(): lax.all_to_all(jnp.broadcast_to(block[None], (count,) + block.shape), axe...  28.4 us
    ppermute x2, waiting for transfers between devices, body(): got.append(lax.ppermute(send, DP + TN, route))  27.1 us
    all_to_all x1, waiting for transfers between devices, body(): turned = lax.all_to_all(lines, TN, 0, 0, tiled=True).reshape(width, own)  24.4 us
    reduce_scatter x1, waiting for transfers between devices, body(): within = lax.psum_scatter(moment, 'z', scatter_dimension=0, tiled=True)  22.3 us
    all_to_all x1, waiting for transfers between devices, body(): taken = lax.all_to_all(sent, DP, 0, 0, tiled=True)  21.2 us
    all_to_all x2, starting transfers between devices, broadcast_gather(): lax.all_to_all(jnp.broadcast_to(block[None], (count,) + block.shape), axe...  20 us
    all_gather x1, waiting for transfers between devices, body(): proj = lax.all_gather(near.reshape(-1, own), 'z', axis=0, tiled=True)  18.5 us
    ppermute x3, starting transfers between devices, shift(): lax.ppermute(block, axis, [(i, (i + step) % count) for i in range(count)])  13.1 us
  transfers between devices with their start and end apart: 14, of which 8 were waited for; matrix products, arithmetic and copies ran while one was open for 4% of the time, Pallas kernels for 3%

profile of v6, /device:TPU:48, one launch (start us, length us, event | category | flops | bytes accessed | tf_op | source)
XLA Modules:
  0.0 274.3 jit_solution(11059924959649345620)
XLA Ops:
  8.6 3.1 %broadcast_multiply_fusion = bf16[4096,256]{1,0:T(8,128)(2,1)} fusion(bf16[4096,256]{1,0:T(8,128)(2,1)} %param.14, bf16[256]{0:T(256)(128)(2,1)S(1)} %add_convert_fusion), kind=kLoop, calls=%fused_computation.9 | loop fusion | flops 1048576 | bytes 4194816 | tf_op jit(solution)/shard_map/mul | solution.py:215
  11.7 4.6 %all-to-all-start = ((bf16[16,256,256]{2,1,0:T(8,128)(2,1)}), bf16[16,256,256]{2,1,0:T(8,128)(2,1)S(1)}, u32[]{:S(2)}, u32[]{:S(2)}) async-start(bf16[16,256,256]{2,1,0:T(8,128)(2,1)} %bitcast.78), calls=%async_computation | async-start | bytes 4194304 | tf_op jit(solution)/shard_map/all_to_all | solution.py:216
  16.4 4.7 %collective-permute-start = (bf16[128,128]{1,0:T(8,128)(2,1)S(1)}, bf16[128,128]{1,0:T(8,128)(2,1)S(1)}, u32[]{:S(2)}, u32[]{:S(2)}) collective-permute-start(bf16[128,128]{1,0:T(8,128)(2,1)S(1)} %get-tuple-element.48), channel_id=1, source_target_pairs={{0,0},{1,32},{2,64},{3,96},{4,128},{5,160},{6,192},{7,224},{8,256}... | collective-permute-start | bytes 98312 | tf_op jit(solution)/shard_map/ppermute | solution.py:205
  21.1 4.6 %collective-permute-start.1 = (bf16[128,128]{1,0:T(8,128)(2,1)S(1)}, bf16[128,128]{1,0:T(8,128)(2,1)S(1)}, u32[]{:S(2)}, u32[]{:S(2)}) collective-permute-start(bf16[128,128]{1,0:T(8,128)(2,1)S(1)} %get-tuple-element.49), channel_id=1, source_target_pairs={{0,16},{1,48},{2,80},{3,112},{4,144},{5,176},{6,208},{7,240},{8,27... | collective-permute-start | bytes 98312 | tf_op jit(solution)/shard_map/ppermute | solution.py:205
  25.7 27.1 %collective-permute-done = bf16[128,128]{1,0:T(8,128)(2,1)S(1)} collective-permute-done((bf16[128,128]{1,0:T(8,128)(2,1)S(1)}, bf16[128,128]{1,0:T(8,128)(2,1)S(1)}, u32[]{:S(2)}, u32[]{:S(2)}) %collective-permute-start) | collective-permute-done | bytes 32800 | tf_op jit(solution)/shard_map/ppermute | solution.py:205
  54.8 12.2 %all-to-all-start.1 = ((bf16[4,128,256]{2,1,0:T(8,128)(2,1)}), bf16[4,128,256]{2,1,0:T(8,128)(2,1)S(1)}, u32[]{:S(2)}, u32[]{:S(2)}) async-start(bf16[4,128,256]{2,1,0:T(8,128)(2,1)} %broadcast_in_dim.16), calls=%async_computation.1 | async-start | bytes 524288 | tf_op jit(solution)/shard_map/all_to_all | solution.py:29
  68.2 4.2 %shard_map.129 = bf16[16,256,256]{2,1,0:T(8,128)(2,1)S(1)} custom-call(f32[1]{0:T(128)S(6)} %div.80.scale_ref, bf16[16,256,256]{2,1,0:T(8,128)(2,1)S(1)} %all-to-all-done.lines_ref, bf16[256,256]{1,0:T(8,128)(2,1)S(1)} %fusion.8.table_ref), custom_call_target="tpu_custom_call" | custom-call | flops 536870912 | bytes 4194304 | tf_op jit(solution)/shard_map/pallas_call | solution.py:221
  73.8 9.0 %all-to-all-start.2 = ((bf16[16,256,256]{2,1,0:T(8,128)(2,1)}), bf16[16,256,256]{2,1,0:T(8,128)(2,1)}, u32[]{:S(2)}, u32[]{:S(2)}) async-start(bf16[16,256,256]{2,1,0:T(8,128)(2,1)} %copy-done.2), calls=%async_computation.2 | async-start | bytes 4194304 | tf_op jit(solution)/shard_map/all_to_all | solution.py:229
  86.4 24.4 %all-to-all-done.2 = bf16[16,256,256]{2,1,0:T(8,128)(2,1)} async-done(((bf16[16,256,256]{2,1,0:T(8,128)(2,1)}), bf16[16,256,256]{2,1,0:T(8,128)(2,1)}, u32[]{:S(2)}, u32[]{:S(2)}) %all-to-all-start.2) | async-done | bytes 2097184 | tf_op jit(solution)/shard_map/all_to_all | solution.py:229
  110.8 18.5 %all-gather.4.cloned.1.call-done.w_ref = bf16[4096,256]{1,0:T(8,128)(2,1)} async-done(((bf16[512,256]{1,0:T(8,128)(2,1)}), bf16[4096,256]{1,0:T(8,128)(2,1)}) %all-gather.4.cloned.1.call-update) | async-done | bytes 2097168 | tf_op jit(solution)/shard_map/all_gather | solution.py:220
  129.3 2.2 copy-done.3
  135.2 28.4 %all_to_all.30.mine_ref = bf16[8,528,256]{2,1,0:T(8,128)(2,1)} all-to-all(bf16[8,528,256]{2,1,0:T(8,128)(2,1)S(1)} %broadcast_in_dim.24), channel_id=1, replica_groups=mesh['z'=8,'yh'=4,'x'=4,'yl'=2,'c'=2] {'x','yl'}, dimensions={0} | all-to-all | bytes 4325376 | tf_op jit(solution)/shard_map/all_to_all | solution.py:29
  163.6 2.0 collective-permute-start.2
  166.7 3.5 %collective-permute-done.2.other_ref = bf16[8,528,256]{2,1,0:T(8,128)(2,1)} collective-permute-done((bf16[8,528,256]{2,1,0:T(8,128)(2,1)}, bf16[8,528,256]{2,1,0:T(8,128)(2,1)}, u32[]{:S(2)}, u32[]{:S(2)}) %collective-permute-start.2) | collective-permute-done | bytes 2162720 | tf_op jit(solution)/shard_map/ppermute | solution.py:39
  172.1 5.8 %shard_map.131 = (bf16[16,512,256]{2,1,0:T(8,128)(2,1)S(1)}, f32[512,256]{1,0:T(8,128)S(1)}, f32[16,1,256]{2,1,0:T(1,128)S(1)}) custom-call(s32[1]{0:T(128)} %bitcast.pos_ref, bf16[8,528,256]{2,1,0:T(8,128)(2,1)} %all_to_all.30.mine_ref, bf16[8,528,256]{2,1,0:T(8,128)(2,1)} %collective-permute-done.2.other_ref, f32[512,16]{1,0:T(8,128)S(1)} %bitcast.75, ...), custom_call_target="tpu_custom_call" | custom-call | flops 1073741824 | bytes 12582912 | tf_op jit(solution)/shard_map/pallas_call | solution.py:272
  182.2 9.8 %all-to-all-start.4 = ((bf16[32,80,128]{2,1,0:T(8,128)(2,1)}), bf16[32,80,128]{2,1,0:T(8,128)(2,1)S(1)}, u32[]{:S(2)}, u32[]{:S(2)}) async-start(bf16[32,80,128]{2,1,0:T(8,128)(2,1)} %shard_map.133), calls=%async_computation.5 | async-start | bytes 1310720 | tf_op jit(solution)/shard_map/all_to_all | solution.py:310
  192.1 21.2 %all-to-all-done.4 = bf16[32,80,128]{2,1,0:T(8,128)(2,1)S(1)} async-done(((bf16[32,80,128]{2,1,0:T(8,128)(2,1)}), bf16[32,80,128]{2,1,0:T(8,128)(2,1)S(1)}, u32[]{:S(2)}, u32[]{:S(2)}) %all-to-all-start.4) | async-done | bytes 655392 | tf_op jit(solution)/shard_map/all_to_all | solution.py:310
  214.3 7.9 %all-to-all-start.5 = ((bf16[32,64,128]{2,1,0:T(8,128)(2,1)}), bf16[32,64,128]{2,1,0:T(8,128)(2,1)S(1)}, u32[]{:S(2)}, u32[]{:S(2)}) async-start(bf16[32,64,128]{2,1,0:T(8,128)(2,1)} %broadcast_in_dim.25), calls=%async_computation.6 | async-start | bytes 1048576 | tf_op jit(solution)/shard_map/all_to_all | solution.py:29
  223.0 22.3 %reduce-scatter.2.cloned.1.call-done = bf16[4,256,128]{2,1,0:T(8,128)(2,1)} async-done(((bf16[32,256,128]{2,1,0:T(8,128)(2,1)}), bf16[4,256,128]{2,1,0:T(8,128)(2,1)}) %reduce-scatter.2.cloned.1.call-update) | async-done | bytes 262160 | tf_op jit(solution)/shard_map/reduce_scatter | solution.py:301
  246.2 1.9 collective-permute-start.3
  248.1 9.3 %collective-permute-start.4 = (bf16[256,128]{1,0:T(8,128)(2,1)S(1)}, bf16[256,128]{1,0:T(8,128)(2,1)S(1)}, u32[]{:S(2)}, u32[]{:S(2)}) collective-permute-start(bf16[256,128]{1,0:T(8,128)(2,1)S(1)} %get-tuple-element.41), channel_id=1, source_target_pairs={{0,32},{16,48},{32,0},{48,16},{1,33},{17,49},{33,1},{49,17},{2,34}... | collective-permute-start | bytes 196616 | tf_op jit(solution)/shard_map/ppermute | solution.py:34
  257.4 1.9 collective-permute-start.5
  260.2 2.1 shard_map.134
  262.3 3.6 %collective-permute-done.5 = bf16[256,128]{1,0:T(8,128)(2,1)S(1)} collective-permute-done((bf16[256,128]{1,0:T(8,128)(2,1)S(1)}, bf16[256,128]{1,0:T(8,128)(2,1)S(1)}, u32[]{:S(2)}, u32[]{:S(2)}) %collective-permute-start.5) | collective-permute-done | bytes 65568 | tf_op jit(solution)/shard_map/ppermute | solution.py:34
  (103 shorter events, 25.1 us)
Async XLA Ops:
  7.2 78.8 %copy-start = (bf16[1024,256]{1,0:T(8,128)(2,1)S(1)}, bf16[1024,256]{1,0:T(8,128)(2,1)}, u32[]{:S(2)}) copy-start(bf16[1024,256]{1,0:T(8,128)(2,1)} %param.18) | copy-start | bytes 1572868
  7.2 75.8 %all-gather.6.cloned.1.call-start = ((), (), s32[]{:S(2)}) async-start(), calls=%async_computation.9 | async-start | bytes 4456448 | tf_op jit(solution)/shard_map/all_gather | solution.py:209
  11.7 4.7 %copy-start.11 = (bf16[256,128]{1,0:T(8,128)(2,1)S(1)}, bf16[256,128]{1,0:T(8,128)(2,1)}, u32[]{:S(2)}) copy-start(bf16[256,128]{1,0:T(8,128)(2,1)} %param.11) | copy-start | bytes 196612
  11.7 42.4 %all-to-all-start = ((bf16[16,256,256]{2,1,0:T(8,128)(2,1)}), bf16[16,256,256]{2,1,0:T(8,128)(2,1)S(1)}, u32[]{:S(2)}, u32[]{:S(2)}) async-start(bf16[16,256,256]{2,1,0:T(8,128)(2,1)} %bitcast.78), calls=%async_computation | async-start | bytes 4194304 | tf_op jit(solution)/shard_map/all_to_all | solution.py:216
  16.4 36.3 %collective-permute-start = (bf16[128,128]{1,0:T(8,128)(2,1)S(1)}, bf16[128,128]{1,0:T(8,128)(2,1)S(1)}, u32[]{:S(2)}, u32[]{:S(2)}) collective-permute-start(bf16[128,128]{1,0:T(8,128)(2,1)S(1)} %get-tuple-element.48), channel_id=1, source_target_pairs={{0,0},{1,32},{2,64},{3,96},{4,128},{5,160},{6,192},{7,224},{8,256}... | collective-permute-start | bytes 98312 | tf_op jit(solution)/shard_map/ppermute | solution.py:205
  21.1 31.6 %collective-permute-start.1 = (bf16[128,128]{1,0:T(8,128)(2,1)S(1)}, bf16[128,128]{1,0:T(8,128)(2,1)S(1)}, u32[]{:S(2)}, u32[]{:S(2)}) collective-permute-start(bf16[128,128]{1,0:T(8,128)(2,1)S(1)} %get-tuple-element.49), channel_id=1, source_target_pairs={{0,16},{1,48},{2,80},{3,112},{4,144},{5,176},{6,208},{7,240},{8,27... | collective-permute-start | bytes 98312 | tf_op jit(solution)/shard_map/ppermute | solution.py:205
  54.8 19.0 %all-to-all-start.1 = ((bf16[4,128,256]{2,1,0:T(8,128)(2,1)}), bf16[4,128,256]{2,1,0:T(8,128)(2,1)S(1)}, u32[]{:S(2)}, u32[]{:S(2)}) async-start(bf16[4,128,256]{2,1,0:T(8,128)(2,1)} %broadcast_in_dim.16), calls=%async_computation.1 | async-start | bytes 524288 | tf_op jit(solution)/shard_map/all_to_all | solution.py:29
  73.8 9.9 %copy-start.10 = (s32[16384]{0:T(1024)S(1)}, s32[16384]{0:T(1024)}, u32[]{:S(2)}) copy-start(s32[16384]{0:T(1024)} %param.19) | copy-start | bytes 196612
  73.8 11.2 %copy-start.7 = (bf16[512,1024]{1,0:T(8,128)(2,1)S(1)}, bf16[512,1024]{1,0:T(8,128)(2,1)}, u32[]{:S(2)}) copy-start(bf16[512,1024]{1,0:T(8,128)(2,1)} %param.17) | copy-start | bytes 3145732
  73.8 9.1 %copy-start.9 = (bf16[4,128,256]{2,1,0:T(8,128)(2,1)}, bf16[4,128,256]{2,1,0:T(8,128)(2,1)S(1)}, u32[]{:S(2)}) copy-start(bf16[4,128,256]{2,1,0:T(8,128)(2,1)S(1)} %all-to-all-done.1) | copy-start | bytes 786436
  73.8 37.0 %all-to-all-start.2 = ((bf16[16,256,256]{2,1,0:T(8,128)(2,1)}), bf16[16,256,256]{2,1,0:T(8,128)(2,1)}, u32[]{:S(2)}, u32[]{:S(2)}) async-start(bf16[16,256,256]{2,1,0:T(8,128)(2,1)} %copy-done.2), calls=%async_computation.2 | async-start | bytes 4194304 | tf_op jit(solution)/shard_map/all_to_all | solution.py:229
  82.9 46.4 %all-gather.4.cloned.1.call-start = ((), (), s32[]{:S(2)}) async-start(), calls=%async_computation.7 | async-start | bytes 2359296 | tf_op jit(solution)/shard_map/all_gather | solution.py:220
  83.6 161.6 %reduce-scatter.2.cloned.1.call-start = ((), (), s32[]{:S(2)}) async-start(), calls=%async_computation.8 | async-start | bytes 2359296 | tf_op jit(solution)/shard_map/reduce_scatter | solution.py:301
  129.3 2.2 copy-start.3
  131.5 1.6 copy-start.4
  163.6 8.5 %copy-start.5 = (f32[4096]{0:T(1024)S(1)}, f32[4096]{0:T(1024)}, u32[]{:S(2)}) copy-start(f32[4096]{0:T(1024)} %param.12) | copy-start | bytes 49156
  163.6 8.5 %copy-start.6 = (f32[4096]{0:T(1024)S(1)}, f32[4096]{0:T(1024)}, u32[]{:S(2)}) copy-start(f32[4096]{0:T(1024)} %param.13) | copy-start | bytes 49156
  163.6 6.6 %collective-permute-start.2 = (bf16[8,528,256]{2,1,0:T(8,128)(2,1)}, bf16[8,528,256]{2,1,0:T(8,128)(2,1)}, u32[]{:S(2)}, u32[]{:S(2)}) collective-permute-start(bf16[8,528,256]{2,1,0:T(8,128)(2,1)} %all_to_all.30.mine_ref), channel_id=1, source_target_pairs={{0,1},{1,0},{2,3},{3,2},{4,5},{5,4},{6,7},{7,6},{8,9},{9,8},{10,11... | collective-permute-start | bytes 6488072 | tf_op jit(solution)/shard_map/ppermute | solution.py:39
  182.2 31.1 %all-to-all-start.4 = ((bf16[32,80,128]{2,1,0:T(8,128)(2,1)}), bf16[32,80,128]{2,1,0:T(8,128)(2,1)S(1)}, u32[]{:S(2)}, u32[]{:S(2)}) async-start(bf16[32,80,128]{2,1,0:T(8,128)(2,1)} %shard_map.133), calls=%async_computation.5 | async-start | bytes 1310720 | tf_op jit(solution)/shard_map/all_to_all | solution.py:310
  214.3 45.1 %all-to-all-start.5 = ((bf16[32,64,128]{2,1,0:T(8,128)(2,1)}), bf16[32,64,128]{2,1,0:T(8,128)(2,1)S(1)}, u32[]{:S(2)}, u32[]{:S(2)}) async-start(bf16[32,64,128]{2,1,0:T(8,128)(2,1)} %broadcast_in_dim.25), calls=%async_computation.6 | async-start | bytes 1048576 | tf_op jit(solution)/shard_map/all_to_all | solution.py:29
  222.4 45.4 %copy-start.12 = (f32[256]{0:T(256)}, f32[256]{0:T(256)S(1)}, u32[]{:S(2)}) copy-start(f32[256]{0:T(256)S(1)} %multiply_bitcast_fusion.2) | copy-start | bytes 3076
  246.2 16.1 %collective-permute-start.3 = (bf16[256,128]{1,0:T(8,128)(2,1)S(1)}, bf16[256,128]{1,0:T(8,128)(2,1)S(1)}, u32[]{:S(2)}, u32[]{:S(2)}) collective-permute-start(bf16[256,128]{1,0:T(8,128)(2,1)S(1)} %get-tuple-element.39), channel_id=1, source_target_pairs={{0,16},{16,32},{32,48},{48,0},{1,17},{17,33},{33,49},{49,1},{2,18}... | collective-permute-start | bytes 196616 | tf_op jit(solution)/shard_map/ppermute | solution.py:34
  248.1 14.2 %collective-permute-start.4 = (bf16[256,128]{1,0:T(8,128)(2,1)S(1)}, bf16[256,128]{1,0:T(8,128)(2,1)S(1)}, u32[]{:S(2)}, u32[]{:S(2)}) collective-permute-start(bf16[256,128]{1,0:T(8,128)(2,1)S(1)} %get-tuple-element.41), channel_id=1, source_target_pairs={{0,32},{16,48},{32,0},{48,16},{1,33},{17,49},{33,1},{49,17},{2,34}... | collective-permute-start | bytes 196616 | tf_op jit(solution)/shard_map/ppermute | solution.py:34
  257.4 8.5 %collective-permute-start.5 = (bf16[256,128]{1,0:T(8,128)(2,1)S(1)}, bf16[256,128]{1,0:T(8,128)(2,1)S(1)}, u32[]{:S(2)}, u32[]{:S(2)}) collective-permute-start(bf16[256,128]{1,0:T(8,128)(2,1)S(1)} %get-tuple-element.40), channel_id=1, source_target_pairs={{0,48},{16,0},{32,16},{48,32},{1,49},{17,1},{33,17},{49,33},{2,50}... | collective-permute-start | bytes 196616 | tf_op jit(solution)/shard_map/ppermute | solution.py:34
  (3 other events, 3.5 us)
Sparse Core Ops, SparseCore 0:
  10.2 59.4 all-gather.5
  86.4 42.8 all-gather.3
  180.7 64.4 reduce-scatter.1

commit v7 on v4

--- a/solution.py
+++ b/solution.py
@@ -37,6 +37,11 @@
 def tensor_gather(block):
     mine = broadcast_gather(block, TN[:2])
     return mine, lax.ppermute(mine, "c", [(0, 1), (1, 0)])
+
+
+def tensor_gather_twice(block):
+    other = lax.ppermute(block, "c", [(0, 1), (1, 0)])
+    return broadcast_gather(block, TN[:2]), broadcast_gather(other, TN[:2])
 
 
 def parity_sign(value):
@@ -202,7 +207,7 @@
     near = broadcast_gather(strip, "yh")
     proj = lax.all_gather(near.reshape(-1, own), "z", axis=0, tiled=True)
     teacher, _ = lax.optimization_barrier((teacher_in, near))
-    teacher = tensor_gather(teacher)
+    teacher = lax.cond(image_ids[0] >= 0, tensor_gather, tensor_gather_twice, teacher)
 
     normed = layer_norm(student_in.astype(F32)).astype(BF)
     predicted = jnp.dot(normed, head_weight, preferred_element_type=F32)
@@ -216,12 +221,13 @@
 
     smem, vmem = pl.BlockSpec(memory_space=pltpu.SMEM), pl.BlockSpec(memory_space=pltpu.VMEM)
     position = tpos.reshape(1)
+    proj, normed, predicted, token_weight = lax.optimization_barrier((proj, normed, predicted, token_weight))
     raw, stat = pl.pallas_call(
         project_kernel,
         out_shape=(jax.ShapeDtypeStruct((rows, own), BF), jax.ShapeDtypeStruct((rows, 2), F32)),
         in_specs=[smem, vmem, vmem, vmem],
         out_specs=(vmem, vmem),
-        compiler_params=pltpu.CompilerParams(vmem_limit_bytes=40 << 20),
+        compiler_params=pltpu.CompilerParams(vmem_limit_bytes=16 << 20),
         cost_estimate=pl.CostEstimate(flops=2 * rows * width * own, bytes_accessed=8 << 20, transcendentals=0),
     )(position, *teacher, proj)
     pieces = jnp.stack(split3(stat.T)).reshape(6 * rows // own, own).astype(BF)
@@ -257,7 +263,7 @@
         ),
         in_specs=[smem] + [vmem] * 8,
         out_specs=(vmem,) * 3,
-        compiler_params=pltpu.CompilerParams(vmem_limit_bytes=40 << 20),
+        compiler_params=pltpu.CompilerParams(vmem_limit_bytes=16 << 20),
         cost_estimate=pl.CostEstimate(flops=2 * rows * width * own, bytes_accessed=12 << 20, transcendentals=0),
     )(
         position,
@@ -276,7 +282,7 @@
         out_shape=jax.ShapeDtypeStruct((chunks, own, part), BF),
         in_specs=[smem, vmem, vmem],
         out_specs=vmem,
-        compiler_params=pltpu.CompilerParams(vmem_limit_bytes=24 << 20),
+        compiler_params=pltpu.CompilerParams(vmem_limit_bytes=12 << 20),
         cost_estimate=pl.CostEstimate(flops=2 * rows * width * own, bytes_accessed=6 << 20, transcendentals=0),
     )(position, features, sums)
     within = lax.psum_scatter(moment, "z", scatter_dimension=0, tiled=True)
@@ -286,7 +292,7 @@
         out_shape=jax.ShapeDtypeStruct(lines.shape, BF),
         in_specs=[smem, vmem, vmem],
         out_specs=vmem,
-        compiler_params=pltpu.CompilerParams(vmem_limit_bytes=24 << 20),
+        compiler_params=pltpu.CompilerParams(vmem_limit_bytes=12 << 20),
     )(scale, lines, table)
     target = lax.all_to_all(lines, TN, 0, 0, tiled=True).reshape(rows, own)
 
@@ -295,12 +301,11 @@
         out_shape=jax.ShapeDtypeStruct((chunks, 2 * depth + 16, part), BF),
         in_specs=[smem] + [vmem] * 5,
         out_specs=vmem,
-        compiler_params=pltpu.CompilerParams(vmem_limit_bytes=24 << 20),
+        compiler_params=pltpu.CompilerParams(vmem_limit_bytes=12 << 20),
     )(position, target, predicted, token_weight, normed, sums)
     taken = lax.all_to_all(sent, DP, 0, 0, tiled=True)
 
     grad_own = jnp.sum(taken[:, : 2 * depth, :].astype(F32), axis=0).astype(BF)
-    within, grad_own = lax.optimization_barrier((within, grad_own))
     places, here = lax.axis_size("yh"), lax.axis_index("yh")
     within_sum = within[here].astype(F32)
     for k in range(1, places):

time: 254 us -> 250 us (0.984)
  blocking collectives: 44.9 us -> 94.2 us
  waiting for transfers between devices: 87.9 us -> 53.2 us
  starting transfers between devices: 69.9 us -> 48.9 us
    all_to_all x2 -> x3, blocking collectives: 44.9 us -> 94.2 us  [broadcast_gather(): lax.all_to_all(jnp.broadcast_to(block[None], (count,) + block.shape), axe...]
    all_to_all x2 -> x1, waiting for transfers between devices: 27.2 us -> 6.2 us  [broadcast_gather(): lax.all_to_all(jnp.broadcast_to(block[None], (count,) + block.shape), axe...]
    all_to_all x2 -> x1, starting transfers between devices: 24.2 us -> 5.08 us  [broadcast_gather(): lax.all_to_all(jnp.broadcast_to(block[None], (count,) + block.shape), axe...]
    all_gather x1, waiting for transfers between devices: 14.9 us -> 0.01 us  [body(): proj = lax.all_gather(near.reshape(-1, own), 'z', axis=0, tiled=True)]
    ppermute x2, waiting for transfers between devices: 4.14 us -> 7.72 us  [tensor_gather(): return (mine, lax.ppermute(mine, 'c', [(0, 1), (1, 0)]))]
    ppermute x3, waiting for transfers between devices: 3.19 us -> 0.01 us  [shift(): lax.ppermute(block, axis, [(i, (i + step) % count) for i in range(count)])]
    unnamed x22 -> x24, local copies, waits for them, and re-layouts: 4.2 us -> 5.65 us
  transfers between devices with their start and end apart: 14 -> 13, of which waited for: 9 -> 7; matrix products, arithmetic and copies ran while one was open for 3% -> 4% of each run, Pallas kernels for 1% -> 2%
where the time goes in v7:
time: 250 us; the launch traced here: 249 us
  blocking collectives  94.2 us (38%)
  waiting for transfers between devices  53.2 us (21%)
  starting transfers between devices  48.9 us (20%)
  between operations  16 us (6%)
  Pallas kernels  15.5 us (6%)
  local copies, waits for them, and re-layouts  11.7 us (5%)
  other arithmetic  6.73 us (3%)
    all_to_all x3, blocking collectives, broadcast_gather(): lax.all_to_all(jnp.broadcast_to(block[None], (count,) + block.shape), axe...  94.2 us
    all_to_all x1, waiting for transfers between devices, body(): taken = lax.all_to_all(sent, DP, 0, 0, tiled=True)  23.4 us
    ppermute x3, starting transfers between devices, shift(): lax.ppermute(block, axis, [(i, (i + step) % count) for i in range(count)])  15.6 us
    ppermute x2, starting transfers between devices, body(): got.append(lax.ppermute(send, DP + TN, route))  7.86 us
    ppermute x2, waiting for transfers between devices, tensor_gather(): return (mine, lax.ppermute(mine, 'c', [(0, 1), (1, 0)]))  7.72 us
    all_to_all x1, waiting for transfers between devices, body(): target = lax.all_to_all(lines, TN, 0, 0, tiled=True).reshape(rows, own)  6.67 us
    all_to_all x1, starting transfers between devices, body(): taken = lax.all_to_all(sent, DP, 0, 0, tiled=True)  6.6 us
    all_to_all x1, waiting for transfers between devices, broadcast_gather(): lax.all_to_all(jnp.broadcast_to(block[None], (count,) + block.shape), axe...  6.2 us
  transfers between devices with their start and end apart: 13, of which 7 were waited for; matrix products, arithmetic and copies ran while one was open for 4% of the time, Pallas kernels for 2%

profile of v7, /device:TPU:8, one launch (start us, length us, event | category | flops | bytes accessed | tf_op | source)
XLA Modules:
  0.0 248.6 jit_solution(3466925986994410017)
XLA Ops:
  8.2 4.2 %collective-permute-start.2 = (bf16[128,128]{1,0:T(8,128)(2,1)S(1)}, bf16[128,128]{1,0:T(8,128)(2,1)S(1)}, u32[]{:S(2)}, u32[]{:S(2)}) collective-permute-start(bf16[128,128]{1,0:T(8,128)(2,1)S(1)} %get-tuple-element.46), channel_id=1, source_target_pairs={{0,0},{1,32},{2,64},{3,96},{4,128},{5,160},{6,192},{7,224},{8,256}... | collective-permute-start | bytes 98312 | tf_op jit(solution)/shard_map/ppermute | solution.py:203
  12.3 3.7 %collective-permute-start.3 = (bf16[128,128]{1,0:T(8,128)(2,1)S(1)}, bf16[128,128]{1,0:T(8,128)(2,1)S(1)}, u32[]{:S(2)}, u32[]{:S(2)}) collective-permute-start(bf16[128,128]{1,0:T(8,128)(2,1)S(1)} %get-tuple-element.47), channel_id=1, source_target_pairs={{0,16},{1,48},{2,80},{3,112},{4,144},{5,176},{6,208},{7,240},{8,27... | collective-permute-start | bytes 98312 | tf_op jit(solution)/shard_map/ppermute | solution.py:203
  16.1 3.6 %collective-permute-done.3 = bf16[128,128]{1,0:T(8,128)(2,1)S(1)} collective-permute-done((bf16[128,128]{1,0:T(8,128)(2,1)S(1)}, bf16[128,128]{1,0:T(8,128)(2,1)S(1)}, u32[]{:S(2)}, u32[]{:S(2)}) %collective-permute-start.3) | collective-permute-done | bytes 32800 | tf_op jit(solution)/shard_map/ppermute | solution.py:203
  19.7 16.9 %all_to_all.44 = bf16[4,128,256]{2,1,0:T(8,128)(2,1)} all-to-all(bf16[4,128,256]{2,1,0:T(8,128)(2,1)S(1)} %broadcast_in_dim.36), channel_id=1, replica_groups=mesh['z'=8,'yh'=4,'x'=4,'yl'=2,'c'=2] {'yh'}, dimensions={0} | all-to-all | bytes 524288 | tf_op jit(solution)/shard_map/all_to_all | solution.py:29
  42.9 52.4 %conditional.1 = (bf16[8,512,256]{2,1,0:T(8,128)(2,1)}, bf16[8,512,256]{2,1,0:T(8,128)(2,1)}) conditional(s32[]{:T(128)} %bitcast.1, bf16[512,256]{1,0:T(8,128)(2,1)S(1)} %copy-done.8, bf16[512,256]{1,0:T(8,128)(2,1)S(1)} %copy-done.8), branch_computations={%region_0.1_spmd, %region_1.2_spmd} | conditional | bytes 16253016 | solution.py:210
  43.1 45.8 %all_to_all.43 = bf16[8,512,256]{2,1,0:T(8,128)(2,1)} all-to-all(bf16[8,512,256]{2,1,0:T(8,128)(2,1)S(1)} %broadcast_in_dim.24), channel_id=1, replica_groups=mesh['z'=8,'yh'=4,'x'=4,'yl'=2,'c'=2] {'x','yl'}, dimensions={0} | all-to-all | bytes 4194304 | tf_op jit(solution)/shard_map/cond/branch_1_fun/all_to_all | solution.py:29
  88.9 2.2 collective-permute-start.1
  91.1 4.2 %collective-permute-done.1 = bf16[8,512,256]{2,1,0:T(8,128)(2,1)} collective-permute-done((bf16[8,512,256]{2,1,0:T(8,128)(2,1)}, bf16[8,512,256]{2,1,0:T(8,128)(2,1)}, u32[]{:S(2)}, u32[]{:S(2)}) %collective-permute-start.1) | collective-permute-done | bytes 2097184 | tf_op jit(solution)/shard_map/cond/branch_1_fun/ppermute | solution.py:39
  96.9 3.6 %shard_map.129 = (bf16[512,256]{1,0:T(8,128)(2,1)S(1)}, f32[512,2]{1,0:T(8,128)S(1)}) custom-call(s32[1]{0:T(128)} %bitcast.pos_ref, bf16[8,512,256]{2,1,0:T(8,128)(2,1)} %get-tuple-element.19.mine_ref, bf16[8,512,256]{2,1,0:T(8,128)(2,1)} %get-tuple-element.20.other_ref, bf16[4096,256]{1,0:T(8,128)(2,1)S(1)} %copy-done.2), custom_call_target="tpu_custom_call" | custom-call | flops 1073741824 | bytes 8388608 | tf_op jit(solution)/shard_map/pallas_call | solution.py:225
  101.3 31.5 %all_to_all.45.mine_ref = bf16[8,528,256]{2,1,0:T(8,128)(2,1)} all-to-all(bf16[8,528,256]{2,1,0:T(8,128)(2,1)S(1)} %broadcast_in_dim.44), channel_id=1, replica_groups=mesh['z'=8,'yh'=4,'x'=4,'yl'=2,'c'=2] {'x','yl'}, dimensions={0} | all-to-all | bytes 4325376 | tf_op jit(solution)/shard_map/all_to_all | solution.py:29
  135.9 3.5 %collective-permute-done.4.other_ref = bf16[8,528,256]{2,1,0:T(8,128)(2,1)} collective-permute-done((bf16[8,528,256]{2,1,0:T(8,128)(2,1)}, bf16[8,528,256]{2,1,0:T(8,128)(2,1)}, u32[]{:S(2)}, u32[]{:S(2)}) %collective-permute-start.4) | collective-permute-done | bytes 2162720 | tf_op jit(solution)/shard_map/ppermute | solution.py:39
  142.9 5.9 %shard_map.130 = (bf16[16,512,256]{2,1,0:T(8,128)(2,1)S(1)}, bf16[512,256]{1,0:T(8,128)(2,1)}, f32[16,1,256]{2,1,0:T(1,128)S(1)}) custom-call(s32[1]{0:T(128)} %bitcast.pos_ref, bf16[8,528,256]{2,1,0:T(8,128)(2,1)} %all_to_all.45.mine_ref, bf16[8,528,256]{2,1,0:T(8,128)(2,1)} %collective-permute-done.4.other_ref, f32[512,16]{1,0:T(8,128)S(1)} %bitcast.75, ...), custom_call_target="tpu_custom_call" | custom-call | flops 1073741824 | bytes 12582912 | tf_op jit(solution)/shard_map/pallas_call | solution.py:257
  151.6 4.6 %all-to-all-start.5 = ((bf16[16,32,256]{2,1,0:T(8,128)(2,1)}), bf16[16,32,256]{2,1,0:T(8,128)(2,1)S(1)}, u32[]{:S(2)}, u32[]{:S(2)}) async-start(bf16[16,32,256]{2,1,0:T(8,128)(2,1)} %bitcast.23), calls=%async_computation.6 | async-start | bytes 524288 | tf_op jit(solution)/shard_map/all_to_all | solution.py:279
  157.4 5.6 %all-to-all-done.5.basis_ref = bf16[16,32,256]{2,1,0:T(8,128)(2,1)S(1)} async-done(((bf16[16,32,256]{2,1,0:T(8,128)(2,1)}), bf16[16,32,256]{2,1,0:T(8,128)(2,1)S(1)}, u32[]{:S(2)}, u32[]{:S(2)}) %all-to-all-start.5) | async-done | bytes 262176 | tf_op jit(solution)/shard_map/all_to_all | solution.py:279
  164.0 4.9 %all-to-all-start.6 = ((bf16[16,32,256]{2,1,0:T(8,128)(2,1)}), bf16[16,32,256]{2,1,0:T(8,128)(2,1)S(1)}, u32[]{:S(2)}, u32[]{:S(2)}) async-start(bf16[16,32,256]{2,1,0:T(8,128)(2,1)} %shard_map.132), calls=%async_computation.7 | async-start | bytes 524288 | tf_op jit(solution)/shard_map/all_to_all | solution.py:297
  169.1 6.7 %all-to-all-done.6 = bf16[16,32,256]{2,1,0:T(8,128)(2,1)S(1)} async-done(((bf16[16,32,256]{2,1,0:T(8,128)(2,1)}), bf16[16,32,256]{2,1,0:T(8,128)(2,1)S(1)}, u32[]{:S(2)}, u32[]{:S(2)}) %all-to-all-start.6) | async-done | bytes 262176 | tf_op jit(solution)/shard_map/all_to_all | solution.py:297
  177.3 6.6 %all-to-all-start.7 = ((bf16[32,80,128]{2,1,0:T(8,128)(2,1)}), bf16[32,80,128]{2,1,0:T(8,128)(2,1)S(1)}, u32[]{:S(2)}, u32[]{:S(2)}) async-start(bf16[32,80,128]{2,1,0:T(8,128)(2,1)} %shard_map.133), calls=%async_computation.8 | async-start | bytes 1310720 | tf_op jit(solution)/shard_map/all_to_all | solution.py:306
  183.9 23.4 %all-to-all-done.7 = bf16[32,80,128]{2,1,0:T(8,128)(2,1)S(1)} async-done(((bf16[32,80,128]{2,1,0:T(8,128)(2,1)}), bf16[32,80,128]{2,1,0:T(8,128)(2,1)S(1)}, u32[]{:S(2)}, u32[]{:S(2)}) %all-to-all-start.7) | async-done | bytes 655392 | tf_op jit(solution)/shard_map/all_to_all | solution.py:306
  208.3 5.1 %all-to-all-start.8 = ((bf16[32,64,128]{2,1,0:T(8,128)(2,1)}), bf16[32,64,128]{2,1,0:T(8,128)(2,1)S(1)}, u32[]{:S(2)}, u32[]{:S(2)}) async-start(bf16[32,64,128]{2,1,0:T(8,128)(2,1)} %broadcast_in_dim.46), calls=%async_computation.9 | async-start | bytes 1048576 | tf_op jit(solution)/shard_map/all_to_all | solution.py:29
  215.1 4.6 %collective-permute-start.5 = (bf16[256,128]{1,0:T(8,128)(2,1)S(1)}, bf16[256,128]{1,0:T(8,128)(2,1)S(1)}, u32[]{:S(2)}, u32[]{:S(2)}) collective-permute-start(bf16[256,128]{1,0:T(8,128)(2,1)S(1)} %get-tuple-element.37), channel_id=1, source_target_pairs={{0,16},{16,32},{32,48},{48,0},{1,17},{17,33},{33,49},{49,1},{2,18}... | collective-permute-start | bytes 196616 | tf_op jit(solution)/shard_map/ppermute | solution.py:34
  219.7 5.5 %collective-permute-start.6 = (bf16[256,128]{1,0:T(8,128)(2,1)S(1)}, bf16[256,128]{1,0:T(8,128)(2,1)S(1)}, u32[]{:S(2)}, u32[]{:S(2)}) collective-permute-start(bf16[256,128]{1,0:T(8,128)(2,1)S(1)} %get-tuple-element.39), channel_id=1, source_target_pairs={{0,32},{16,48},{32,0},{48,16},{1,33},{17,49},{33,1},{49,17},{2,34}... | collective-permute-start | bytes 196616 | tf_op jit(solution)/shard_map/ppermute | solution.py:34
  225.2 5.5 %collective-permute-start.7 = (bf16[256,128]{1,0:T(8,128)(2,1)S(1)}, bf16[256,128]{1,0:T(8,128)(2,1)S(1)}, u32[]{:S(2)}, u32[]{:S(2)}) collective-permute-start(bf16[256,128]{1,0:T(8,128)(2,1)S(1)} %get-tuple-element.38), channel_id=1, source_target_pairs={{0,48},{16,0},{32,16},{48,32},{1,49},{17,1},{33,17},{49,33},{2,50}... | collective-permute-start | bytes 196616 | tf_op jit(solution)/shard_map/ppermute | solution.py:34
  230.8 6.2 %all-to-all-done.8.in_ref = bf16[32,64,128]{2,1,0:T(8,128)(2,1)S(1)} async-done(((bf16[32,64,128]{2,1,0:T(8,128)(2,1)}), bf16[32,64,128]{2,1,0:T(8,128)(2,1)S(1)}, u32[]{:S(2)}, u32[]{:S(2)}) %all-to-all-start.8) | async-done | bytes 524320 | tf_op jit(solution)/shard_map/all_to_all | solution.py:29
  237.8 2.1 shard_map.134
  (101 shorter events, 26.7 us)
Async XLA Ops:
  7.2 35.1 %copy-start = (bf16[1024,256]{1,0:T(8,128)(2,1)S(1)}, bf16[1024,256]{1,0:T(8,128)(2,1)}, u32[]{:S(2)}) copy-start(bf16[1024,256]{1,0:T(8,128)(2,1)} %param.20) | copy-start | bytes 1572868
  7.2 34.1 %copy-start.6 = (bf16[512,1024]{1,0:T(8,128)(2,1)S(1)}, bf16[512,1024]{1,0:T(8,128)(2,1)}, u32[]{:S(2)}) copy-start(bf16[512,1024]{1,0:T(8,128)(2,1)} %param.19) | copy-start | bytes 3145732
  7.2 88.1 %all-gather.2.cloned.1.call-start = ((), (), s32[]{:S(2)}) async-start(), calls=%async_computation.10 | async-start | bytes 2359296 | tf_op jit(solution)/shard_map/all_gather | solution.py:208
  8.2 7.9 %collective-permute-start.2 = (bf16[128,128]{1,0:T(8,128)(2,1)S(1)}, bf16[128,128]{1,0:T(8,128)(2,1)S(1)}, u32[]{:S(2)}, u32[]{:S(2)}) collective-permute-start(bf16[128,128]{1,0:T(8,128)(2,1)S(1)} %get-tuple-element.46), channel_id=1, source_target_pairs={{0,0},{1,32},{2,64},{3,96},{4,128},{5,160},{6,192},{7,224},{8,256}... | collective-permute-start | bytes 98312 | tf_op jit(solution)/shard_map/ppermute | solution.py:203
  12.3 7.3 %collective-permute-start.3 = (bf16[128,128]{1,0:T(8,128)(2,1)S(1)}, bf16[128,128]{1,0:T(8,128)(2,1)S(1)}, u32[]{:S(2)}, u32[]{:S(2)}) collective-permute-start(bf16[128,128]{1,0:T(8,128)(2,1)S(1)} %get-tuple-element.47), channel_id=1, source_target_pairs={{0,16},{1,48},{2,80},{3,112},{4,144},{5,176},{6,208},{7,240},{8,27... | collective-permute-start | bytes 98312 | tf_op jit(solution)/shard_map/ppermute | solution.py:203
  36.6 177.6 %reduce-scatter.2.cloned.1.call-start = ((), (), s32[]{:S(2)}) async-start(), calls=%async_computation.11 | async-start | bytes 2359296 | tf_op jit(solution)/shard_map/reduce_scatter | solution.py:288
  42.0 1.0 copy-start.8
  88.9 6.4 %collective-permute-start.1 = (bf16[8,512,256]{2,1,0:T(8,128)(2,1)}, bf16[8,512,256]{2,1,0:T(8,128)(2,1)}, u32[]{:S(2)}, u32[]{:S(2)}) collective-permute-start(bf16[8,512,256]{2,1,0:T(8,128)(2,1)} %all_to_all.43), channel_id=1, source_target_pairs={{0,1},{1,0},{2,3},{3,2},{4,5},{5,4},{6,7},{7,6},{8,9},{9,8},{10,11... | collective-permute-start | bytes 6291464 | tf_op jit(solution)/shard_map/cond/branch_1_fun/ppermute | solution.py:39
  95.3 1.6 copy-start.2
  101.3 33.6 %copy-start.10 = (s32[256]{0:T(256)S(1)}, s32[256]{0:T(256)}, u32[]{:S(2)}) copy-start(s32[256]{0:T(256)} %param.17) | copy-start | bytes 3076
  132.8 8.5 %copy-start.4 = (f32[4096]{0:T(1024)S(1)}, f32[4096]{0:T(1024)}, u32[]{:S(2)}) copy-start(f32[4096]{0:T(1024)} %param.14) | copy-start | bytes 49156
  132.8 8.5 %copy-start.5 = (f32[4096]{0:T(1024)S(1)}, f32[4096]{0:T(1024)}, u32[]{:S(2)}) copy-start(f32[4096]{0:T(1024)} %param.15) | copy-start | bytes 49156
  132.8 6.6 %collective-permute-start.4 = (bf16[8,528,256]{2,1,0:T(8,128)(2,1)}, bf16[8,528,256]{2,1,0:T(8,128)(2,1)}, u32[]{:S(2)}, u32[]{:S(2)}) collective-permute-start(bf16[8,528,256]{2,1,0:T(8,128)(2,1)} %all_to_all.45.mine_ref), channel_id=1, source_target_pairs={{0,1},{1,0},{2,3},{3,2},{4,5},{5,4},{6,7},{7,6},{8,9},{9,8},{10,11... | collective-permute-start | bytes 6488072 | tf_op jit(solution)/shard_map/ppermute | solution.py:39
  141.3 1.6 copy-start.3
  150.2 1.4 copy-start.1
  151.6 11.5 %all-to-all-start.5 = ((bf16[16,32,256]{2,1,0:T(8,128)(2,1)}), bf16[16,32,256]{2,1,0:T(8,128)(2,1)S(1)}, u32[]{:S(2)}, u32[]{:S(2)}) async-start(bf16[16,32,256]{2,1,0:T(8,128)(2,1)} %bitcast.23), calls=%async_computation.6 | async-start | bytes 524288 | tf_op jit(solution)/shard_map/all_to_all | solution.py:279
  164.0 11.7 %all-to-all-start.6 = ((bf16[16,32,256]{2,1,0:T(8,128)(2,1)}), bf16[16,32,256]{2,1,0:T(8,128)(2,1)S(1)}, u32[]{:S(2)}, u32[]{:S(2)}) async-start(bf16[16,32,256]{2,1,0:T(8,128)(2,1)} %shard_map.132), calls=%async_computation.7 | async-start | bytes 524288 | tf_op jit(solution)/shard_map/all_to_all | solution.py:297
  177.3 30.1 %all-to-all-start.7 = ((bf16[32,80,128]{2,1,0:T(8,128)(2,1)}), bf16[32,80,128]{2,1,0:T(8,128)(2,1)S(1)}, u32[]{:S(2)}, u32[]{:S(2)}) async-start(bf16[32,80,128]{2,1,0:T(8,128)(2,1)} %shard_map.133), calls=%async_computation.8 | async-start | bytes 1310720 | tf_op jit(solution)/shard_map/all_to_all | solution.py:306
  208.3 28.6 %all-to-all-start.8 = ((bf16[32,64,128]{2,1,0:T(8,128)(2,1)}), bf16[32,64,128]{2,1,0:T(8,128)(2,1)S(1)}, u32[]{:S(2)}, u32[]{:S(2)}) async-start(bf16[32,64,128]{2,1,0:T(8,128)(2,1)} %broadcast_in_dim.46), calls=%async_computation.9 | async-start | bytes 1048576 | tf_op jit(solution)/shard_map/all_to_all | solution.py:29
  213.6 28.1 %copy-start.9 = (f32[256]{0:T(256)}, f32[256]{0:T(256)S(1)}, u32[]{:S(2)}) copy-start(f32[256]{0:T(256)S(1)} %multiply_bitcast_fusion.2) | copy-start | bytes 3076
  215.1 24.7 %collective-permute-start.5 = (bf16[256,128]{1,0:T(8,128)(2,1)S(1)}, bf16[256,128]{1,0:T(8,128)(2,1)S(1)}, u32[]{:S(2)}, u32[]{:S(2)}) collective-permute-start(bf16[256,128]{1,0:T(8,128)(2,1)S(1)} %get-tuple-element.37), channel_id=1, source_target_pairs={{0,16},{16,32},{32,48},{48,0},{1,17},{17,33},{33,49},{49,1},{2,18}... | collective-permute-start | bytes 196616 | tf_op jit(solution)/shard_map/ppermute | solution.py:34
  219.7 20.1 %collective-permute-start.6 = (bf16[256,128]{1,0:T(8,128)(2,1)S(1)}, bf16[256,128]{1,0:T(8,128)(2,1)S(1)}, u32[]{:S(2)}, u32[]{:S(2)}) collective-permute-start(bf16[256,128]{1,0:T(8,128)(2,1)S(1)} %get-tuple-element.39), channel_id=1, source_target_pairs={{0,32},{16,48},{32,0},{48,16},{1,33},{17,49},{33,1},{49,17},{2,34}... | collective-permute-start | bytes 196616 | tf_op jit(solution)/shard_map/ppermute | solution.py:34
  225.2 14.6 %collective-permute-start.7 = (bf16[256,128]{1,0:T(8,128)(2,1)S(1)}, bf16[256,128]{1,0:T(8,128)(2,1)S(1)}, u32[]{:S(2)}, u32[]{:S(2)}) collective-permute-start(bf16[256,128]{1,0:T(8,128)(2,1)S(1)} %get-tuple-element.38), channel_id=1, source_target_pairs={{0,48},{16,0},{32,16},{48,32},{1,49},{17,1},{33,17},{49,33},{2,50}... | collective-permute-start | bytes 196616 | tf_op jit(solution)/shard_map/ppermute | solution.py:34
  237.0 0.8 copy-start.7
Sparse Core Ops, SparseCore 0:
  36.7 54.2 all-gather.1
  151.7 43.9 reduce-scatter.1

commit v8 on v7

--- a/solution.py
+++ b/solution.py
@@ -57,14 +57,26 @@
     return centred * lax.rsqrt(spread + 1e-06)
 
 
-def project_kernel(pos_ref, mine_ref, other_ref, w_ref, out_ref, stat_ref):
-    own = w_ref.shape[1]
+def fetch(copies):
+    for copy in copies:
+        copy.start()
+    return copies
+
+
+def project_kernel(pos_ref, mine_hbm, other_hbm, w_hbm, out_ref, stat_ref, x_ref, w_ref, x_sem, w_sem):
+    count, own = x_ref.shape[0], x_ref.shape[2]
     core = lax.rem(pos_ref[0], 2)
+    order = [(mine_hbm, q, 2 * q + core) for q in range(count // 2)]
+    order += [(other_hbm, q, 2 * q + 1 - core) for q in range(count // 2)]
+    x_copies, w_copies = [], []
+    for j, (source, q, b) in enumerate(order):
+        x_copies += fetch([pltpu.make_async_copy(source.at[q], x_ref.at[j], x_sem.at[j])])
+        w_copies += fetch([pltpu.make_async_copy(w_hbm.at[b], w_ref.at[j], w_sem.at[j])])
     total = jnp.zeros(out_ref.shape, F32)
-    for source, side in ((mine_ref, core), (other_ref, 1 - core)):
-        for q in range(source.shape[0]):
-            start = pl.multiple_of((2 * q + side) * own, own)
-            total += jnp.dot(source[q], w_ref[pl.ds(start, own), :], preferred_element_type=F32)
+    for j in range(count):
+        x_copies[j].wait()
+        w_copies[j].wait()
+        total += jnp.dot(x_ref[j], w_ref[j], preferred_element_type=F32)
     mean = jnp.sum(total, axis=1, keepdims=True) * (1.0 / own)
     centred = total - mean
     out_ref[...] = centred.astype(BF)
@@ -74,29 +86,30 @@
 
 
 def feature_kernel(
-    pos_ref, mine_ref, other_ref, adj_ref, rstd_ref, gain_ref, prev_ref, rot_ref, sign_ref,
-    f_ref, basis_ref, sums_ref,
+    pos_ref, mine_hbm, other_hbm, adj_ref, rstd_ref, gain_ref, prev_ref, rot_hbm, sign_ref,
+    out_ref, basis_ref, sums_ref, f_ref, x_ref, rot_ref, x_sem, rot_sem,
 ):
     blocks, rows, own = f_ref.shape
     core = lax.rem(pos_ref[0], 2)
+    order = [(mine_hbm, q, 2 * q + core) for q in range(blocks // 2)]
+    order += [(other_hbm, q, 2 * q + 1 - core) for q in range(blocks // 2)]
+    x_copies, rot_copies = [], []
+    for j, (source, q, b) in enumerate(order):
+        x_copies += fetch([pltpu.make_async_copy(source.at[q], x_ref.at[j], x_sem.at[j])])
+        rot_copies += fetch([pltpu.make_async_copy(rot_hbm.at[b], rot_ref.at[j], rot_sem.at[j])])
     rstd = rstd_ref[...]
     total = jnp.zeros((rows, own), F32)
-    for j in range(blocks):
-        source, q, side = (mine_ref, j, core) if j < blocks // 2 else (other_ref, j - blocks // 2, 1 - core)
-        b = 2 * q + side
-        value = (source[q, :rows, :].astype(F32) + adj_ref[:, j : j + 1]) * rstd * gain_ref[b]
+    for j, (_, _, b) in enumerate(order):
+        x_copies[j].wait()
+        value = (x_ref[j, :rows, :].astype(F32) + adj_ref[:, j : j + 1]) * rstd * gain_ref[b]
         feature = value.astype(BF)
         f_ref[b] = feature
         feature = feature.astype(F32)
         sums_ref[b] = jnp.sum(feature, axis=0, keepdims=True)
         shifted = (feature - prev_ref[b]).astype(BF)
-        turn = rot_ref[pl.ds(pl.multiple_of(b * own, own), own), :]
-        total += jnp.dot(shifted, turn, preferred_element_type=F32)
+        rot_copies[j].wait()
+        total += jnp.dot(shifted, rot_ref[j], preferred_element_type=F32)
     basis_ref[...] = total.astype(BF) * sign_ref[...]
-
-
-def moment_kernel(pos_ref, f_ref, sums_ref, out_ref):
-    blocks, rows, own = f_ref.shape
     part = out_ref.shape[2]
     own_t = f_ref[pos_ref[0]].astype(F32).T
     own_col = jnp.sum(own_t, axis=1, keepdims=True)
@@ -207,7 +220,7 @@
     near = broadcast_gather(strip, "yh")
     proj = lax.all_gather(near.reshape(-1, own), "z", axis=0, tiled=True)
     teacher, _ = lax.optimization_barrier((teacher_in, near))
-    teacher = lax.cond(image_ids[0] >= 0, tensor_gather, tensor_gather_twice, teacher)
+    teacher = lax.cond(prev_scale[0] > 0.0, tensor_gather, tensor_gather_twice, teacher)
 
     normed = layer_norm(student_in.astype(F32)).astype(BF)
     predicted = jnp.dot(normed, head_weight, preferred_element_type=F32)
@@ -220,16 +233,22 @@
     token_weight = 1.0 / token_counts
 
     smem, vmem = pl.BlockSpec(memory_space=pltpu.SMEM), pl.BlockSpec(memory_space=pltpu.VMEM)
+    anywhere = pl.BlockSpec(memory_space=pl.ANY)
     position = tpos.reshape(1)
-    proj, normed, predicted, token_weight = lax.optimization_barrier((proj, normed, predicted, token_weight))
     raw, stat = pl.pallas_call(
         project_kernel,
         out_shape=(jax.ShapeDtypeStruct((rows, own), BF), jax.ShapeDtypeStruct((rows, 2), F32)),
-        in_specs=[smem, vmem, vmem, vmem],
+        in_specs=[smem] + [anywhere] * 3,
         out_specs=(vmem, vmem),
-        compiler_params=pltpu.CompilerParams(vmem_limit_bytes=16 << 20),
+        scratch_shapes=[
+            pltpu.VMEM((blocks, rows, own), BF),
+            pltpu.VMEM((blocks, own, own), BF),
+            pltpu.SemaphoreType.DMA((blocks,)),
+            pltpu.SemaphoreType.DMA((blocks,)),
+        ],
+        compiler_params=pltpu.CompilerParams(vmem_limit_bytes=52 << 20),
         cost_estimate=pl.CostEstimate(flops=2 * rows * width * own, bytes_accessed=8 << 20, transcendentals=0),
-    )(position, *teacher, proj)
+    )(position, *teacher, proj.reshape(blocks, own, own))
     pieces = jnp.stack(split3(stat.T)).reshape(6 * rows // own, own).astype(BF)
     spare = -pieces.shape[0] % 16
     packed = jnp.concatenate([raw, pieces, jnp.zeros((spare, own), BF)])
@@ -254,17 +273,24 @@
     index_col = lax.broadcasted_iota(jnp.int32, (own, own), 1)
     table = parity_sign(index_row & index_col).astype(BF)
 
-    features, basis, sums = pl.pallas_call(
+    moment, basis, sums = pl.pallas_call(
         feature_kernel,
         out_shape=(
-            jax.ShapeDtypeStruct((blocks, rows, own), BF),
+            jax.ShapeDtypeStruct((chunks, own, part), BF),
             jax.ShapeDtypeStruct((rows, own), BF),
             jax.ShapeDtypeStruct((blocks, 1, own), F32),
         ),
-        in_specs=[smem] + [vmem] * 8,
+        in_specs=[smem, anywhere, anywhere, vmem, vmem, vmem, vmem, anywhere, vmem],
         out_specs=(vmem,) * 3,
-        compiler_params=pltpu.CompilerParams(vmem_limit_bytes=16 << 20),
-        cost_estimate=pl.CostEstimate(flops=2 * rows * width * own, bytes_accessed=12 << 20, transcendentals=0),
+        scratch_shapes=[
+            pltpu.VMEM((blocks, rows, own), BF),
+            pltpu.VMEM((blocks,) + packed.shape, BF),
+            pltpu.VMEM((blocks, own, own), BF),
+            pltpu.SemaphoreType.DMA((blocks,)),
+            pltpu.SemaphoreType.DMA((blocks,)),
+        ],
+        compiler_params=pltpu.CompilerParams(vmem_limit_bytes=52 << 20),
+        cost_estimate=pl.CostEstimate(flops=4 * rows * width * own, bytes_accessed=12 << 20, transcendentals=0),
     )(
         position,
         mine,
@@ -273,18 +299,10 @@
         rstd[:, None],
         final_gain.reshape(blocks, 1, own),
         mean_prev.reshape(blocks, 1, own),
-        rotation,
+        rotation.reshape(blocks, own, own),
         (2 * signs - 1).astype(BF)[None, :],
     )
     lines = lax.all_to_all(basis.reshape(blocks, rows // blocks, own), TN, 0, 0, tiled=True)
-    moment = pl.pallas_call(
-        moment_kernel,
-        out_shape=jax.ShapeDtypeStruct((chunks, own, part), BF),
-        in_specs=[smem, vmem, vmem],
-        out_specs=vmem,
-        compiler_params=pltpu.CompilerParams(vmem_limit_bytes=12 << 20),
-        cost_estimate=pl.CostEstimate(flops=2 * rows * width * own, bytes_accessed=6 << 20, transcendentals=0),
-    )(position, features, sums)
     within = lax.psum_scatter(moment, "z", scatter_dimension=0, tiled=True)
 
     lines = pl.pallas_call(

time: 250 us -> 246 us (0.984)
  local copies, waits for them, and re-layouts: 11.7 us -> 6.76 us
  Pallas kernels: 15.5 us -> 20 us
    unnamed x24 -> x20, local copies, waits for them, and re-layouts: 5.65 us -> 1.7 us
    pallas_call x2 -> x1, Pallas kernels: 7.25 us -> 11 us  [body(): pl.pallas_call(feature_kernel, out_shape=(jax.ShapeDtypeStruct((chunks, o...]
  transfers between devices with their start and end apart: 13 -> 13, of which waited for: 7 -> 8; matrix products, arithmetic and copies ran while one was open for 4% -> 3% of each run, Pallas kernels for 2% -> 2%
where the time goes in v8:
time: 246 us; the launch traced here: 245 us
  blocking collectives  93.4 us (38%)
  waiting for transfers between devices  52.6 us (21%)
  starting transfers between devices  49 us (20%)
  Pallas kernels  20 us (8%)
  between operations  15.3 us (6%)
  local copies, waits for them, and re-layouts  6.76 us (3%)
  other arithmetic  5.04 us (2%)
    all_to_all x3, blocking collectives, broadcast_gather(): lax.all_to_all(jnp.broadcast_to(block[None], (count,) + block.shape), axe...  93.4 us
    all_to_all x1, waiting for transfers between devices, body(): taken = lax.all_to_all(sent, DP, 0, 0, tiled=True)  23.4 us
    ppermute x3, starting transfers between devices, shift(): lax.ppermute(block, axis, [(i, (i + step) % count) for i in range(count)])  15.6 us
    pallas_call x1, Pallas kernels, body(): pl.pallas_call(feature_kernel, out_shape=(jax.ShapeDtypeStruct((chunks, o...  11 us
    ppermute x2, starting transfers between devices, body(): got.append(lax.ppermute(send, DP + TN, route))  7.86 us
    ppermute x2, waiting for transfers between devices, tensor_gather(): return (mine, lax.ppermute(mine, 'c', [(0, 1), (1, 0)]))  7.19 us
    all_to_all x1, starting transfers between devices, body(): taken = lax.all_to_all(sent, DP, 0, 0, tiled=True)  6.57 us
    all_to_all x1, waiting for transfers between devices, broadcast_gather(): lax.all_to_all(jnp.broadcast_to(block[None], (count,) + block.shape), axe...  6.11 us
  transfers between devices with their start and end apart: 13, of which 8 were waited for; matrix products, arithmetic and copies ran while one was open for 3% of the time, Pallas kernels for 2%

profile of v8, /device:TPU:8, one launch (start us, length us, event | category | flops | bytes accessed | tf_op | source)
XLA Modules:
  0.0 244.5 jit_solution(719614613604003135)
XLA Ops:
  8.1 4.2 %collective-permute-start.2 = (bf16[128,128]{1,0:T(8,128)(2,1)S(1)}, bf16[128,128]{1,0:T(8,128)(2,1)S(1)}, u32[]{:S(2)}, u32[]{:S(2)}) collective-permute-start(bf16[128,128]{1,0:T(8,128)(2,1)S(1)} %get-tuple-element.38), channel_id=1, source_target_pairs={{0,0},{1,32},{2,64},{3,96},{4,128},{5,160},{6,192},{7,224},{8,256}... | collective-permute-start | bytes 98312 | tf_op jit(solution)/shard_map/ppermute | solution.py:216
  12.3 3.7 %collective-permute-start.3 = (bf16[128,128]{1,0:T(8,128)(2,1)S(1)}, bf16[128,128]{1,0:T(8,128)(2,1)S(1)}, u32[]{:S(2)}, u32[]{:S(2)}) collective-permute-start(bf16[128,128]{1,0:T(8,128)(2,1)S(1)} %get-tuple-element.39), channel_id=1, source_target_pairs={{0,16},{1,48},{2,80},{3,112},{4,144},{5,176},{6,208},{7,240},{8,27... | collective-permute-start | bytes 98312 | tf_op jit(solution)/shard_map/ppermute | solution.py:216
  16.0 3.6 %collective-permute-done.3 = bf16[128,128]{1,0:T(8,128)(2,1)S(1)} collective-permute-done((bf16[128,128]{1,0:T(8,128)(2,1)S(1)}, bf16[128,128]{1,0:T(8,128)(2,1)S(1)}, u32[]{:S(2)}, u32[]{:S(2)}) %collective-permute-start.3) | collective-permute-done | bytes 32800 | tf_op jit(solution)/shard_map/ppermute | solution.py:216
  19.6 16.9 %all_to_all.44 = bf16[4,128,256]{2,1,0:T(8,128)(2,1)} all-to-all(bf16[4,128,256]{2,1,0:T(8,128)(2,1)S(1)} %broadcast_in_dim.36), channel_id=1, replica_groups=mesh['z'=8,'yh'=4,'x'=4,'yl'=2,'c'=2] {'yh'}, dimensions={0} | all-to-all | bytes 524288 | tf_op jit(solution)/shard_map/all_to_all | solution.py:29
  37.3 53.3 %conditional.1 = (bf16[8,512,256]{2,1,0:T(8,128)(2,1)}, bf16[8,512,256]{2,1,0:T(8,128)(2,1)}) conditional(s32[]{:T(128)} %bitcast.1, bf16[512,256]{1,0:T(8,128)(2,1)} %param.12, bf16[512,256]{1,0:T(8,128)(2,1)} %param.12), branch_computations={%region_0.1_spmd, %region_1.2_spmd} | conditional | bytes 17301620 | solution.py:223
  38.4 45.8 %all_to_all.43 = bf16[8,512,256]{2,1,0:T(8,128)(2,1)} all-to-all(bf16[8,512,256]{2,1,0:T(8,128)(2,1)S(1)} %broadcast_in_dim.24), channel_id=1, replica_groups=mesh['z'=8,'yh'=4,'x'=4,'yl'=2,'c'=2] {'x','yl'}, dimensions={0} | all-to-all | bytes 4194304 | tf_op jit(solution)/shard_map/cond/branch_1_fun/all_to_all | solution.py:29
  84.2 2.2 collective-permute-start.1
  86.4 4.2 %collective-permute-done.1 = bf16[8,512,256]{2,1,0:T(8,128)(2,1)} collective-permute-done((bf16[8,512,256]{2,1,0:T(8,128)(2,1)}, bf16[8,512,256]{2,1,0:T(8,128)(2,1)}, u32[]{:S(2)}, u32[]{:S(2)}) %collective-permute-start.1) | collective-permute-done | bytes 2097184 | tf_op jit(solution)/shard_map/cond/branch_1_fun/ppermute | solution.py:39
  91.0 4.5 %shard_map.129 = (bf16[512,256]{1,0:T(8,128)(2,1)S(1)}, f32[512,2]{1,0:T(8,128)S(1)}) custom-call(s32[1]{0:T(128)} %bitcast.pos_ref, bf16[8,512,256]{2,1,0:T(8,128)(2,1)} %get-tuple-element.15.mine_hbm, bf16[8,512,256]{2,1,0:T(8,128)(2,1)} %get-tuple-element.16.other_hbm, bf16[16,256,256]{2,1,0:T(8,128)(2,1)} %bitcast.80), custom_call_target="tpu_custom_call" | custom-call | flops 1073741824 | bytes 8388608 | tf_op jit(solution)/shard_map/pallas_call | solution.py:238
  96.3 30.7 %all_to_all.45.mine_hbm = bf16[8,528,256]{2,1,0:T(8,128)(2,1)S(1)} all-to-all(bf16[8,528,256]{2,1,0:T(8,128)(2,1)S(1)} %broadcast_in_dim.38), channel_id=1, replica_groups=mesh['z'=8,'yh'=4,'x'=4,'yl'=2,'c'=2] {'x','yl'}, dimensions={0} | all-to-all | bytes 4325376 | tf_op jit(solution)/shard_map/all_to_all | solution.py:29
  127.0 2.2 collective-permute-start.4
  130.4 3.0 %collective-permute-done.4.other_hbm = bf16[8,528,256]{2,1,0:T(8,128)(2,1)} collective-permute-done((bf16[8,528,256]{2,1,0:T(8,128)(2,1)S(1)}, bf16[8,528,256]{2,1,0:T(8,128)(2,1)}, u32[]{:S(2)}, u32[]{:S(2)}) %collective-permute-start.4) | collective-permute-done | bytes 2162720 | tf_op jit(solution)/shard_map/ppermute | solution.py:39
  135.3 11.0 %shard_map.130 = (bf16[32,256,128]{2,1,0:T(8,128)(2,1)}, bf16[512,256]{1,0:T(8,128)(2,1)}, f32[16,1,256]{2,1,0:T(1,128)S(1)}) custom-call(s32[1]{0:T(128)} %bitcast.pos_ref, bf16[8,528,256]{2,1,0:T(8,128)(2,1)} %copy-done.4, bf16[8,528,256]{2,1,0:T(8,128)(2,1)} %collective-permute-done.4.other_hbm, f32[512,16]{1,0:T(8,128)S(1)} %bitcast.77, ...), custom_call_target="tpu_custom_call" | custom-call | flops 2147483648 | bytes 12582912 | tf_op jit(solution)/shard_map/pallas_call | solution.py:276
  147.7 4.6 %all-to-all-start.5 = ((bf16[16,32,256]{2,1,0:T(8,128)(2,1)}), bf16[16,32,256]{2,1,0:T(8,128)(2,1)S(1)}, u32[]{:S(2)}, u32[]{:S(2)}) async-start(bf16[16,32,256]{2,1,0:T(8,128)(2,1)} %bitcast.24), calls=%async_computation.6 | async-start | bytes 524288 | tf_op jit(solution)/shard_map/all_to_all | solution.py:305
  153.3 5.9 %all-to-all-done.5.basis_ref = bf16[16,32,256]{2,1,0:T(8,128)(2,1)S(1)} async-done(((bf16[16,32,256]{2,1,0:T(8,128)(2,1)}), bf16[16,32,256]{2,1,0:T(8,128)(2,1)S(1)}, u32[]{:S(2)}, u32[]{:S(2)}) %all-to-all-start.5) | async-done | bytes 262176 | tf_op jit(solution)/shard_map/all_to_all | solution.py:305
  160.2 4.7 %all-to-all-start.6 = ((bf16[16,32,256]{2,1,0:T(8,128)(2,1)}), bf16[16,32,256]{2,1,0:T(8,128)(2,1)S(1)}, u32[]{:S(2)}, u32[]{:S(2)}) async-start(bf16[16,32,256]{2,1,0:T(8,128)(2,1)} %shard_map.131), calls=%async_computation.7 | async-start | bytes 524288 | tf_op jit(solution)/shard_map/all_to_all | solution.py:315
  165.7 6.1 %all-to-all-done.6 = bf16[16,32,256]{2,1,0:T(8,128)(2,1)S(1)} async-done(((bf16[16,32,256]{2,1,0:T(8,128)(2,1)}), bf16[16,32,256]{2,1,0:T(8,128)(2,1)S(1)}, u32[]{:S(2)}, u32[]{:S(2)}) %all-to-all-start.6) | async-done | bytes 262176 | tf_op jit(solution)/shard_map/all_to_all | solution.py:315
  173.2 6.6 %all-to-all-start.7 = ((bf16[32,80,128]{2,1,0:T(8,128)(2,1)}), bf16[32,80,128]{2,1,0:T(8,128)(2,1)S(1)}, u32[]{:S(2)}, u32[]{:S(2)}) async-start(bf16[32,80,128]{2,1,0:T(8,128)(2,1)} %shard_map.132), calls=%async_computation.8 | async-start | bytes 1310720 | tf_op jit(solution)/shard_map/all_to_all | solution.py:324
  179.9 23.4 %all-to-all-done.7 = bf16[32,80,128]{2,1,0:T(8,128)(2,1)S(1)} async-done(((bf16[32,80,128]{2,1,0:T(8,128)(2,1)}), bf16[32,80,128]{2,1,0:T(8,128)(2,1)S(1)}, u32[]{:S(2)}, u32[]{:S(2)}) %all-to-all-start.7) | async-done | bytes 655392 | tf_op jit(solution)/shard_map/all_to_all | solution.py:324
  204.2 5.2 %all-to-all-start.8 = ((bf16[32,64,128]{2,1,0:T(8,128)(2,1)}), bf16[32,64,128]{2,1,0:T(8,128)(2,1)S(1)}, u32[]{:S(2)}, u32[]{:S(2)}) async-start(bf16[32,64,128]{2,1,0:T(8,128)(2,1)} %broadcast_in_dim.46), calls=%async_computation.9 | async-start | bytes 1048576 | tf_op jit(solution)/shard_map/all_to_all | solution.py:29
  211.1 4.6 %collective-permute-start.5 = (bf16[256,128]{1,0:T(8,128)(2,1)S(1)}, bf16[256,128]{1,0:T(8,128)(2,1)S(1)}, u32[]{:S(2)}, u32[]{:S(2)}) collective-permute-start(bf16[256,128]{1,0:T(8,128)(2,1)S(1)} %get-tuple-element.28), channel_id=1, source_target_pairs={{0,16},{16,32},{32,48},{48,0},{1,17},{17,33},{33,49},{49,1},{2,18}... | collective-permute-start | bytes 196616 | tf_op jit(solution)/shard_map/ppermute | solution.py:34
  215.7 5.5 %collective-permute-start.6 = (bf16[256,128]{1,0:T(8,128)(2,1)S(1)}, bf16[256,128]{1,0:T(8,128)(2,1)S(1)}, u32[]{:S(2)}, u32[]{:S(2)}) collective-permute-start(bf16[256,128]{1,0:T(8,128)(2,1)S(1)} %get-tuple-element.30), channel_id=1, source_target_pairs={{0,32},{16,48},{32,0},{48,16},{1,33},{17,49},{33,1},{49,17},{2,34}... | collective-permute-start | bytes 196616 | tf_op jit(solution)/shard_map/ppermute | solution.py:34
  221.2 5.5 %collective-permute-start.7 = (bf16[256,128]{1,0:T(8,128)(2,1)S(1)}, bf16[256,128]{1,0:T(8,128)(2,1)S(1)}, u32[]{:S(2)}, u32[]{:S(2)}) collective-permute-start(bf16[256,128]{1,0:T(8,128)(2,1)S(1)} %get-tuple-element.29), channel_id=1, source_target_pairs={{0,48},{16,0},{32,16},{48,32},{1,49},{17,1},{33,17},{49,33},{2,50}... | collective-permute-start | bytes 196616 | tf_op jit(solution)/shard_map/ppermute | solution.py:34
  226.8 6.1 %all-to-all-done.8.in_ref = bf16[32,64,128]{2,1,0:T(8,128)(2,1)S(1)} async-done(((bf16[32,64,128]{2,1,0:T(8,128)(2,1)}), bf16[32,64,128]{2,1,0:T(8,128)(2,1)S(1)}, u32[]{:S(2)}, u32[]{:S(2)}) %all-to-all-start.8) | async-done | bytes 524320 | tf_op jit(solution)/shard_map/all_to_all | solution.py:29
  (95 shorter events, 19.2 us)
Async XLA Ops:
  7.2 158.0 %copy-start = (bf16[1024,256]{1,0:T(8,128)(2,1)S(1)}, bf16[1024,256]{1,0:T(8,128)(2,1)}, u32[]{:S(2)}) copy-start(bf16[1024,256]{1,0:T(8,128)(2,1)} %param.20) | copy-start | bytes 1572868
  7.2 83.9 %all-gather.2.cloned.1.call-start = ((), (), s32[]{:S(2)}) async-start(), calls=%async_computation.10 | async-start | bytes 2359296 | tf_op jit(solution)/shard_map/all_gather | solution.py:221
  8.1 7.9 %collective-permute-start.2 = (bf16[128,128]{1,0:T(8,128)(2,1)S(1)}, bf16[128,128]{1,0:T(8,128)(2,1)S(1)}, u32[]{:S(2)}, u32[]{:S(2)}) collective-permute-start(bf16[128,128]{1,0:T(8,128)(2,1)S(1)} %get-tuple-element.38), channel_id=1, source_target_pairs={{0,0},{1,32},{2,64},{3,96},{4,128},{5,160},{6,192},{7,224},{8,256}... | collective-permute-start | bytes 98312 | tf_op jit(solution)/shard_map/ppermute | solution.py:216
  12.3 7.3 %collective-permute-start.3 = (bf16[128,128]{1,0:T(8,128)(2,1)S(1)}, bf16[128,128]{1,0:T(8,128)(2,1)S(1)}, u32[]{:S(2)}, u32[]{:S(2)}) collective-permute-start(bf16[128,128]{1,0:T(8,128)(2,1)S(1)} %get-tuple-element.39), channel_id=1, source_target_pairs={{0,16},{1,48},{2,80},{3,112},{4,144},{5,176},{6,208},{7,240},{8,27... | collective-permute-start | bytes 98312 | tf_op jit(solution)/shard_map/ppermute | solution.py:216
  36.5 173.7 %reduce-scatter.2.cloned.1.call-start = ((), (), s32[]{:S(2)}) async-start(), calls=%async_computation.11 | async-start | bytes 2359296 | tf_op jit(solution)/shard_map/reduce_scatter | solution.py:306
  84.2 6.4 %collective-permute-start.1 = (bf16[8,512,256]{2,1,0:T(8,128)(2,1)}, bf16[8,512,256]{2,1,0:T(8,128)(2,1)}, u32[]{:S(2)}, u32[]{:S(2)}) collective-permute-start(bf16[8,512,256]{2,1,0:T(8,128)(2,1)} %all_to_all.43), channel_id=1, source_target_pairs={{0,1},{1,0},{2,3},{3,2},{4,5},{5,4},{6,7},{7,6},{8,9},{9,8},{10,11... | collective-permute-start | bytes 6291464 | tf_op jit(solution)/shard_map/cond/branch_1_fun/ppermute | solution.py:39
  96.3 33.0 %copy-start.9 = (s32[256]{0:T(256)S(1)}, s32[256]{0:T(256)}, u32[]{:S(2)}) copy-start(s32[256]{0:T(256)} %param.17) | copy-start | bytes 3076
  96.3 33.0 %copy-start.7 = (s32[16384]{0:T(1024)S(1)}, s32[16384]{0:T(1024)}, u32[]{:S(2)}) copy-start(s32[16384]{0:T(1024)} %param.21) | copy-start | bytes 196612
  127.0 8.3 %copy-start.4 = (bf16[8,528,256]{2,1,0:T(8,128)(2,1)}, bf16[8,528,256]{2,1,0:T(8,128)(2,1)S(1)}, u32[]{:S(2)}) copy-start(bf16[8,528,256]{2,1,0:T(8,128)(2,1)S(1)} %all_to_all.45.mine_hbm) | copy-start | bytes 6488068
  127.0 8.3 %copy-start.1 = (f32[4096]{0:T(1024)S(1)}, f32[4096]{0:T(1024)}, u32[]{:S(2)}) copy-start(f32[4096]{0:T(1024)} %param.14) | copy-start | bytes 49156
  127.0 8.3 %copy-start.2 = (f32[4096]{0:T(1024)S(1)}, f32[4096]{0:T(1024)}, u32[]{:S(2)}) copy-start(f32[4096]{0:T(1024)} %param.15) | copy-start | bytes 49156
  127.0 6.4 %collective-permute-start.4 = (bf16[8,528,256]{2,1,0:T(8,128)(2,1)S(1)}, bf16[8,528,256]{2,1,0:T(8,128)(2,1)}, u32[]{:S(2)}, u32[]{:S(2)}) collective-permute-start(bf16[8,528,256]{2,1,0:T(8,128)(2,1)S(1)} %all_to_all.45.mine_hbm), channel_id=1, source_target_pairs={{0,1},{1,0},{2,3},{3,2},{4,5},{5,4},{6,7},{7,6},{8,9},{9,8},{10,11... | collective-permute-start | bytes 6488072 | tf_op jit(solution)/shard_map/ppermute | solution.py:39
  146.3 1.2 copy-start.3
  147.7 11.4 %all-to-all-start.5 = ((bf16[16,32,256]{2,1,0:T(8,128)(2,1)}), bf16[16,32,256]{2,1,0:T(8,128)(2,1)S(1)}, u32[]{:S(2)}, u32[]{:S(2)}) async-start(bf16[16,32,256]{2,1,0:T(8,128)(2,1)} %bitcast.24), calls=%async_computation.6 | async-start | bytes 524288 | tf_op jit(solution)/shard_map/all_to_all | solution.py:305
  160.2 11.6 %all-to-all-start.6 = ((bf16[16,32,256]{2,1,0:T(8,128)(2,1)}), bf16[16,32,256]{2,1,0:T(8,128)(2,1)S(1)}, u32[]{:S(2)}, u32[]{:S(2)}) async-start(bf16[16,32,256]{2,1,0:T(8,128)(2,1)} %shard_map.131), calls=%async_computation.7 | async-start | bytes 524288 | tf_op jit(solution)/shard_map/all_to_all | solution.py:315
  173.2 30.0 %all-to-all-start.7 = ((bf16[32,80,128]{2,1,0:T(8,128)(2,1)}), bf16[32,80,128]{2,1,0:T(8,128)(2,1)S(1)}, u32[]{:S(2)}, u32[]{:S(2)}) async-start(bf16[32,80,128]{2,1,0:T(8,128)(2,1)} %shard_map.132), calls=%async_computation.8 | async-start | bytes 1310720 | tf_op jit(solution)/shard_map/all_to_all | solution.py:324
  204.2 28.6 %all-to-all-start.8 = ((bf16[32,64,128]{2,1,0:T(8,128)(2,1)}), bf16[32,64,128]{2,1,0:T(8,128)(2,1)S(1)}, u32[]{:S(2)}, u32[]{:S(2)}) async-start(bf16[32,64,128]{2,1,0:T(8,128)(2,1)} %broadcast_in_dim.46), calls=%async_computation.9 | async-start | bytes 1048576 | tf_op jit(solution)/shard_map/all_to_all | solution.py:29
  209.6 28.0 %copy-start.8 = (f32[256]{0:T(256)}, f32[256]{0:T(256)S(1)}, u32[]{:S(2)}) copy-start(f32[256]{0:T(256)S(1)} %multiply_bitcast_fusion.2) | copy-start | bytes 3076
  211.1 24.6 %collective-permute-start.5 = (bf16[256,128]{1,0:T(8,128)(2,1)S(1)}, bf16[256,128]{1,0:T(8,128)(2,1)S(1)}, u32[]{:S(2)}, u32[]{:S(2)}) collective-permute-start(bf16[256,128]{1,0:T(8,128)(2,1)S(1)} %get-tuple-element.28), channel_id=1, source_target_pairs={{0,16},{16,32},{32,48},{48,0},{1,17},{17,33},{33,49},{49,1},{2,18}... | collective-permute-start | bytes 196616 | tf_op jit(solution)/shard_map/ppermute | solution.py:34
  215.7 20.0 %collective-permute-start.6 = (bf16[256,128]{1,0:T(8,128)(2,1)S(1)}, bf16[256,128]{1,0:T(8,128)(2,1)S(1)}, u32[]{:S(2)}, u32[]{:S(2)}) collective-permute-start(bf16[256,128]{1,0:T(8,128)(2,1)S(1)} %get-tuple-element.30), channel_id=1, source_target_pairs={{0,32},{16,48},{32,0},{48,16},{1,33},{17,49},{33,1},{49,17},{2,34}... | collective-permute-start | bytes 196616 | tf_op jit(solution)/shard_map/ppermute | solution.py:34
  221.2 14.5 %collective-permute-start.7 = (bf16[256,128]{1,0:T(8,128)(2,1)S(1)}, bf16[256,128]{1,0:T(8,128)(2,1)S(1)}, u32[]{:S(2)}, u32[]{:S(2)}) collective-permute-start(bf16[256,128]{1,0:T(8,128)(2,1)S(1)} %get-tuple-element.29), channel_id=1, source_target_pairs={{0,48},{16,0},{32,16},{48,32},{1,49},{17,1},{33,17},{49,33},{2,50}... | collective-permute-start | bytes 196616 | tf_op jit(solution)/shard_map/ppermute | solution.py:34
  232.9 0.8 copy-start.5
Sparse Core Ops, SparseCore 0:
  36.6 54.3 all-gather.1
  146.5 44.0 reduce-scatter.1

commit v9 on v7

--- a/solution.py
+++ b/solution.py
@@ -57,14 +57,26 @@
     return centred * lax.rsqrt(spread + 1e-06)
 
 
-def project_kernel(pos_ref, mine_ref, other_ref, w_ref, out_ref, stat_ref):
-    own = w_ref.shape[1]
+def fetch(copies):
+    for copy in copies:
+        copy.start()
+    return copies
+
+
+def project_kernel(pos_ref, mine_hbm, other_hbm, w_hbm, out_ref, stat_ref, x_ref, w_ref, x_sem, w_sem):
+    count, own = x_ref.shape[0], x_ref.shape[2]
     core = lax.rem(pos_ref[0], 2)
+    order = [(mine_hbm, q, 2 * q + core) for q in range(count // 2)]
+    order += [(other_hbm, q, 2 * q + 1 - core) for q in range(count // 2)]
+    x_copies, w_copies = [], []
+    for j, (source, q, b) in enumerate(order):
+        x_copies += fetch([pltpu.make_async_copy(source.at[q], x_ref.at[j], x_sem.at[j])])
+        w_copies += fetch([pltpu.make_async_copy(w_hbm.at[b], w_ref.at[j], w_sem.at[j])])
     total = jnp.zeros(out_ref.shape, F32)
-    for source, side in ((mine_ref, core), (other_ref, 1 - core)):
-        for q in range(source.shape[0]):
-            start = pl.multiple_of((2 * q + side) * own, own)
-            total += jnp.dot(source[q], w_ref[pl.ds(start, own), :], preferred_element_type=F32)
+    for j in range(count):
+        x_copies[j].wait()
+        w_copies[j].wait()
+        total += jnp.dot(x_ref[j], w_ref[j], preferred_element_type=F32)
     mean = jnp.sum(total, axis=1, keepdims=True) * (1.0 / own)
     centred = total - mean
     out_ref[...] = centred.astype(BF)
@@ -207,7 +219,8 @@
     near = broadcast_gather(strip, "yh")
     proj = lax.all_gather(near.reshape(-1, own), "z", axis=0, tiled=True)
     teacher, _ = lax.optimization_barrier((teacher_in, near))
-    teacher = lax.cond(image_ids[0] >= 0, tensor_gather, tensor_gather_twice, teacher)
+    positive = prev_scale[0] > 0.0
+    teacher = lax.cond(positive, tensor_gather, tensor_gather_twice, teacher)
 
     normed = layer_norm(student_in.astype(F32)).astype(BF)
     predicted = jnp.dot(normed, head_weight, preferred_element_type=F32)
@@ -220,16 +233,22 @@
     token_weight = 1.0 / token_counts
 
     smem, vmem = pl.BlockSpec(memory_space=pltpu.SMEM), pl.BlockSpec(memory_space=pltpu.VMEM)
+    anywhere = pl.BlockSpec(memory_space=pl.ANY)
     position = tpos.reshape(1)
-    proj, normed, predicted, token_weight = lax.optimization_barrier((proj, normed, predicted, token_weight))
     raw, stat = pl.pallas_call(
         project_kernel,
         out_shape=(jax.ShapeDtypeStruct((rows, own), BF), jax.ShapeDtypeStruct((rows, 2), F32)),
-        in_specs=[smem, vmem, vmem, vmem],
+        in_specs=[smem] + [anywhere] * 3,
         out_specs=(vmem, vmem),
-        compiler_params=pltpu.CompilerParams(vmem_limit_bytes=16 << 20),
+        scratch_shapes=[
+            pltpu.VMEM((blocks, rows, own), BF),
+            pltpu.VMEM((blocks, own, own), BF),
+            pltpu.SemaphoreType.DMA((blocks,)),
+            pltpu.SemaphoreType.DMA((blocks,)),
+        ],
+        compiler_params=pltpu.CompilerParams(vmem_limit_bytes=52 << 20),
         cost_estimate=pl.CostEstimate(flops=2 * rows * width * own, bytes_accessed=8 << 20, transcendentals=0),
-    )(position, *teacher, proj)
+    )(position, *teacher, proj.reshape(blocks, own, own))
     pieces = jnp.stack(split3(stat.T)).reshape(6 * rows // own, own).astype(BF)
     spare = -pieces.shape[0] % 16
     packed = jnp.concatenate([raw, pieces, jnp.zeros((spare, own), BF)])
@@ -306,16 +325,19 @@
     taken = lax.all_to_all(sent, DP, 0, 0, tiled=True)
 
     grad_own = jnp.sum(taken[:, : 2 * depth, :].astype(F32), axis=0).astype(BF)
-    places, here = lax.axis_size("yh"), lax.axis_index("yh")
-    within_sum = within[here].astype(F32)
-    for k in range(1, places):
-        within_sum += shift(within[(here + k) % places], "yh", k).astype(F32)
+    within = lax.psum_scatter(within, "yh", scatter_dimension=0, tiled=True)
+    grads = lax.cond(
+        positive,
+        lambda block: broadcast_gather(block, DP),
+        lambda block: lax.all_gather(block, DP, axis=0, tiled=False),
+        grad_own,
+    )
     grad_head = pl.pallas_call(
         place_kernel,
         out_shape=jax.ShapeDtypeStruct((chunks * depth, own), F32),
         in_specs=[vmem],
         out_specs=vmem,
-    )(broadcast_gather(grad_own, DP))
+    )(grads)
 
     tail = taken[:, 2 * depth :, :].astype(F32)
     sums_t = tail[:, 0:6].reshape(chunks, 2, 3, part).sum(2).reshape(chunks, own)
@@ -328,7 +350,7 @@
     between = lax.dot_general(
         off_t, off_d, (((0,), (0,)), ((), ())), precision=lax.Precision.HIGHEST, preferred_element_type=F32
     )
-    new_cov = (within_sum + between * rows) / all_tokens
+    new_cov = (within.reshape(own, part).astype(F32) + between * rows) / all_tokens
     return (new_cov, new_mean, grad_head, loss / image_count)
 
 

time: 250 us -> 241 us (0.964)
  the two profiles are of different devices: /device:TPU:8 before, /device:TPU:18 now
where the time goes in v9:
time: 241 us; the launch traced here: 240 us
  blocking collectives  140 us (58%)
  waiting for transfers between devices  32.5 us (13%)
  starting transfers between devices  23.1 us (10%)
  Pallas kernels  15.1 us (6%)
  between operations  14.9 us (6%)
  other arithmetic  6.28 us (3%)
  local copies, waits for them, and re-layouts  5.9 us (2%)
    all_to_all x4, blocking collectives, broadcast_gather(): lax.all_to_all(jnp.broadcast_to(block[None], (count,) + block.shape), axe...  111 us
    all_to_all x1, blocking collectives, body(): taken = lax.all_to_all(sent, DP, 0, 0, tiled=True)  29.2 us
    ppermute x2, waiting for transfers between devices, tensor_gather(): return (mine, lax.ppermute(mine, 'c', [(0, 1), (1, 0)]))  8.61 us
    ppermute x2, starting transfers between devices, body(): got.append(lax.ppermute(send, DP + TN, route))  7.97 us
    ppermute x2, waiting for transfers between devices, body(): got.append(lax.ppermute(send, DP + TN, route))  7.46 us
    reduce_scatter x1, waiting for transfers between devices, body(): within = lax.psum_scatter(within, 'yh', scatter_dimension=0, tiled=True)  6.42 us
    all_to_all x1, starting transfers between devices, body(): target = lax.all_to_all(lines, TN, 0, 0, tiled=True).reshape(rows, own)  6.04 us
    pallas_call x1, Pallas kernels, body(): pl.pallas_call(feature_kernel, out_shape=(jax.ShapeDtypeStruct((blocks, r...  5.3 us
  transfers between devices with their start and end apart: 9, of which 7 were waited for; matrix products, arithmetic and copies ran while one was open for 3% of the time, Pallas kernels for 1%

profile of v9, /device:TPU:18, one launch (start us, length us, event | category | flops | bytes accessed | tf_op | source)
XLA Modules:
  0.0 240.0 jit_solution(1606432524097090028)
XLA Ops:
  8.1 6.0 %collective-permute-start.2 = (bf16[128,128]{1,0:T(8,128)(2,1)S(1)}, bf16[128,128]{1,0:T(8,128)(2,1)S(1)}, u32[]{:S(2)}, u32[]{:S(2)}) collective-permute-start(bf16[128,128]{1,0:T(8,128)(2,1)S(1)} %get-tuple-element.40), channel_id=1, source_target_pairs={{0,0},{1,32},{2,64},{3,96},{4,128},{5,160},{6,192},{7,224},{8,256}... | collective-permute-start | bytes 98312 | tf_op jit(solution)/shard_map/ppermute | solution.py:215
  14.2 1.9 collective-permute-start.3
  16.1 7.5 %collective-permute-done.3 = bf16[128,128]{1,0:T(8,128)(2,1)S(1)} collective-permute-done((bf16[128,128]{1,0:T(8,128)(2,1)S(1)}, bf16[128,128]{1,0:T(8,128)(2,1)S(1)}, u32[]{:S(2)}, u32[]{:S(2)}) %collective-permute-start.3) | collective-permute-done | bytes 32800 | tf_op jit(solution)/shard_map/ppermute | solution.py:215
  23.6 15.2 %all_to_all.44 = bf16[4,128,256]{2,1,0:T(8,128)(2,1)} all-to-all(bf16[4,128,256]{2,1,0:T(8,128)(2,1)S(1)} %broadcast_in_dim.36), channel_id=1, replica_groups=mesh['z'=8,'yh'=4,'x'=4,'yl'=2,'c'=2] {'yh'}, dimensions={0} | all-to-all | bytes 524288 | tf_op jit(solution)/shard_map/all_to_all | solution.py:29
  39.6 49.3 %conditional.2 = (bf16[8,512,256]{2,1,0:T(8,128)(2,1)}, bf16[8,512,256]{2,1,0:T(8,128)(2,1)}) conditional(s32[]{:T(128)} %bitcast.2, bf16[512,256]{1,0:T(8,128)(2,1)} %param.14, bf16[512,256]{1,0:T(8,128)(2,1)} %param.14), branch_computations={%region_0.1_spmd, %region_1.2_spmd} | conditional | bytes 17301620 | solution.py:223
  40.7 41.8 %all_to_all.42 = bf16[8,512,256]{2,1,0:T(8,128)(2,1)} all-to-all(bf16[8,512,256]{2,1,0:T(8,128)(2,1)S(1)} %broadcast_in_dim.24), channel_id=1, replica_groups=mesh['z'=8,'yh'=4,'x'=4,'yl'=2,'c'=2] {'x','yl'}, dimensions={0} | all-to-all | bytes 4194304 | tf_op jit(solution)/shard_map/cond/branch_1_fun/all_to_all | solution.py:29
  82.5 1.9 collective-permute-start.1
  84.5 4.5 %collective-permute-done.1 = bf16[8,512,256]{2,1,0:T(8,128)(2,1)} collective-permute-done((bf16[8,512,256]{2,1,0:T(8,128)(2,1)}, bf16[8,512,256]{2,1,0:T(8,128)(2,1)}, u32[]{:S(2)}, u32[]{:S(2)}) %collective-permute-start.1) | collective-permute-done | bytes 2097184 | tf_op jit(solution)/shard_map/cond/branch_1_fun/ppermute | solution.py:39
  88.9 2.1 all-gather.3.cloned.1.call-done
  91.0 4.5 %shard_map.129 = (bf16[512,256]{1,0:T(8,128)(2,1)S(1)}, f32[512,2]{1,0:T(8,128)S(1)}) custom-call(s32[1]{0:T(128)} %bitcast.1.pos_ref, bf16[8,512,256]{2,1,0:T(8,128)(2,1)} %get-tuple-element.20.mine_hbm, bf16[8,512,256]{2,1,0:T(8,128)(2,1)} %get-tuple-element.21.other_hbm, bf16[16,256,256]{2,1,0:T(8,128)(2,1)} %bitcast.72), custom_call_target="tpu_custom_call" | custom-call | flops 1073741824 | bytes 8388608 | tf_op jit(solution)/shard_map/pallas_call | solution.py:238
  96.3 29.3 %all_to_all.45.mine_ref = bf16[8,528,256]{2,1,0:T(8,128)(2,1)S(1)} all-to-all(bf16[8,528,256]{2,1,0:T(8,128)(2,1)S(1)} %broadcast_in_dim.38), channel_id=1, replica_groups=mesh['z'=8,'yh'=4,'x'=4,'yl'=2,'c'=2] {'x','yl'}, dimensions={0} | all-to-all | bytes 4325376 | tf_op jit(solution)/shard_map/all_to_all | solution.py:29
  125.5 2.0 collective-permute-start.4
  127.8 4.1 %collective-permute-done.4.other_ref = bf16[8,528,256]{2,1,0:T(8,128)(2,1)} collective-permute-done((bf16[8,528,256]{2,1,0:T(8,128)(2,1)S(1)}, bf16[8,528,256]{2,1,0:T(8,128)(2,1)}, u32[]{:S(2)}, u32[]{:S(2)}) %collective-permute-start.4) | collective-permute-done | bytes 2162720 | tf_op jit(solution)/shard_map/ppermute | solution.py:39
  135.4 5.3 %shard_map.130 = (bf16[16,512,256]{2,1,0:T(8,128)(2,1)S(1)}, bf16[512,256]{1,0:T(8,128)(2,1)}, f32[16,1,256]{2,1,0:T(1,128)S(1)}) custom-call(s32[1]{0:T(128)} %bitcast.1.pos_ref, bf16[8,528,256]{2,1,0:T(8,128)(2,1)S(1)} %all_to_all.45.mine_ref, bf16[8,528,256]{2,1,0:T(8,128)(2,1)} %collective-permute-done.4.other_ref, f32[512,16]{1,0:T(8,128)S(1)} %bitcast.69, ...), custom_call_target="tpu_custom_call" | custom-call | flops 1073741824 | bytes 12582912 | tf_op jit(solution)/shard_map/pallas_call | solution.py:276
  140.7 2.7 %shard_map.131 = bf16[32,256,128]{2,1,0:T(8,128)(2,1)} custom-call(s32[1]{0:T(128)} %bitcast.1.pos_ref, bf16[16,512,256]{2,1,0:T(8,128)(2,1)S(1)} %get-tuple-element.24.f_ref, f32[16,1,256]{2,1,0:T(1,128)S(1)} %get-tuple-element.25.sums_ref), custom_call_target="tpu_custom_call" | custom-call | flops 1073741824 | bytes 6291456 | tf_op jit(solution)/shard_map/pallas_call | solution.py:299
  145.9 4.8 %all-to-all-start.6 = ((bf16[16,32,256]{2,1,0:T(8,128)(2,1)}), bf16[16,32,256]{2,1,0:T(8,128)(2,1)S(1)}, u32[]{:S(2)}, u32[]{:S(2)}) async-start(bf16[16,32,256]{2,1,0:T(8,128)(2,1)} %bitcast.21), calls=%async_computation.8 | async-start | bytes 524288 | tf_op jit(solution)/shard_map/all_to_all | solution.py:298
  151.7 4.6 %all-to-all-done.6.basis_ref = bf16[16,32,256]{2,1,0:T(8,128)(2,1)S(1)} async-done(((bf16[16,32,256]{2,1,0:T(8,128)(2,1)}), bf16[16,32,256]{2,1,0:T(8,128)(2,1)S(1)}, u32[]{:S(2)}, u32[]{:S(2)}) %all-to-all-start.6) | async-done | bytes 262176 | tf_op jit(solution)/shard_map/all_to_all | solution.py:298
  157.2 6.0 %all-to-all-start.7 = ((bf16[16,32,256]{2,1,0:T(8,128)(2,1)}), bf16[16,32,256]{2,1,0:T(8,128)(2,1)S(1)}, u32[]{:S(2)}, u32[]{:S(2)}) async-start(bf16[16,32,256]{2,1,0:T(8,128)(2,1)} %shard_map.132), calls=%async_computation.9 | async-start | bytes 524288 | tf_op jit(solution)/shard_map/all_to_all | solution.py:316
  165.5 3.3 %all-to-all-done.7 = bf16[16,32,256]{2,1,0:T(8,128)(2,1)S(1)} async-done(((bf16[16,32,256]{2,1,0:T(8,128)(2,1)}), bf16[16,32,256]{2,1,0:T(8,128)(2,1)S(1)}, u32[]{:S(2)}, u32[]{:S(2)}) %all-to-all-start.7) | async-done | bytes 262176 | tf_op jit(solution)/shard_map/all_to_all | solution.py:316
  169.5 29.2 %all_to_all.46 = bf16[32,80,128]{2,1,0:T(8,128)(2,1)S(1)} all-to-all(bf16[32,80,128]{2,1,0:T(8,128)(2,1)S(1)} %shard_map.133), channel_id=1, replica_groups=mesh['z'=8,'yh'=4,'x'=4,'yl'=2,'c'=2] {'z','yh'}, dimensions={0} | all-to-all | bytes 1310720 | tf_op jit(solution)/shard_map/all_to_all | solution.py:325
  199.0 24.4 %conditional.3 = (bf16[32,64,128]{2,1,0:T(8,128)(2,1)S(1)}) conditional(s32[]{:T(128)} %bitcast.2, bf16[64,128]{1,0:T(8,128)(2,1)S(1)} %slice_reduce_fusion, bf16[64,128]{1,0:T(8,128)(2,1)S(1)} %slice_reduce_fusion), branch_computations={%region_19.20_spmd, %region_20.21_spmd} | conditional | bytes 1589256 | solution.py:329
  199.1 24.3 %all_to_all.43 = bf16[32,64,128]{2,1,0:T(8,128)(2,1)S(1)} all-to-all(bf16[32,64,128]{2,1,0:T(8,128)(2,1)S(1)} %broadcast_in_dim.29), channel_id=1, replica_groups=mesh['z'=8,'yh'=4,'x'=4,'yl'=2,'c'=2] {'z','yh'}, dimensions={0} | all-to-all | bytes 1048576 | tf_op jit(solution)/shard_map/cond/branch_1_fun/all_to_all | solution.py:29
  225.1 6.4 %reduce-scatter.5.cloned.1.call-done = bf16[1,256,128]{2,1,0:T(8,128)(2,1)} async-done(((bf16[4,256,128]{2,1,0:T(8,128)(2,1)}), bf16[1,256,128]{2,1,0:T(8,128)(2,1)}) %reduce-scatter.5.cloned.1.call-update) | async-done | bytes 65552 | tf_op jit(solution)/shard_map/reduce_scatter | solution.py:328
  231.6 1.9 fusion.5
  (89 shorter events, 15.7 us)
Async XLA Ops:
  7.2 157.9 %copy-start = (bf16[1024,256]{1,0:T(8,128)(2,1)S(1)}, bf16[1024,256]{1,0:T(8,128)(2,1)}, u32[]{:S(2)}) copy-start(bf16[1024,256]{1,0:T(8,128)(2,1)} %param.22) | copy-start | bytes 1572868
  7.2 83.9 %all-gather.3.cloned.1.call-start = ((), (), s32[]{:S(2)}) async-start(), calls=%async_computation.11 | async-start | bytes 2359296 | tf_op jit(solution)/shard_map/all_gather | solution.py:220
  8.1 8.0 %collective-permute-start.2 = (bf16[128,128]{1,0:T(8,128)(2,1)S(1)}, bf16[128,128]{1,0:T(8,128)(2,1)S(1)}, u32[]{:S(2)}, u32[]{:S(2)}) collective-permute-start(bf16[128,128]{1,0:T(8,128)(2,1)S(1)} %get-tuple-element.40), channel_id=1, source_target_pairs={{0,0},{1,32},{2,64},{3,96},{4,128},{5,160},{6,192},{7,224},{8,256}... | collective-permute-start | bytes 98312 | tf_op jit(solution)/shard_map/ppermute | solution.py:215
  14.2 9.4 %collective-permute-start.3 = (bf16[128,128]{1,0:T(8,128)(2,1)S(1)}, bf16[128,128]{1,0:T(8,128)(2,1)S(1)}, u32[]{:S(2)}, u32[]{:S(2)}) collective-permute-start(bf16[128,128]{1,0:T(8,128)(2,1)S(1)} %get-tuple-element.41), channel_id=1, source_target_pairs={{0,16},{1,48},{2,80},{3,112},{4,144},{5,176},{6,208},{7,240},{8,27... | collective-permute-start | bytes 98312 | tf_op jit(solution)/shard_map/ppermute | solution.py:215
  38.8 160.0 %reduce-scatter.3.cloned.1.call-start = ((), (), s32[]{:S(2)}) async-start(), calls=%async_computation.12 | async-start | bytes 2359296 | tf_op jit(solution)/shard_map/reduce_scatter | solution.py:307
  82.5 6.4 %collective-permute-start.1 = (bf16[8,512,256]{2,1,0:T(8,128)(2,1)}, bf16[8,512,256]{2,1,0:T(8,128)(2,1)}, u32[]{:S(2)}, u32[]{:S(2)}) collective-permute-start(bf16[8,512,256]{2,1,0:T(8,128)(2,1)} %all_to_all.42), channel_id=1, source_target_pairs={{0,1},{1,0},{2,3},{3,2},{4,5},{5,4},{6,7},{7,6},{8,9},{9,8},{10,11... | collective-permute-start | bytes 6291464 | tf_op jit(solution)/shard_map/cond/branch_1_fun/ppermute | solution.py:39
  96.3 31.3 %copy-start.8 = (s32[256]{0:T(256)S(1)}, s32[256]{0:T(256)}, u32[]{:S(2)}) copy-start(s32[256]{0:T(256)} %param.19) | copy-start | bytes 3076
  125.5 8.3 %copy-start.2 = (f32[4096]{0:T(1024)S(1)}, f32[4096]{0:T(1024)}, u32[]{:S(2)}) copy-start(f32[4096]{0:T(1024)} %param.16) | copy-start | bytes 49156
  125.5 8.3 %copy-start.3 = (f32[4096]{0:T(1024)S(1)}, f32[4096]{0:T(1024)}, u32[]{:S(2)}) copy-start(f32[4096]{0:T(1024)} %param.17) | copy-start | bytes 49156
  125.5 6.4 %collective-permute-start.4 = (bf16[8,528,256]{2,1,0:T(8,128)(2,1)S(1)}, bf16[8,528,256]{2,1,0:T(8,128)(2,1)}, u32[]{:S(2)}, u32[]{:S(2)}) collective-permute-start(bf16[8,528,256]{2,1,0:T(8,128)(2,1)S(1)} %all_to_all.45.mine_ref), channel_id=1, source_target_pairs={{0,1},{1,0},{2,3},{3,2},{4,5},{5,4},{6,7},{7,6},{8,9},{9,8},{10,11... | collective-permute-start | bytes 6488072 | tf_op jit(solution)/shard_map/ppermute | solution.py:39
  133.9 1.6 copy-start.1
  143.4 0.8 copy-start.6
  143.4 2.3 copy-start.4
  145.9 10.3 %all-to-all-start.6 = ((bf16[16,32,256]{2,1,0:T(8,128)(2,1)}), bf16[16,32,256]{2,1,0:T(8,128)(2,1)S(1)}, u32[]{:S(2)}, u32[]{:S(2)}) async-start(bf16[16,32,256]{2,1,0:T(8,128)(2,1)} %bitcast.21), calls=%async_computation.8 | async-start | bytes 524288 | tf_op jit(solution)/shard_map/all_to_all | solution.py:298
  157.2 11.6 %all-to-all-start.7 = ((bf16[16,32,256]{2,1,0:T(8,128)(2,1)}), bf16[16,32,256]{2,1,0:T(8,128)(2,1)S(1)}, u32[]{:S(2)}, u32[]{:S(2)}) async-start(bf16[16,32,256]{2,1,0:T(8,128)(2,1)} %shard_map.132), calls=%async_computation.9 | async-start | bytes 524288 | tf_op jit(solution)/shard_map/all_to_all | solution.py:316
  163.3 68.3 %reduce-scatter.5.cloned.1.call-start = ((), (), s32[]{:S(2)}) async-start(), calls=%async_computation.13 | async-start | bytes 327680 | tf_op jit(solution)/shard_map/reduce_scatter | solution.py:328
  224.6 8.9 %copy-start.7 = (f32[256]{0:T(256)}, f32[256]{0:T(256)S(1)}, u32[]{:S(2)}) copy-start(f32[256]{0:T(256)S(1)} %multiply_bitcast_fusion.2) | copy-start | bytes 3076
Sparse Core Ops, SparseCore 0:
  39.0 52.0 all-gather.2
  143.6 52.9 reduce-scatter.2
  199.4 32.1 reduce-scatter.4

commit v10 on v9

--- a/solution.py
+++ b/solution.py
@@ -221,6 +221,7 @@
     teacher, _ = lax.optimization_barrier((teacher_in, near))
     positive = prev_scale[0] > 0.0
     teacher = lax.cond(positive, tensor_gather, tensor_gather_twice, teacher)
+    teacher, image_ids = lax.optimization_barrier((teacher, image_ids))
 
     normed = layer_norm(student_in.astype(F32)).astype(BF)
     predicted = jnp.dot(normed, head_weight, preferred_element_type=F32)
@@ -235,6 +236,7 @@
     smem, vmem = pl.BlockSpec(memory_space=pltpu.SMEM), pl.BlockSpec(memory_space=pltpu.VMEM)
     anywhere = pl.BlockSpec(memory_space=pl.ANY)
     position = tpos.reshape(1)
+    proj, token_weight = lax.optimization_barrier((proj, token_weight))
     raw, stat = pl.pallas_call(
         project_kernel,
         out_shape=(jax.ShapeDtypeStruct((rows, own), BF), jax.ShapeDtypeStruct((rows, 2), F32)),
@@ -325,7 +327,7 @@
     taken = lax.all_to_all(sent, DP, 0, 0, tiled=True)
 
     grad_own = jnp.sum(taken[:, : 2 * depth, :].astype(F32), axis=0).astype(BF)
-    within = lax.psum_scatter(within, "yh", scatter_dimension=0, tiled=True)
+    within = lax.psum_scatter(within.astype(F32), "yh", scatter_dimension=0, tiled=True)
     grads = lax.cond(
         positive,
         lambda block: broadcast_gather(block, DP),
@@ -350,7 +352,7 @@
     between = lax.dot_general(
         off_t, off_d, (((0,), (0,)), ((), ())), precision=lax.Precision.HIGHEST, preferred_element_type=F32
     )
-    new_cov = (within.reshape(own, part).astype(F32) + between * rows) / all_tokens
+    new_cov = (within.reshape(own, part) + between * rows) / all_tokens
     return (new_cov, new_mean, grad_head, loss / image_count)
 
 

time: 241 us -> 245 us (1.017)
  the two profiles are of different devices: /device:TPU:18 before, /device:TPU:8 now
where the time goes in v10:
time: 245 us; the launch traced here: 244 us
  blocking collectives  152 us (62%)
  waiting for transfers between devices  23.9 us (10%)
  starting transfers between devices  21.7 us (9%)
  Pallas kernels  15.1 us (6%)
  between operations  14.9 us (6%)
  other arithmetic  8.05 us (3%)
  local copies, waits for them, and re-layouts  6.27 us (3%)
    all_to_all x4, blocking collectives, broadcast_gather(): lax.all_to_all(jnp.broadcast_to(block[None], (count,) + block.shape), axe...  122 us
    all_to_all x1, blocking collectives, body(): taken = lax.all_to_all(sent, DP, 0, 0, tiled=True)  29.6 us
    ppermute x2, waiting for transfers between devices, tensor_gather(): return (mine, lax.ppermute(mine, 'c', [(0, 1), (1, 0)]))  8.35 us
    ppermute x2, starting transfers between devices, body(): got.append(lax.ppermute(send, DP + TN, route))  7.86 us
    all_to_all x1, waiting for transfers between devices, body(): lax.all_to_all(basis.reshape(blocks, rows // blocks, own), TN, 0, 0, tile...  5.86 us
    pallas_call x1, Pallas kernels, body(): pl.pallas_call(feature_kernel, out_shape=(jax.ShapeDtypeStruct((blocks, r...  5.3 us
  transfers between devices with their start and end apart: 9, of which 6 were waited for; matrix products, arithmetic and copies ran while one was open for 3% of the time, Pallas kernels for 1%

profile of v10, /device:TPU:8, one launch (start us, length us, event | category | flops | bytes accessed | tf_op | source)
XLA Modules:
  0.0 244.1 jit_solution(2442412448670083549)
XLA Ops:
  8.1 4.2 %collective-permute-start.2 = (bf16[128,128]{1,0:T(8,128)(2,1)S(1)}, bf16[128,128]{1,0:T(8,128)(2,1)S(1)}, u32[]{:S(2)}, u32[]{:S(2)}) collective-permute-start(bf16[128,128]{1,0:T(8,128)(2,1)S(1)} %get-tuple-element.50), channel_id=1, source_target_pairs={{0,0},{1,32},{2,64},{3,96},{4,128},{5,160},{6,192},{7,224},{8,256}... | collective-permute-start | bytes 98312 | tf_op jit(solution)/shard_map/ppermute | solution.py:215
  12.3 3.7 %collective-permute-start.3 = (bf16[128,128]{1,0:T(8,128)(2,1)S(1)}, bf16[128,128]{1,0:T(8,128)(2,1)S(1)}, u32[]{:S(2)}, u32[]{:S(2)}) collective-permute-start(bf16[128,128]{1,0:T(8,128)(2,1)S(1)} %get-tuple-element.51), channel_id=1, source_target_pairs={{0,16},{1,48},{2,80},{3,112},{4,144},{5,176},{6,208},{7,240},{8,27... | collective-permute-start | bytes 98312 | tf_op jit(solution)/shard_map/ppermute | solution.py:215
  16.0 3.6 %collective-permute-done.3 = bf16[128,128]{1,0:T(8,128)(2,1)S(1)} collective-permute-done((bf16[128,128]{1,0:T(8,128)(2,1)S(1)}, bf16[128,128]{1,0:T(8,128)(2,1)S(1)}, u32[]{:S(2)}, u32[]{:S(2)}) %collective-permute-start.3) | collective-permute-done | bytes 32800 | tf_op jit(solution)/shard_map/ppermute | solution.py:215
  19.6 16.9 %all_to_all.44 = bf16[4,128,256]{2,1,0:T(8,128)(2,1)} all-to-all(bf16[4,128,256]{2,1,0:T(8,128)(2,1)S(1)} %broadcast_in_dim.36), channel_id=1, replica_groups=mesh['z'=8,'yh'=4,'x'=4,'yl'=2,'c'=2] {'yh'}, dimensions={0} | all-to-all | bytes 524288 | tf_op jit(solution)/shard_map/all_to_all | solution.py:29
  37.3 53.4 %conditional.2 = (bf16[8,512,256]{2,1,0:T(8,128)(2,1)}, bf16[8,512,256]{2,1,0:T(8,128)(2,1)}) conditional(s32[]{:T(128)} %bitcast.2, bf16[512,256]{1,0:T(8,128)(2,1)} %param.14, bf16[512,256]{1,0:T(8,128)(2,1)} %param.14), branch_computations={%region_0.1_spmd, %region_1.2_spmd} | conditional | bytes 17301620 | solution.py:223
  38.4 45.8 %all_to_all.42 = bf16[8,512,256]{2,1,0:T(8,128)(2,1)} all-to-all(bf16[8,512,256]{2,1,0:T(8,128)(2,1)S(1)} %broadcast_in_dim.24), channel_id=1, replica_groups=mesh['z'=8,'yh'=4,'x'=4,'yl'=2,'c'=2] {'x','yl'}, dimensions={0} | all-to-all | bytes 4194304 | tf_op jit(solution)/shard_map/cond/branch_1_fun/all_to_all | solution.py:29
  84.3 2.2 collective-permute-start.1
  86.5 4.2 %collective-permute-done.1 = bf16[8,512,256]{2,1,0:T(8,128)(2,1)} collective-permute-done((bf16[8,512,256]{2,1,0:T(8,128)(2,1)}, bf16[8,512,256]{2,1,0:T(8,128)(2,1)}, u32[]{:S(2)}, u32[]{:S(2)}) %collective-permute-start.1) | collective-permute-done | bytes 2097184 | tf_op jit(solution)/shard_map/cond/branch_1_fun/ppermute | solution.py:39
  91.9 4.5 %shard_map.129 = (bf16[512,256]{1,0:T(8,128)(2,1)S(1)}, f32[512,2]{1,0:T(8,128)S(1)}) custom-call(s32[1]{0:T(128)} %bitcast.1.pos_ref, bf16[8,512,256]{2,1,0:T(8,128)(2,1)} %get-tuple-element.27.mine_hbm, bf16[8,512,256]{2,1,0:T(8,128)(2,1)} %get-tuple-element.28.other_hbm, bf16[16,256,256]{2,1,0:T(8,128)(2,1)} %bitcast.71), custom_call_target="tpu_custom_call" | custom-call | flops 1073741824 | bytes 8388608 | tf_op jit(solution)/shard_map/pallas_call | solution.py:240
  97.2 31.0 %all_to_all.45.mine_ref = bf16[8,528,256]{2,1,0:T(8,128)(2,1)S(1)} all-to-all(bf16[8,528,256]{2,1,0:T(8,128)(2,1)S(1)} %broadcast_in_dim.44), channel_id=1, replica_groups=mesh['z'=8,'yh'=4,'x'=4,'yl'=2,'c'=2] {'x','yl'}, dimensions={0} | all-to-all | bytes 4325376 | tf_op jit(solution)/shard_map/all_to_all | solution.py:29
  128.2 2.0 collective-permute-start.4
  130.4 4.1 %collective-permute-done.4.other_ref = bf16[8,528,256]{2,1,0:T(8,128)(2,1)} collective-permute-done((bf16[8,528,256]{2,1,0:T(8,128)(2,1)S(1)}, bf16[8,528,256]{2,1,0:T(8,128)(2,1)}, u32[]{:S(2)}, u32[]{:S(2)}) %collective-permute-start.4) | collective-permute-done | bytes 2162720 | tf_op jit(solution)/shard_map/ppermute | solution.py:39
  136.5 1.6 copy-done.1
  138.1 5.3 %shard_map.130 = (bf16[16,512,256]{2,1,0:T(8,128)(2,1)S(1)}, bf16[512,256]{1,0:T(8,128)(2,1)}, f32[16,1,256]{2,1,0:T(1,128)S(1)}) custom-call(s32[1]{0:T(128)} %bitcast.1.pos_ref, bf16[8,528,256]{2,1,0:T(8,128)(2,1)S(1)} %all_to_all.45.mine_ref, bf16[8,528,256]{2,1,0:T(8,128)(2,1)} %collective-permute-done.4.other_ref, f32[512,16]{1,0:T(8,128)S(1)} %bitcast.68, ...), custom_call_target="tpu_custom_call" | custom-call | flops 1073741824 | bytes 12582912 | tf_op jit(solution)/shard_map/pallas_call | solution.py:278
  143.4 2.7 %shard_map.131 = bf16[32,256,128]{2,1,0:T(8,128)(2,1)} custom-call(s32[1]{0:T(128)} %bitcast.1.pos_ref, bf16[16,512,256]{2,1,0:T(8,128)(2,1)S(1)} %get-tuple-element.33.f_ref, f32[16,1,256]{2,1,0:T(1,128)S(1)} %get-tuple-element.34.sums_ref), custom_call_target="tpu_custom_call" | custom-call | flops 1073741824 | bytes 6291456 | tf_op jit(solution)/shard_map/pallas_call | solution.py:301
  147.5 4.6 %all-to-all-start.6 = ((bf16[16,32,256]{2,1,0:T(8,128)(2,1)}), bf16[16,32,256]{2,1,0:T(8,128)(2,1)S(1)}, u32[]{:S(2)}, u32[]{:S(2)}) async-start(bf16[16,32,256]{2,1,0:T(8,128)(2,1)} %bitcast.22), calls=%async_computation.8 | async-start | bytes 524288 | tf_op jit(solution)/shard_map/all_to_all | solution.py:300
  153.1 5.9 %all-to-all-done.6.basis_ref = bf16[16,32,256]{2,1,0:T(8,128)(2,1)S(1)} async-done(((bf16[16,32,256]{2,1,0:T(8,128)(2,1)}), bf16[16,32,256]{2,1,0:T(8,128)(2,1)S(1)}, u32[]{:S(2)}, u32[]{:S(2)}) %all-to-all-start.6) | async-done | bytes 262176 | tf_op jit(solution)/shard_map/all_to_all | solution.py:300
  159.9 4.7 %all-to-all-start.7 = ((bf16[16,32,256]{2,1,0:T(8,128)(2,1)}), bf16[16,32,256]{2,1,0:T(8,128)(2,1)S(1)}, u32[]{:S(2)}, u32[]{:S(2)}) async-start(bf16[16,32,256]{2,1,0:T(8,128)(2,1)} %shard_map.132), calls=%async_computation.9 | async-start | bytes 524288 | tf_op jit(solution)/shard_map/all_to_all | solution.py:318
  167.0 4.4 %all-to-all-done.7 = bf16[16,32,256]{2,1,0:T(8,128)(2,1)S(1)} async-done(((bf16[16,32,256]{2,1,0:T(8,128)(2,1)}), bf16[16,32,256]{2,1,0:T(8,128)(2,1)S(1)}, u32[]{:S(2)}, u32[]{:S(2)}) %all-to-all-start.7) | async-done | bytes 262176 | tf_op jit(solution)/shard_map/all_to_all | solution.py:318
  172.1 29.6 %all_to_all.46 = bf16[32,80,128]{2,1,0:T(8,128)(2,1)S(1)} all-to-all(bf16[32,80,128]{2,1,0:T(8,128)(2,1)S(1)} %shard_map.133), channel_id=1, replica_groups=mesh['z'=8,'yh'=4,'x'=4,'yl'=2,'c'=2] {'z','yh'}, dimensions={0} | all-to-all | bytes 1310720 | tf_op jit(solution)/shard_map/all_to_all | solution.py:327
  201.8 1.8 convert_element_type.45
  203.7 28.6 %conditional.3 = (bf16[32,64,128]{2,1,0:T(8,128)(2,1)S(1)}) conditional(s32[]{:T(128)} %bitcast.2, bf16[64,128]{1,0:T(8,128)(2,1)S(1)} %slice_reduce_fusion, bf16[64,128]{1,0:T(8,128)(2,1)S(1)} %slice_reduce_fusion), branch_computations={%region_19.20_spmd, %region_20.21_spmd} | conditional | bytes 1589256 | solution.py:331
  203.8 28.4 %all_to_all.43 = bf16[32,64,128]{2,1,0:T(8,128)(2,1)S(1)} all-to-all(bf16[32,64,128]{2,1,0:T(8,128)(2,1)S(1)} %broadcast_in_dim.29), channel_id=1, replica_groups=mesh['z'=8,'yh'=4,'x'=4,'yl'=2,'c'=2] {'z','yh'}, dimensions={0} | all-to-all | bytes 1048576 | tf_op jit(solution)/shard_map/cond/branch_1_fun/all_to_all | solution.py:29
  235.7 2.0 fusion.5
  (90 shorter events, 16.0 us)
Async XLA Ops:
  7.2 159.3 %copy-start = (bf16[1024,256]{1,0:T(8,128)(2,1)S(1)}, bf16[1024,256]{1,0:T(8,128)(2,1)}, u32[]{:S(2)}) copy-start(bf16[1024,256]{1,0:T(8,128)(2,1)} %param.22) | copy-start | bytes 1572868
  7.2 84.7 %all-gather.3.cloned.1.call-start = ((), (), s32[]{:S(2)}) async-start(), calls=%async_computation.11 | async-start | bytes 2359296 | tf_op jit(solution)/shard_map/all_gather | solution.py:220
  8.1 7.9 %collective-permute-start.2 = (bf16[128,128]{1,0:T(8,128)(2,1)S(1)}, bf16[128,128]{1,0:T(8,128)(2,1)S(1)}, u32[]{:S(2)}, u32[]{:S(2)}) collective-permute-start(bf16[128,128]{1,0:T(8,128)(2,1)S(1)} %get-tuple-element.50), channel_id=1, source_target_pairs={{0,0},{1,32},{2,64},{3,96},{4,128},{5,160},{6,192},{7,224},{8,256}... | collective-permute-start | bytes 98312 | tf_op jit(solution)/shard_map/ppermute | solution.py:215
  12.3 7.3 %collective-permute-start.3 = (bf16[128,128]{1,0:T(8,128)(2,1)S(1)}, bf16[128,128]{1,0:T(8,128)(2,1)S(1)}, u32[]{:S(2)}, u32[]{:S(2)}) collective-permute-start(bf16[128,128]{1,0:T(8,128)(2,1)S(1)} %get-tuple-element.51), channel_id=1, source_target_pairs={{0,16},{1,48},{2,80},{3,112},{4,144},{5,176},{6,208},{7,240},{8,27... | collective-permute-start | bytes 98312 | tf_op jit(solution)/shard_map/ppermute | solution.py:215
  36.5 165.3 %reduce-scatter.3.cloned.1.call-start = ((), (), s32[]{:S(2)}) async-start(), calls=%async_computation.12 | async-start | bytes 2359296 | tf_op jit(solution)/shard_map/reduce_scatter | solution.py:309
  37.3 53.4 %copy-start.6 = (s32[16384]{0:T(1024)S(1)}, s32[16384]{0:T(1024)}, u32[]{:S(2)}) copy-start(s32[16384]{0:T(1024)} %param.23) | copy-start | bytes 196612
  84.3 6.4 %collective-permute-start.1 = (bf16[8,512,256]{2,1,0:T(8,128)(2,1)}, bf16[8,512,256]{2,1,0:T(8,128)(2,1)}, u32[]{:S(2)}, u32[]{:S(2)}) collective-permute-start(bf16[8,512,256]{2,1,0:T(8,128)(2,1)} %all_to_all.42), channel_id=1, source_target_pairs={{0,1},{1,0},{2,3},{3,2},{4,5},{5,4},{6,7},{7,6},{8,9},{9,8},{10,11... | collective-permute-start | bytes 6291464 | tf_op jit(solution)/shard_map/cond/branch_1_fun/ppermute | solution.py:39
  97.2 33.1 %copy-start.8 = (s32[256]{0:T(256)S(1)}, s32[256]{0:T(256)}, u32[]{:S(2)}) copy-start(s32[256]{0:T(256)} %param.19) | copy-start | bytes 3076
  128.2 8.3 %copy-start.2 = (f32[4096]{0:T(1024)S(1)}, f32[4096]{0:T(1024)}, u32[]{:S(2)}) copy-start(f32[4096]{0:T(1024)} %param.16) | copy-start | bytes 49156
  128.2 8.3 %copy-start.3 = (f32[4096]{0:T(1024)S(1)}, f32[4096]{0:T(1024)}, u32[]{:S(2)}) copy-start(f32[4096]{0:T(1024)} %param.17) | copy-start | bytes 49156
  128.2 6.4 %collective-permute-start.4 = (bf16[8,528,256]{2,1,0:T(8,128)(2,1)S(1)}, bf16[8,528,256]{2,1,0:T(8,128)(2,1)}, u32[]{:S(2)}, u32[]{:S(2)}) collective-permute-start(bf16[8,528,256]{2,1,0:T(8,128)(2,1)S(1)} %all_to_all.45.mine_ref), channel_id=1, source_target_pairs={{0,1},{1,0},{2,3},{3,2},{4,5},{5,4},{6,7},{7,6},{8,9},{9,8},{10,11... | collective-permute-start | bytes 6488072 | tf_op jit(solution)/shard_map/ppermute | solution.py:39
  136.5 1.6 copy-start.1
  146.0 1.2 copy-start.4
  147.5 11.4 %all-to-all-start.6 = ((bf16[16,32,256]{2,1,0:T(8,128)(2,1)}), bf16[16,32,256]{2,1,0:T(8,128)(2,1)S(1)}, u32[]{:S(2)}, u32[]{:S(2)}) async-start(bf16[16,32,256]{2,1,0:T(8,128)(2,1)} %bitcast.22), calls=%async_computation.8 | async-start | bytes 524288 | tf_op jit(solution)/shard_map/all_to_all | solution.py:300
  159.9 11.6 %all-to-all-start.7 = ((bf16[16,32,256]{2,1,0:T(8,128)(2,1)}), bf16[16,32,256]{2,1,0:T(8,128)(2,1)S(1)}, u32[]{:S(2)}, u32[]{:S(2)}) async-start(bf16[16,32,256]{2,1,0:T(8,128)(2,1)} %shard_map.132), calls=%async_computation.9 | async-start | bytes 524288 | tf_op jit(solution)/shard_map/all_to_all | solution.py:318
  164.6 71.0 %reduce-scatter.5.cloned.1.call-start = ((), (), s32[]{:S(2)}) async-start(), calls=%async_computation.13 | async-start | bytes 655360 | tf_op jit(solution)/shard_map/reduce_scatter | solution.py:330
  233.5 4.1 %copy-start.7 = (f32[256]{0:T(256)}, f32[256]{0:T(256)S(1)}, u32[]{:S(2)}) copy-start(f32[256]{0:T(256)S(1)} %multiply_bitcast_fusion.2) | copy-start | bytes 3076
Sparse Core Ops, SparseCore 0:
  36.6 54.3 all-gather.2
  146.2 43.3 reduce-scatter.2
  203.7 31.8 reduce-scatter.4

commit v11 on v9

--- a/solution.py
+++ b/solution.py
@@ -93,17 +93,18 @@
     core = lax.rem(pos_ref[0], 2)
     rstd = rstd_ref[...]
     total = jnp.zeros((rows, own), F32)
+    offset = jnp.zeros((16, own), F32)
     for j in range(blocks):
         source, q, side = (mine_ref, j, core) if j < blocks // 2 else (other_ref, j - blocks // 2, 1 - core)
         b = 2 * q + side
         value = (source[q, :rows, :].astype(F32) + adj_ref[:, j : j + 1]) * rstd * gain_ref[b]
         feature = value.astype(BF)
         f_ref[b] = feature
-        feature = feature.astype(F32)
-        sums_ref[b] = jnp.sum(feature, axis=0, keepdims=True)
-        shifted = (feature - prev_ref[b]).astype(BF)
+        sums_ref[b] = jnp.sum(feature.astype(F32), axis=0, keepdims=True)
         turn = rot_ref[pl.ds(pl.multiple_of(b * own, own), own), :]
-        total += jnp.dot(shifted, turn, preferred_element_type=F32)
+        total += jnp.dot(feature, turn, preferred_element_type=F32)
+        offset += jnp.dot(prev_ref[b], turn, preferred_element_type=F32)
+    total -= jnp.sum(offset, axis=0, keepdims=True)
     basis_ref[...] = total.astype(BF) * sign_ref[...]
 
 
@@ -218,9 +219,6 @@
     )
     near = broadcast_gather(strip, "yh")
     proj = lax.all_gather(near.reshape(-1, own), "z", axis=0, tiled=True)
-    teacher, _ = lax.optimization_barrier((teacher_in, near))
-    positive = prev_scale[0] > 0.0
-    teacher = lax.cond(positive, tensor_gather, tensor_gather_twice, teacher)
 
     normed = layer_norm(student_in.astype(F32)).astype(BF)
     predicted = jnp.dot(normed, head_weight, preferred_element_type=F32)
@@ -235,6 +233,9 @@
     smem, vmem = pl.BlockSpec(memory_space=pltpu.SMEM), pl.BlockSpec(memory_space=pltpu.VMEM)
     anywhere = pl.BlockSpec(memory_space=pl.ANY)
     position = tpos.reshape(1)
+    teacher, _, token_weight = lax.optimization_barrier((teacher_in, near, token_weight))
+    positive = prev_scale[0] > 0.0
+    teacher = lax.cond(positive, tensor_gather, tensor_gather_twice, teacher)
     raw, stat = pl.pallas_call(
         project_kernel,
         out_shape=(jax.ShapeDtypeStruct((rows, own), BF), jax.ShapeDtypeStruct((rows, 2), F32)),
@@ -273,6 +274,8 @@
     index_col = lax.broadcasted_iota(jnp.int32, (own, own), 1)
     table = parity_sign(index_row & index_col).astype(BF)
 
+    prev_parts = jnp.stack(split3(mean_prev.reshape(blocks, own)), axis=1)
+    prev_parts = jnp.pad(prev_parts, ((0, 0), (0, 13), (0, 0))).astype(BF)
     features, basis, sums = pl.pallas_call(
         feature_kernel,
         out_shape=(
@@ -291,7 +294,7 @@
         adjust.T,
         rstd[:, None],
         final_gain.reshape(blocks, 1, own),
-        mean_prev.reshape(blocks, 1, own),
+        prev_parts,
         rotation,
         (2 * signs - 1).astype(BF)[None, :],
     )

time: 241 us -> 242 us (level)
  transfers between devices with their start and end apart: 9 -> 9, of which waited for: 7 -> 6; matrix products, arithmetic and copies ran while one was open for 3% -> 3% of each run, Pallas kernels for 1% -> 1%
where the time goes in v11:
time: 242 us; the launch traced here: 241 us
  blocking collectives  142 us (59%)
  waiting for transfers between devices  30.5 us (13%)
  starting transfers between devices  23.1 us (10%)
  Pallas kernels  14.9 us (6%)
  between operations  14.9 us (6%)
  other arithmetic  7.23 us (3%)
  local copies, waits for them, and re-layouts  6.93 us (3%)
    all_to_all x4, blocking collectives, broadcast_gather(): lax.all_to_all(jnp.broadcast_to(block[None], (count,) + block.shape), axe...  113 us
    all_to_all x1, blocking collectives, body(): taken = lax.all_to_all(sent, DP, 0, 0, tiled=True)  29.1 us
    ppermute x2, waiting for transfers between devices, tensor_gather(): return (mine, lax.ppermute(mine, 'c', [(0, 1), (1, 0)]))  8.47 us
    ppermute x2, starting transfers between devices, body(): got.append(lax.ppermute(send, DP + TN, route))  7.97 us
    ppermute x2, waiting for transfers between devices, body(): got.append(lax.ppermute(send, DP + TN, route))  7.46 us
    reduce_scatter x1, waiting for transfers between devices, body(): within = lax.psum_scatter(within, 'yh', scatter_dimension=0, tiled=True)  6.76 us
    all_to_all x1, starting transfers between devices, body(): target = lax.all_to_all(lines, TN, 0, 0, tiled=True).reshape(rows, own)  6.03 us
    pallas_call x1, Pallas kernels, body(): pl.pallas_call(feature_kernel, out_shape=(jax.ShapeDtypeStruct((blocks, r...  5.07 us
  transfers between devices with their start and end apart: 9, of which 6 were waited for; matrix products, arithmetic and copies ran while one was open for 3% of the time, Pallas kernels for 1%

profile of v11, /device:TPU:18, one launch (start us, length us, event | category | flops | bytes accessed | tf_op | source)
XLA Modules:
  0.0 241.5 jit_solution(67631534456779956)
XLA Ops:
  8.1 6.0 %collective-permute-start.2 = (bf16[128,128]{1,0:T(8,128)(2,1)S(1)}, bf16[128,128]{1,0:T(8,128)(2,1)S(1)}, u32[]{:S(2)}, u32[]{:S(2)}) collective-permute-start(bf16[128,128]{1,0:T(8,128)(2,1)S(1)} %get-tuple-element.42), channel_id=1, source_target_pairs={{0,0},{1,32},{2,64},{3,96},{4,128},{5,160},{6,192},{7,224},{8,256}... | collective-permute-start | bytes 98312 | tf_op jit(solution)/shard_map/ppermute | solution.py:216
  14.2 1.9 collective-permute-start.3
  16.1 7.5 %collective-permute-done.3 = bf16[128,128]{1,0:T(8,128)(2,1)S(1)} collective-permute-done((bf16[128,128]{1,0:T(8,128)(2,1)S(1)}, bf16[128,128]{1,0:T(8,128)(2,1)S(1)}, u32[]{:S(2)}, u32[]{:S(2)}) %collective-permute-start.3) | collective-permute-done | bytes 32800 | tf_op jit(solution)/shard_map/ppermute | solution.py:216
  23.6 15.2 %all_to_all.44 = bf16[4,128,256]{2,1,0:T(8,128)(2,1)} all-to-all(bf16[4,128,256]{2,1,0:T(8,128)(2,1)S(1)} %broadcast_in_dim.28), channel_id=1, replica_groups=mesh['z'=8,'yh'=4,'x'=4,'yl'=2,'c'=2] {'yh'}, dimensions={0} | all-to-all | bytes 524288 | tf_op jit(solution)/shard_map/all_to_all | solution.py:29
  40.4 1.7 convert_reduce_fusion
  42.4 49.3 %conditional.2 = (bf16[8,512,256]{2,1,0:T(8,128)(2,1)}, bf16[8,512,256]{2,1,0:T(8,128)(2,1)}) conditional(s32[]{:T(128)} %bitcast.2, bf16[512,256]{1,0:T(8,128)(2,1)} %param.14, bf16[512,256]{1,0:T(8,128)(2,1)} %param.14), branch_computations={%region_2.3_spmd, %region_3.4_spmd} | conditional | bytes 17301620 | solution.py:238
  43.5 41.8 %all_to_all.42 = bf16[8,512,256]{2,1,0:T(8,128)(2,1)} all-to-all(bf16[8,512,256]{2,1,0:T(8,128)(2,1)S(1)} %broadcast_in_dim.20), channel_id=1, replica_groups=mesh['z'=8,'yh'=4,'x'=4,'yl'=2,'c'=2] {'x','yl'}, dimensions={0} | all-to-all | bytes 4194304 | tf_op jit(solution)/shard_map/cond/branch_1_fun/all_to_all | solution.py:29
  85.3 1.9 collective-permute-start.1
  87.2 4.5 %collective-permute-done.1 = bf16[8,512,256]{2,1,0:T(8,128)(2,1)} collective-permute-done((bf16[8,512,256]{2,1,0:T(8,128)(2,1)}, bf16[8,512,256]{2,1,0:T(8,128)(2,1)}, u32[]{:S(2)}, u32[]{:S(2)}) %collective-permute-start.1) | collective-permute-done | bytes 2097184 | tf_op jit(solution)/shard_map/cond/branch_1_fun/ppermute | solution.py:39
  91.7 4.5 %shard_map.129 = (bf16[512,256]{1,0:T(8,128)(2,1)S(1)}, f32[512,2]{1,0:T(8,128)S(1)}) custom-call(s32[1]{0:T(128)} %bitcast.1.pos_ref, bf16[8,512,256]{2,1,0:T(8,128)(2,1)} %get-tuple-element.21.mine_hbm, bf16[8,512,256]{2,1,0:T(8,128)(2,1)} %get-tuple-element.22.other_hbm, bf16[16,256,256]{2,1,0:T(8,128)(2,1)} %bitcast.71), custom_call_target="tpu_custom_call" | custom-call | flops 1073741824 | bytes 8388608 | tf_op jit(solution)/shard_map/pallas_call | solution.py:239
  97.0 31.4 %all_to_all.45.mine_ref = bf16[8,528,256]{2,1,0:T(8,128)(2,1)S(1)} all-to-all(bf16[8,528,256]{2,1,0:T(8,128)(2,1)S(1)} %broadcast_in_dim.40), channel_id=1, replica_groups=mesh['z'=8,'yh'=4,'x'=4,'yl'=2,'c'=2] {'x','yl'}, dimensions={0} | all-to-all | bytes 4325376 | tf_op jit(solution)/shard_map/all_to_all | solution.py:29
  128.3 2.0 collective-permute-start.4
  130.7 4.0 %collective-permute-done.4.other_ref = bf16[8,528,256]{2,1,0:T(8,128)(2,1)} collective-permute-done((bf16[8,528,256]{2,1,0:T(8,128)(2,1)S(1)}, bf16[8,528,256]{2,1,0:T(8,128)(2,1)}, u32[]{:S(2)}, u32[]{:S(2)}) %collective-permute-start.4) | collective-permute-done | bytes 2162720 | tf_op jit(solution)/shard_map/ppermute | solution.py:39
  138.2 5.1 %shard_map.130 = (bf16[16,512,256]{2,1,0:T(8,128)(2,1)S(1)}, bf16[512,256]{1,0:T(8,128)(2,1)}, f32[16,1,256]{2,1,0:T(1,128)S(1)}) custom-call(s32[1]{0:T(128)} %bitcast.1.pos_ref, bf16[8,528,256]{2,1,0:T(8,128)(2,1)S(1)} %all_to_all.45.mine_ref, bf16[8,528,256]{2,1,0:T(8,128)(2,1)} %collective-permute-done.4.other_ref, f32[512,16]{1,0:T(8,128)S(1)} %bitcast.69, ...), custom_call_target="tpu_custom_call" | custom-call | flops 1073741824 | bytes 12582912 | tf_op jit(solution)/shard_map/pallas_call | solution.py:279
  143.3 2.7 %shard_map.131 = bf16[32,256,128]{2,1,0:T(8,128)(2,1)} custom-call(s32[1]{0:T(128)} %bitcast.1.pos_ref, bf16[16,512,256]{2,1,0:T(8,128)(2,1)S(1)} %get-tuple-element.25.f_ref, f32[16,1,256]{2,1,0:T(1,128)S(1)} %get-tuple-element.26.sums_ref), custom_call_target="tpu_custom_call" | custom-call | flops 1073741824 | bytes 6291456 | tf_op jit(solution)/shard_map/pallas_call | solution.py:302
  147.4 4.8 %all-to-all-start.6 = ((bf16[16,32,256]{2,1,0:T(8,128)(2,1)}), bf16[16,32,256]{2,1,0:T(8,128)(2,1)S(1)}, u32[]{:S(2)}, u32[]{:S(2)}) async-start(bf16[16,32,256]{2,1,0:T(8,128)(2,1)} %bitcast.22), calls=%async_computation.8 | async-start | bytes 524288 | tf_op jit(solution)/shard_map/all_to_all | solution.py:301
  153.2 4.6 %all-to-all-done.6.basis_ref = bf16[16,32,256]{2,1,0:T(8,128)(2,1)S(1)} async-done(((bf16[16,32,256]{2,1,0:T(8,128)(2,1)}), bf16[16,32,256]{2,1,0:T(8,128)(2,1)S(1)}, u32[]{:S(2)}, u32[]{:S(2)}) %all-to-all-start.6) | async-done | bytes 262176 | tf_op jit(solution)/shard_map/all_to_all | solution.py:301
  158.7 6.0 %all-to-all-start.7 = ((bf16[16,32,256]{2,1,0:T(8,128)(2,1)}), bf16[16,32,256]{2,1,0:T(8,128)(2,1)S(1)}, u32[]{:S(2)}, u32[]{:S(2)}) async-start(bf16[16,32,256]{2,1,0:T(8,128)(2,1)} %shard_map.132), calls=%async_computation.9 | async-start | bytes 524288 | tf_op jit(solution)/shard_map/all_to_all | solution.py:319
  167.1 3.1 %all-to-all-done.7 = bf16[16,32,256]{2,1,0:T(8,128)(2,1)S(1)} async-done(((bf16[16,32,256]{2,1,0:T(8,128)(2,1)}), bf16[16,32,256]{2,1,0:T(8,128)(2,1)S(1)}, u32[]{:S(2)}, u32[]{:S(2)}) %all-to-all-start.7) | async-done | bytes 262176 | tf_op jit(solution)/shard_map/all_to_all | solution.py:319
  170.9 29.1 %all_to_all.46 = bf16[32,80,128]{2,1,0:T(8,128)(2,1)S(1)} all-to-all(bf16[32,80,128]{2,1,0:T(8,128)(2,1)S(1)} %shard_map.133), channel_id=1, replica_groups=mesh['z'=8,'yh'=4,'x'=4,'yl'=2,'c'=2] {'z','yh'}, dimensions={0} | all-to-all | bytes 1310720 | tf_op jit(solution)/shard_map/all_to_all | solution.py:328
  200.3 24.3 %conditional.3 = (bf16[32,64,128]{2,1,0:T(8,128)(2,1)S(1)}) conditional(s32[]{:T(128)} %bitcast.2, bf16[64,128]{1,0:T(8,128)(2,1)S(1)} %slice_reduce_fusion, bf16[64,128]{1,0:T(8,128)(2,1)S(1)} %slice_reduce_fusion), branch_computations={%region_19.20_spmd, %region_20.21_spmd} | conditional | bytes 1589256 | solution.py:332
  200.4 24.1 %all_to_all.43 = bf16[32,64,128]{2,1,0:T(8,128)(2,1)S(1)} all-to-all(bf16[32,64,128]{2,1,0:T(8,128)(2,1)S(1)} %broadcast_in_dim.21), channel_id=1, replica_groups=mesh['z'=8,'yh'=4,'x'=4,'yl'=2,'c'=2] {'z','yh'}, dimensions={0} | all-to-all | bytes 1048576 | tf_op jit(solution)/shard_map/cond/branch_1_fun/all_to_all | solution.py:29
  226.3 6.8 %reduce-scatter.5.cloned.1.call-done = bf16[1,256,128]{2,1,0:T(8,128)(2,1)} async-done(((bf16[4,256,128]{2,1,0:T(8,128)(2,1)}), bf16[1,256,128]{2,1,0:T(8,128)(2,1)}) %reduce-scatter.5.cloned.1.call-update) | async-done | bytes 65552 | tf_op jit(solution)/shard_map/reduce_scatter | solution.py:331
  233.0 1.9 fusion.5
  (89 shorter events, 15.9 us)
Async XLA Ops:
  7.2 159.4 %copy-start = (bf16[1024,256]{1,0:T(8,128)(2,1)S(1)}, bf16[1024,256]{1,0:T(8,128)(2,1)}, u32[]{:S(2)}) copy-start(bf16[1024,256]{1,0:T(8,128)(2,1)} %param.22) | copy-start | bytes 1572868
  7.2 84.5 %all-gather.3.cloned.1.call-start = ((), (), s32[]{:S(2)}) async-start(), calls=%async_computation.11 | async-start | bytes 2359296 | tf_op jit(solution)/shard_map/all_gather | solution.py:221
  8.1 8.0 %collective-permute-start.2 = (bf16[128,128]{1,0:T(8,128)(2,1)S(1)}, bf16[128,128]{1,0:T(8,128)(2,1)S(1)}, u32[]{:S(2)}, u32[]{:S(2)}) collective-permute-start(bf16[128,128]{1,0:T(8,128)(2,1)S(1)} %get-tuple-element.42), channel_id=1, source_target_pairs={{0,0},{1,32},{2,64},{3,96},{4,128},{5,160},{6,192},{7,224},{8,256}... | collective-permute-start | bytes 98312 | tf_op jit(solution)/shard_map/ppermute | solution.py:216
  14.2 9.4 %collective-permute-start.3 = (bf16[128,128]{1,0:T(8,128)(2,1)S(1)}, bf16[128,128]{1,0:T(8,128)(2,1)S(1)}, u32[]{:S(2)}, u32[]{:S(2)}) collective-permute-start(bf16[128,128]{1,0:T(8,128)(2,1)S(1)} %get-tuple-element.43), channel_id=1, source_target_pairs={{0,16},{1,48},{2,80},{3,112},{4,144},{5,176},{6,208},{7,240},{8,27... | collective-permute-start | bytes 98312 | tf_op jit(solution)/shard_map/ppermute | solution.py:216
  38.8 161.3 %reduce-scatter.3.cloned.1.call-start = ((), (), s32[]{:S(2)}) async-start(), calls=%async_computation.12 | async-start | bytes 2359296 | tf_op jit(solution)/shard_map/reduce_scatter | solution.py:310
  85.3 6.4 %collective-permute-start.1 = (bf16[8,512,256]{2,1,0:T(8,128)(2,1)}, bf16[8,512,256]{2,1,0:T(8,128)(2,1)}, u32[]{:S(2)}, u32[]{:S(2)}) collective-permute-start(bf16[8,512,256]{2,1,0:T(8,128)(2,1)} %all_to_all.42), channel_id=1, source_target_pairs={{0,1},{1,0},{2,3},{3,2},{4,5},{5,4},{6,7},{7,6},{8,9},{9,8},{10,11... | collective-permute-start | bytes 6291464 | tf_op jit(solution)/shard_map/cond/branch_1_fun/ppermute | solution.py:39
  96.9 33.5 %copy-start.7 = (s32[256]{0:T(256)S(1)}, s32[256]{0:T(256)}, u32[]{:S(2)}) copy-start(s32[256]{0:T(256)} %param.19) | copy-start | bytes 3076
  96.9 33.5 %copy-start.5 = (f32[4096]{0:T(1024)S(1)}, f32[4096]{0:T(1024)}, u32[]{:S(2)}) copy-start(f32[4096]{0:T(1024)} %param.17) | copy-start | bytes 49156
  128.3 8.3 %copy-start.2 = (f32[4096]{0:T(1024)S(1)}, f32[4096]{0:T(1024)}, u32[]{:S(2)}) copy-start(f32[4096]{0:T(1024)} %param.16) | copy-start | bytes 49156
  128.3 6.4 %collective-permute-start.4 = (bf16[8,528,256]{2,1,0:T(8,128)(2,1)S(1)}, bf16[8,528,256]{2,1,0:T(8,128)(2,1)}, u32[]{:S(2)}, u32[]{:S(2)}) collective-permute-start(bf16[8,528,256]{2,1,0:T(8,128)(2,1)S(1)} %all_to_all.45.mine_ref), channel_id=1, source_target_pairs={{0,1},{1,0},{2,3},{3,2},{4,5},{5,4},{6,7},{7,6},{8,9},{9,8},{10,11... | collective-permute-start | bytes 6488072 | tf_op jit(solution)/shard_map/ppermute | solution.py:39
  136.6 1.6 copy-start.1
  146.0 1.2 copy-start.3
  147.4 10.3 %all-to-all-start.6 = ((bf16[16,32,256]{2,1,0:T(8,128)(2,1)}), bf16[16,32,256]{2,1,0:T(8,128)(2,1)S(1)}, u32[]{:S(2)}, u32[]{:S(2)}) async-start(bf16[16,32,256]{2,1,0:T(8,128)(2,1)} %bitcast.22), calls=%async_computation.8 | async-start | bytes 524288 | tf_op jit(solution)/shard_map/all_to_all | solution.py:301
  158.7 11.5 %all-to-all-start.7 = ((bf16[16,32,256]{2,1,0:T(8,128)(2,1)}), bf16[16,32,256]{2,1,0:T(8,128)(2,1)S(1)}, u32[]{:S(2)}, u32[]{:S(2)}) async-start(bf16[16,32,256]{2,1,0:T(8,128)(2,1)} %shard_map.132), calls=%async_computation.9 | async-start | bytes 524288 | tf_op jit(solution)/shard_map/all_to_all | solution.py:319
  164.7 68.3 %reduce-scatter.5.cloned.1.call-start = ((), (), s32[]{:S(2)}) async-start(), calls=%async_computation.13 | async-start | bytes 327680 | tf_op jit(solution)/shard_map/reduce_scatter | solution.py:331
  225.7 9.2 %copy-start.6 = (f32[256]{0:T(256)}, f32[256]{0:T(256)S(1)}, u32[]{:S(2)}) copy-start(f32[256]{0:T(256)S(1)} %multiply_bitcast_fusion.2) | copy-start | bytes 3076
Sparse Core Ops, SparseCore 0:
  39.0 52.0 all-gather.2
  146.1 51.9 reduce-scatter.2
  200.9 32.0 reduce-scatter.4

commit v12 on v11

--- a/solution.py
+++ b/solution.py
@@ -219,6 +219,9 @@
     )
     near = broadcast_gather(strip, "yh")
     proj = lax.all_gather(near.reshape(-1, own), "z", axis=0, tiled=True)
+    teacher, _ = lax.optimization_barrier((teacher_in, near))
+    positive = prev_scale[0] > 0.0
+    teacher = lax.cond(positive, tensor_gather, tensor_gather_twice, teacher)
 
     normed = layer_norm(student_in.astype(F32)).astype(BF)
     predicted = jnp.dot(normed, head_weight, preferred_element_type=F32)
@@ -233,9 +236,6 @@
     smem, vmem = pl.BlockSpec(memory_space=pltpu.SMEM), pl.BlockSpec(memory_space=pltpu.VMEM)
     anywhere = pl.BlockSpec(memory_space=pl.ANY)
     position = tpos.reshape(1)
-    teacher, _, token_weight = lax.optimization_barrier((teacher_in, near, token_weight))
-    positive = prev_scale[0] > 0.0
-    teacher = lax.cond(positive, tensor_gather, tensor_gather_twice, teacher)
     raw, stat = pl.pallas_call(
         project_kernel,
         out_shape=(jax.ShapeDtypeStruct((rows, own), BF), jax.ShapeDtypeStruct((rows, 2), F32)),

time: 242 us -> 241 us (level)
  transfers between devices with their start and end apart: 9 -> 9, of which waited for: 6 -> 7; matrix products, arithmetic and copies ran while one was open for 3% -> 3% of each run, Pallas kernels for 1% -> 1%
where the time goes in v12:
time: 241 us; the launch traced here: 240 us
  blocking collectives  140 us (58%)
  waiting for transfers between devices  32.5 us (13%)
  starting transfers between devices  23.1 us (10%)
  between operations  15 us (6%)
  Pallas kernels  14.9 us (6%)
  other arithmetic  6.39 us (3%)
  local copies, waits for them, and re-layouts  5.9 us (2%)
    all_to_all x4, blocking collectives, broadcast_gather(): lax.all_to_all(jnp.broadcast_to(block[None], (count,) + block.shape), axe...  111 us
    all_to_all x1, blocking collectives, body(): taken = lax.all_to_all(sent, DP, 0, 0, tiled=True)  29.3 us
    ppermute x2, waiting for transfers between devices, tensor_gather(): return (mine, lax.ppermute(mine, 'c', [(0, 1), (1, 0)]))  8.47 us
    ppermute x2, starting transfers between devices, body(): got.append(lax.ppermute(send, DP + TN, route))  7.97 us
    ppermute x2, waiting for transfers between devices, body(): got.append(lax.ppermute(send, DP + TN, route))  7.46 us
    reduce_scatter x1, waiting for transfers between devices, body(): within = lax.psum_scatter(within, 'yh', scatter_dimension=0, tiled=True)  6.51 us
    all_to_all x1, starting transfers between devices, body(): target = lax.all_to_all(lines, TN, 0, 0, tiled=True).reshape(rows, own)  6.04 us
    pallas_call x1, Pallas kernels, body(): pl.pallas_call(feature_kernel, out_shape=(jax.ShapeDtypeStruct((blocks, r...  5.07 us
  transfers between devices with their start and end apart: 9, of which 7 were waited for; matrix products, arithmetic and copies ran while one was open for 3% of the time, Pallas kernels for 1%

profile of v12, /device:TPU:18, one launch (start us, length us, event | category | flops | bytes accessed | tf_op | source)
XLA Modules:
  0.0 239.9 jit_solution(9412711287528771759)
XLA Ops:
  8.1 6.0 %collective-permute-start.2 = (bf16[128,128]{1,0:T(8,128)(2,1)S(1)}, bf16[128,128]{1,0:T(8,128)(2,1)S(1)}, u32[]{:S(2)}, u32[]{:S(2)}) collective-permute-start(bf16[128,128]{1,0:T(8,128)(2,1)S(1)} %get-tuple-element.40), channel_id=1, source_target_pairs={{0,0},{1,32},{2,64},{3,96},{4,128},{5,160},{6,192},{7,224},{8,256}... | collective-permute-start | bytes 98312 | tf_op jit(solution)/shard_map/ppermute | solution.py:216
  14.2 1.9 collective-permute-start.3
  16.1 7.5 %collective-permute-done.3 = bf16[128,128]{1,0:T(8,128)(2,1)S(1)} collective-permute-done((bf16[128,128]{1,0:T(8,128)(2,1)S(1)}, bf16[128,128]{1,0:T(8,128)(2,1)S(1)}, u32[]{:S(2)}, u32[]{:S(2)}) %collective-permute-start.3) | collective-permute-done | bytes 32800 | tf_op jit(solution)/shard_map/ppermute | solution.py:216
  23.6 15.2 %all_to_all.44 = bf16[4,128,256]{2,1,0:T(8,128)(2,1)} all-to-all(bf16[4,128,256]{2,1,0:T(8,128)(2,1)S(1)} %broadcast_in_dim.36), channel_id=1, replica_groups=mesh['z'=8,'yh'=4,'x'=4,'yl'=2,'c'=2] {'yh'}, dimensions={0} | all-to-all | bytes 524288 | tf_op jit(solution)/shard_map/all_to_all | solution.py:29
  39.6 49.3 %conditional.2 = (bf16[8,512,256]{2,1,0:T(8,128)(2,1)}, bf16[8,512,256]{2,1,0:T(8,128)(2,1)}) conditional(s32[]{:T(128)} %bitcast.2, bf16[512,256]{1,0:T(8,128)(2,1)} %param.14, bf16[512,256]{1,0:T(8,128)(2,1)} %param.14), branch_computations={%region_0.1_spmd, %region_1.2_spmd} | conditional | bytes 17301620 | solution.py:224
  40.7 41.8 %all_to_all.42 = bf16[8,512,256]{2,1,0:T(8,128)(2,1)} all-to-all(bf16[8,512,256]{2,1,0:T(8,128)(2,1)S(1)} %broadcast_in_dim.24), channel_id=1, replica_groups=mesh['z'=8,'yh'=4,'x'=4,'yl'=2,'c'=2] {'x','yl'}, dimensions={0} | all-to-all | bytes 4194304 | tf_op jit(solution)/shard_map/cond/branch_1_fun/all_to_all | solution.py:29
  82.5 1.9 collective-permute-start.1
  84.5 4.5 %collective-permute-done.1 = bf16[8,512,256]{2,1,0:T(8,128)(2,1)} collective-permute-done((bf16[8,512,256]{2,1,0:T(8,128)(2,1)}, bf16[8,512,256]{2,1,0:T(8,128)(2,1)}, u32[]{:S(2)}, u32[]{:S(2)}) %collective-permute-start.1) | collective-permute-done | bytes 2097184 | tf_op jit(solution)/shard_map/cond/branch_1_fun/ppermute | solution.py:39
  88.9 2.1 all-gather.3.cloned.1.call-done
  91.0 4.5 %shard_map.129 = (bf16[512,256]{1,0:T(8,128)(2,1)S(1)}, f32[512,2]{1,0:T(8,128)S(1)}) custom-call(s32[1]{0:T(128)} %bitcast.1.pos_ref, bf16[8,512,256]{2,1,0:T(8,128)(2,1)} %get-tuple-element.20.mine_hbm, bf16[8,512,256]{2,1,0:T(8,128)(2,1)} %get-tuple-element.21.other_hbm, bf16[16,256,256]{2,1,0:T(8,128)(2,1)} %bitcast.71), custom_call_target="tpu_custom_call" | custom-call | flops 1073741824 | bytes 8388608 | tf_op jit(solution)/shard_map/pallas_call | solution.py:239
  96.3 29.3 %all_to_all.45.mine_ref = bf16[8,528,256]{2,1,0:T(8,128)(2,1)S(1)} all-to-all(bf16[8,528,256]{2,1,0:T(8,128)(2,1)S(1)} %broadcast_in_dim.38), channel_id=1, replica_groups=mesh['z'=8,'yh'=4,'x'=4,'yl'=2,'c'=2] {'x','yl'}, dimensions={0} | all-to-all | bytes 4325376 | tf_op jit(solution)/shard_map/all_to_all | solution.py:29
  125.6 2.0 collective-permute-start.4
  128.0 4.0 %collective-permute-done.4.other_ref = bf16[8,528,256]{2,1,0:T(8,128)(2,1)} collective-permute-done((bf16[8,528,256]{2,1,0:T(8,128)(2,1)S(1)}, bf16[8,528,256]{2,1,0:T(8,128)(2,1)}, u32[]{:S(2)}, u32[]{:S(2)}) %collective-permute-start.4) | collective-permute-done | bytes 2162720 | tf_op jit(solution)/shard_map/ppermute | solution.py:39
  135.4 5.1 %shard_map.130 = (bf16[16,512,256]{2,1,0:T(8,128)(2,1)S(1)}, bf16[512,256]{1,0:T(8,128)(2,1)}, f32[16,1,256]{2,1,0:T(1,128)S(1)}) custom-call(s32[1]{0:T(128)} %bitcast.1.pos_ref, bf16[8,528,256]{2,1,0:T(8,128)(2,1)S(1)} %all_to_all.45.mine_ref, bf16[8,528,256]{2,1,0:T(8,128)(2,1)} %collective-permute-done.4.other_ref, f32[512,16]{1,0:T(8,128)S(1)} %bitcast.69, ...), custom_call_target="tpu_custom_call" | custom-call | flops 1073741824 | bytes 12582912 | tf_op jit(solution)/shard_map/pallas_call | solution.py:279
  140.5 2.7 %shard_map.131 = bf16[32,256,128]{2,1,0:T(8,128)(2,1)} custom-call(s32[1]{0:T(128)} %bitcast.1.pos_ref, bf16[16,512,256]{2,1,0:T(8,128)(2,1)S(1)} %get-tuple-element.24.f_ref, f32[16,1,256]{2,1,0:T(1,128)S(1)} %get-tuple-element.25.sums_ref), custom_call_target="tpu_custom_call" | custom-call | flops 1073741824 | bytes 6291456 | tf_op jit(solution)/shard_map/pallas_call | solution.py:302
  145.7 4.8 %all-to-all-start.6 = ((bf16[16,32,256]{2,1,0:T(8,128)(2,1)}), bf16[16,32,256]{2,1,0:T(8,128)(2,1)S(1)}, u32[]{:S(2)}, u32[]{:S(2)}) async-start(bf16[16,32,256]{2,1,0:T(8,128)(2,1)} %bitcast.21), calls=%async_computation.8 | async-start | bytes 524288 | tf_op jit(solution)/shard_map/all_to_all | solution.py:301
  151.4 4.6 %all-to-all-done.6.basis_ref = bf16[16,32,256]{2,1,0:T(8,128)(2,1)S(1)} async-done(((bf16[16,32,256]{2,1,0:T(8,128)(2,1)}), bf16[16,32,256]{2,1,0:T(8,128)(2,1)S(1)}, u32[]{:S(2)}, u32[]{:S(2)}) %all-to-all-start.6) | async-done | bytes 262176 | tf_op jit(solution)/shard_map/all_to_all | solution.py:301
  157.0 6.0 %all-to-all-start.7 = ((bf16[16,32,256]{2,1,0:T(8,128)(2,1)}), bf16[16,32,256]{2,1,0:T(8,128)(2,1)S(1)}, u32[]{:S(2)}, u32[]{:S(2)}) async-start(bf16[16,32,256]{2,1,0:T(8,128)(2,1)} %shard_map.132), calls=%async_computation.9 | async-start | bytes 524288 | tf_op jit(solution)/shard_map/all_to_all | solution.py:319
  165.3 3.3 %all-to-all-done.7 = bf16[16,32,256]{2,1,0:T(8,128)(2,1)S(1)} async-done(((bf16[16,32,256]{2,1,0:T(8,128)(2,1)}), bf16[16,32,256]{2,1,0:T(8,128)(2,1)S(1)}, u32[]{:S(2)}, u32[]{:S(2)}) %all-to-all-start.7) | async-done | bytes 262176 | tf_op jit(solution)/shard_map/all_to_all | solution.py:319
  169.2 29.3 %all_to_all.46 = bf16[32,80,128]{2,1,0:T(8,128)(2,1)S(1)} all-to-all(bf16[32,80,128]{2,1,0:T(8,128)(2,1)S(1)} %shard_map.133), channel_id=1, replica_groups=mesh['z'=8,'yh'=4,'x'=4,'yl'=2,'c'=2] {'z','yh'}, dimensions={0} | all-to-all | bytes 1310720 | tf_op jit(solution)/shard_map/all_to_all | solution.py:328
  198.8 24.5 %conditional.3 = (bf16[32,64,128]{2,1,0:T(8,128)(2,1)S(1)}) conditional(s32[]{:T(128)} %bitcast.2, bf16[64,128]{1,0:T(8,128)(2,1)S(1)} %slice_reduce_fusion, bf16[64,128]{1,0:T(8,128)(2,1)S(1)} %slice_reduce_fusion), branch_computations={%region_19.20_spmd, %region_20.21_spmd} | conditional | bytes 1589256 | solution.py:332
  198.9 24.3 %all_to_all.43 = bf16[32,64,128]{2,1,0:T(8,128)(2,1)S(1)} all-to-all(bf16[32,64,128]{2,1,0:T(8,128)(2,1)S(1)} %broadcast_in_dim.29), channel_id=1, replica_groups=mesh['z'=8,'yh'=4,'x'=4,'yl'=2,'c'=2] {'z','yh'}, dimensions={0} | all-to-all | bytes 1048576 | tf_op jit(solution)/shard_map/cond/branch_1_fun/all_to_all | solution.py:29
  225.0 6.5 %reduce-scatter.5.cloned.1.call-done = bf16[1,256,128]{2,1,0:T(8,128)(2,1)} async-done(((bf16[4,256,128]{2,1,0:T(8,128)(2,1)}), bf16[1,256,128]{2,1,0:T(8,128)(2,1)}) %reduce-scatter.5.cloned.1.call-update) | async-done | bytes 65552 | tf_op jit(solution)/shard_map/reduce_scatter | solution.py:331
  231.5 1.9 fusion.5
  (91 shorter events, 15.8 us)
Async XLA Ops:
  7.2 157.7 %copy-start = (bf16[1024,256]{1,0:T(8,128)(2,1)S(1)}, bf16[1024,256]{1,0:T(8,128)(2,1)}, u32[]{:S(2)}) copy-start(bf16[1024,256]{1,0:T(8,128)(2,1)} %param.22) | copy-start | bytes 1572868
  7.2 83.9 %all-gather.3.cloned.1.call-start = ((), (), s32[]{:S(2)}) async-start(), calls=%async_computation.11 | async-start | bytes 2359296 | tf_op jit(solution)/shard_map/all_gather | solution.py:221
  8.1 8.0 %collective-permute-start.2 = (bf16[128,128]{1,0:T(8,128)(2,1)S(1)}, bf16[128,128]{1,0:T(8,128)(2,1)S(1)}, u32[]{:S(2)}, u32[]{:S(2)}) collective-permute-start(bf16[128,128]{1,0:T(8,128)(2,1)S(1)} %get-tuple-element.40), channel_id=1, source_target_pairs={{0,0},{1,32},{2,64},{3,96},{4,128},{5,160},{6,192},{7,224},{8,256}... | collective-permute-start | bytes 98312 | tf_op jit(solution)/shard_map/ppermute | solution.py:216
  14.2 9.4 %collective-permute-start.3 = (bf16[128,128]{1,0:T(8,128)(2,1)S(1)}, bf16[128,128]{1,0:T(8,128)(2,1)S(1)}, u32[]{:S(2)}, u32[]{:S(2)}) collective-permute-start(bf16[128,128]{1,0:T(8,128)(2,1)S(1)} %get-tuple-element.41), channel_id=1, source_target_pairs={{0,16},{1,48},{2,80},{3,112},{4,144},{5,176},{6,208},{7,240},{8,27... | collective-permute-start | bytes 98312 | tf_op jit(solution)/shard_map/ppermute | solution.py:216
  38.8 159.8 %reduce-scatter.3.cloned.1.call-start = ((), (), s32[]{:S(2)}) async-start(), calls=%async_computation.12 | async-start | bytes 2359296 | tf_op jit(solution)/shard_map/reduce_scatter | solution.py:310
  82.5 6.4 %collective-permute-start.1 = (bf16[8,512,256]{2,1,0:T(8,128)(2,1)}, bf16[8,512,256]{2,1,0:T(8,128)(2,1)}, u32[]{:S(2)}, u32[]{:S(2)}) collective-permute-start(bf16[8,512,256]{2,1,0:T(8,128)(2,1)} %all_to_all.42), channel_id=1, source_target_pairs={{0,1},{1,0},{2,3},{3,2},{4,5},{5,4},{6,7},{7,6},{8,9},{9,8},{10,11... | collective-permute-start | bytes 6291464 | tf_op jit(solution)/shard_map/cond/branch_1_fun/ppermute | solution.py:39
  96.3 31.3 %copy-start.8 = (s32[256]{0:T(256)S(1)}, s32[256]{0:T(256)}, u32[]{:S(2)}) copy-start(s32[256]{0:T(256)} %param.19) | copy-start | bytes 3076
  96.3 31.4 %copy-start.6 = (f32[4096]{0:T(1024)S(1)}, f32[4096]{0:T(1024)}, u32[]{:S(2)}) copy-start(f32[4096]{0:T(1024)} %param.17) | copy-start | bytes 49156
  125.6 8.3 %copy-start.2 = (f32[4096]{0:T(1024)S(1)}, f32[4096]{0:T(1024)}, u32[]{:S(2)}) copy-start(f32[4096]{0:T(1024)} %param.16) | copy-start | bytes 49156
  125.6 6.4 %collective-permute-start.4 = (bf16[8,528,256]{2,1,0:T(8,128)(2,1)S(1)}, bf16[8,528,256]{2,1,0:T(8,128)(2,1)}, u32[]{:S(2)}, u32[]{:S(2)}) collective-permute-start(bf16[8,528,256]{2,1,0:T(8,128)(2,1)S(1)} %all_to_all.45.mine_ref), channel_id=1, source_target_pairs={{0,1},{1,0},{2,3},{3,2},{4,5},{5,4},{6,7},{7,6},{8,9},{9,8},{10,11... | collective-permute-start | bytes 6488072 | tf_op jit(solution)/shard_map/ppermute | solution.py:39
  133.9 1.6 copy-start.1
  143.2 0.8 copy-start.5
  143.2 2.3 copy-start.3
  145.7 10.3 %all-to-all-start.6 = ((bf16[16,32,256]{2,1,0:T(8,128)(2,1)}), bf16[16,32,256]{2,1,0:T(8,128)(2,1)S(1)}, u32[]{:S(2)}, u32[]{:S(2)}) async-start(bf16[16,32,256]{2,1,0:T(8,128)(2,1)} %bitcast.21), calls=%async_computation.8 | async-start | bytes 524288 | tf_op jit(solution)/shard_map/all_to_all | solution.py:301
  157.0 11.6 %all-to-all-start.7 = ((bf16[16,32,256]{2,1,0:T(8,128)(2,1)}), bf16[16,32,256]{2,1,0:T(8,128)(2,1)S(1)}, u32[]{:S(2)}, u32[]{:S(2)}) async-start(bf16[16,32,256]{2,1,0:T(8,128)(2,1)} %shard_map.132), calls=%async_computation.9 | async-start | bytes 524288 | tf_op jit(solution)/shard_map/all_to_all | solution.py:319
  163.0 68.4 %reduce-scatter.5.cloned.1.call-start = ((), (), s32[]{:S(2)}) async-start(), calls=%async_computation.13 | async-start | bytes 327680 | tf_op jit(solution)/shard_map/reduce_scatter | solution.py:331
  224.4 9.0 %copy-start.7 = (f32[256]{0:T(256)}, f32[256]{0:T(256)S(1)}, u32[]{:S(2)}) copy-start(f32[256]{0:T(256)S(1)} %multiply_bitcast_fusion.2) | copy-start | bytes 3076
Sparse Core Ops, SparseCore 0:
  39.0 52.0 all-gather.2
  143.3 53.3 reduce-scatter.2
  199.5 31.9 reduce-scatter.4
